TPU v7x, 32 devices: a whole 2x2x4 slice. The times are simulated.
32 devices in a mesh: gx: 8 (over y, x, core), gy: 4 (over z).
Axes of the slice: x: 2, y: 2, z: 4, core: 2. Of those that a mesh axis runs over, the one named last changes fastest.
Arguments:
- velocity: float32 [2, 3, 384, 512], P(None, None, 'gx', 'gy'), may hold values from -6 to 6
- stretch: float32 [512], replicated, may hold values from 0.7 to 1.4
- second_metric: float32 [512], replicated, may hold values from -1 to 1
Outputs:
- section_rhs: float32 [2, 3, 384, 512], P(None, None, 'gx', 'gy')
All inputs are finite; a program needn't handle non-finite values.
Results may differ from a plain program's by a relative error of at most 0.000054.
Values sent between devices are 32-bit elements; how exact they have to be, the bound alone decides.
No kernel may reach another device: no remote copies, remote signals or barrier semaphores. Data moves between devices by JAX's collectives and lax.ppermute only.
A program may use at most 64 MiB of HBM per device.

v0:
```python
import jax
import jax.numpy as jnp
import numpy as np
from jax import lax
from jax.sharding import PartitionSpec as P

VISCOSITY = 0.5


def shifted(value, axis, steps):
    count = lax.axis_size(axis)
    leading, last = (max(0, -steps), min(count, count - steps))
    return lax.ppermute(value, axis, [(source, source + steps) for source in range(leading, last)])


def with_halo(value, sides, width):
    for axis, dim in sides:
        count, length = (lax.axis_size(axis), value.shape[dim])
        up = [(i, (i + 1) % count) for i in range(count - 1)]
        down = [(j, i) for i, j in up]
        last = lax.slice_in_dim(value, length - width, length, axis=dim)
        leading = lax.slice_in_dim(value, 0, width, axis=dim)
        before = lax.ppermute(last, axis, up)
        after = lax.ppermute(leading, axis, down)
        value = jnp.concatenate([before, value, after], axis=dim)
    return value


def x_stencils(padded, length, axis_pos):
    centre = lax.slice_in_dim(padded, 2, 2 + length, axis=axis_pos)
    plus_one = lax.slice_in_dim(padded, 3, 3 + length, axis=axis_pos)
    minus_one = lax.slice_in_dim(padded, 1, 1 + length, axis=axis_pos)
    plus_two = lax.slice_in_dim(padded, 4, 4 + length, axis=axis_pos)
    minus_two = lax.slice_in_dim(padded, 0, length, axis=axis_pos)
    first_rhs = 7.0 / 9.0 * (plus_one - minus_one) + 1.0 / 36.0 * (plus_two - minus_two)
    second = 12.0 / 11.0 * (plus_one - 2.0 * centre + minus_one) + 3.0 / 44.0 * (
        plus_two - 2.0 * centre + minus_two
    )
    return (first_rhs, second)


def y_stencils(padded, local, row_ids, total_rows):
    length = local.shape[-1]
    centre = padded[..., 2 : 2 + length]
    plus_one = padded[..., 3 : 3 + length]
    minus_one = padded[..., 1 : 1 + length]
    plus_two = padded[..., 4 : 4 + length]
    minus_two = padded[..., 0:length]
    near_wall = (row_ids == 1) | (row_ids == total_rows - 2)
    start_edge = row_ids == 0
    end_edge = row_ids == total_rows - 1
    head_rows = local[..., 0:4]
    tail_rows = local[..., length - 4 : length]
    first_start = (
        -3.0 * head_rows[..., 0:1] + 4.0 * head_rows[..., 1:2] - head_rows[..., 2:3]
    ) / 2.0
    first_end = (3.0 * tail_rows[..., 3:4] - 4.0 * tail_rows[..., 2:3] + tail_rows[..., 1:2]) / 2.0
    second_start = (
        2.0 * head_rows[..., 0:1]
        - 5.0 * head_rows[..., 1:2]
        + 4.0 * head_rows[..., 2:3]
        - head_rows[..., 3:4]
    )
    second_end = (
        2.0 * tail_rows[..., 3:4]
        - 5.0 * tail_rows[..., 2:3]
        + 4.0 * tail_rows[..., 1:2]
        - tail_rows[..., 0:1]
    )
    inner_first = 7.0 / 9.0 * (plus_one - minus_one) + 1.0 / 36.0 * (plus_two - minus_two)
    inner_second = 12.0 / 11.0 * (plus_one - 2.0 * centre + minus_one) + 3.0 / 44.0 * (
        plus_two - 2.0 * centre + minus_two
    )
    first_rhs = jnp.where(near_wall, 0.75 * (plus_one - minus_one), inner_first)
    first_rhs = jnp.where(start_edge, first_start, jnp.where(end_edge, first_end, first_rhs))
    second = jnp.where(near_wall, 1.2 * (plus_one - 2.0 * centre + minus_one), inner_second)
    second = jnp.where(start_edge, second_start, jnp.where(end_edge, second_end, second))
    return (first_rhs, second)


def static_coefs(row_ids, total_rows):
    near_wall = (row_ids == 1) | (row_ids == total_rows - 2)
    edge_rows = (row_ids == 0) | (row_ids == total_rows - 1)
    band_one = np.where(edge_rows, 0.0, np.where(near_wall, 0.25, 1.0 / 3.0))
    band_two = np.where(edge_rows, 0.0, np.where(near_wall, 0.1, 2.0 / 11.0))
    return (band_one, band_two)


def inverse_table(lower, diagonal, upper):
    length = lower.shape[-1]
    inner_rows = length - 1
    sub_band = jnp.asarray(lower[..., :inner_rows], jnp.float32)
    super_band = jnp.asarray(upper[..., :inner_rows], jnp.float32)
    diag_part = jnp.asarray(diagonal[..., :inner_rows], jnp.float32)
    places = jnp.arange(inner_rows)
    sub_band = jnp.where(places == 0, jnp.float32(0.0), sub_band)
    super_band = jnp.where(places == inner_rows - 1, jnp.float32(0.0), super_band)
    identity_cols = jnp.broadcast_to(
        jnp.eye(inner_rows, dtype=jnp.float32), sub_band.shape + (inner_rows,)
    )
    return lax.linalg.tridiagonal_solve(sub_band, diag_part, super_band, identity_cols)


def expand(values):
    return values.reshape((2, 1, 1, 1))


def block_solve(right_side, lower, diagonal, upper, inverse, solve_dim):
    length = right_side.shape[solve_dim]
    inner_rows = length - 1
    reach_low = lower[:, 0:1] * inverse[:, :, 0]
    reach_high = upper[:, inner_rows - 1 : inner_rows] * inverse[:, :, inner_rows - 1]
    inner_rhs = lax.slice_in_dim(right_side, 0, inner_rows, axis=solve_dim)
    partial_sol = jnp.einsum(
        "tscxy,tky->tscxk", inner_rhs, inverse, precision=lax.Precision.HIGHEST
    )
    coef_shape = (2, 1, 1, 1, inner_rows)
    first_row = lax.index_in_dim(partial_sol, 0, solve_dim, keepdims=False)
    near_row = lax.index_in_dim(partial_sol, inner_rows - 1, solve_dim, keepdims=False)
    last_rhs = lax.index_in_dim(right_side, length - 1, solve_dim, keepdims=False)
    next_first, next_low = shifted((first_row, reach_low[:, 0]), "gy", -1)
    low_end = lower[:, length - 1]
    diag_end = diagonal[:, length - 1]
    high_end = upper[:, length - 1]
    pivot = diag_end - low_end * reach_high[:, inner_rows - 1] - high_end * next_low
    boundary = (last_rhs - expand(low_end) * near_row - expand(high_end) * next_first) / expand(
        pivot
    )
    prior_value = shifted(boundary, "gy", 1)
    filled = partial_sol - jnp.expand_dims(prior_value, solve_dim) * reach_low.reshape(coef_shape)
    filled = filled - jnp.expand_dims(boundary, solve_dim) * reach_high.reshape(coef_shape)
    return jnp.concatenate([filled, jnp.expand_dims(boundary, solve_dim)], axis=solve_dim)


def neighbour(values, axis, step):
    rolled = jnp.roll(values, step, axis=axis)
    return rolled


def line_blocks(right_side, lower, diagonal, upper, inverse):
    blocks = lower.shape[1]
    length = lower.shape[2]
    inner_rows = length - 1
    reach_low = lower[:, :, 0:1] * inverse[:, :, :, 0]
    reach_high = upper[:, :, inner_rows - 1 : inner_rows] * inverse[:, :, :, inner_rows - 1]
    row_axis = 5
    inner_rhs = lax.slice_in_dim(right_side, 0, inner_rows, axis=row_axis)
    partial_sol = jnp.einsum(
        "tscwbx,tbkx->tscwbk", inner_rhs, inverse, precision=lax.Precision.HIGHEST
    )
    coef_shape = (2, 1, 1, 1, blocks, inner_rows)
    edge_shape = (2, 1, 1, 1, blocks)
    block_axis = row_axis - 1
    first_row = lax.index_in_dim(partial_sol, 0, row_axis, keepdims=False)
    near_row = lax.index_in_dim(partial_sol, inner_rows - 1, row_axis, keepdims=False)
    last_rhs = lax.index_in_dim(right_side, length - 1, row_axis, keepdims=False)
    next_first = neighbour(first_row, block_axis, -1)
    next_low = neighbour(reach_low[:, :, 0], 1, -1)
    low_end = lower[:, :, length - 1]
    diag_end = diagonal[:, :, length - 1]
    high_end = upper[:, :, length - 1]
    pivot = diag_end - low_end * reach_high[:, :, inner_rows - 1] - high_end * next_low
    boundary = (
        last_rhs
        - low_end.reshape(edge_shape) * near_row
        - high_end.reshape(edge_shape) * next_first
    ) / pivot.reshape(edge_shape)
    prior_value = neighbour(boundary, block_axis, 1)
    filled = partial_sol - jnp.expand_dims(prior_value, row_axis) * reach_low.reshape(coef_shape)
    filled = filled - jnp.expand_dims(boundary, row_axis) * reach_high.reshape(coef_shape)
    return jnp.concatenate([filled, jnp.expand_dims(boundary, row_axis)], axis=row_axis)


def x_lines(velocity):
    rows_x = velocity.shape[2]
    blocks = lax.axis_size("gx")
    whole = lax.all_to_all(velocity, "gx", split_axis=3, concat_axis=2, tiled=True)
    planes, comps, total_x, width = whole.shape
    turned = jnp.swapaxes(whole, 2, 3)
    padded = jnp.concatenate([turned[..., -2:], turned, turned[..., :2]], axis=3)
    first_rhs, second = x_stencils(padded, total_x, 3)
    right_side = jnp.stack([first_rhs, second]).reshape((2, planes, comps, width, blocks, rows_x))
    coef_np = np.array([1.0 / 3.0, 2.0 / 11.0])
    lower_np = np.broadcast_to(coef_np[:, None], (2, rows_x))
    ones_np = np.ones((2, rows_x))
    inverse = jnp.broadcast_to(
        inverse_table(lower_np, ones_np, lower_np)[:, None], (2, blocks, rows_x - 1, rows_x - 1)
    )
    lower = jnp.broadcast_to(
        jnp.asarray(lower_np.astype(np.float32))[:, None, :], (2, blocks, rows_x)
    )
    diagonal = jnp.ones((2, blocks, rows_x), jnp.float32)
    solved = line_blocks(right_side, lower, diagonal, lower, inverse)
    solved = solved.reshape((2, planes, comps, width, total_x))
    term_part = -(turned[:, 0:1] * solved[0]) + VISCOSITY * solved[1]
    return lax.all_to_all(
        jnp.swapaxes(term_part, 2, 3), "gx", split_axis=2, concat_axis=3, tiled=True
    )


def wall_terms(velocity, eta_one, eta_two, stretch, second_metric):
    grad_y = eta_one / stretch
    curv_y = eta_two / (stretch * stretch) - second_metric * eta_one / (stretch * stretch * stretch)
    return -(velocity[:, 1:2] * grad_y) + VISCOSITY * curv_y


def y_blocks(velocity, stretch_local, metric_local, offset_rows, total_rows):
    rows_y = velocity.shape[3]
    blocks = lax.axis_size("gy")
    padded = with_halo(velocity, (("gy", 3),), 2)
    row_ids = offset_rows + jnp.arange(rows_y, dtype=jnp.int32)
    first_rhs, second = y_stencils(padded, velocity, row_ids, total_rows)
    all_rows = np.arange(total_rows).reshape((blocks, rows_y))
    band_one, band_two = static_coefs(all_rows, total_rows)
    lower_np = np.stack([band_one, band_two], axis=1)
    ones_np = np.ones((blocks, 2, rows_y))
    inverse_all = inverse_table(lower_np, ones_np, lower_np)
    position = lax.axis_index("gy")
    lower = lax.dynamic_index_in_dim(
        jnp.asarray(lower_np.astype(np.float32)), position, 0, keepdims=False
    )
    inverse = lax.dynamic_index_in_dim(inverse_all, position, 0, keepdims=False)
    diagonal = jnp.ones((2, rows_y), jnp.float32)
    solved = block_solve(jnp.stack([first_rhs, second]), lower, diagonal, lower, inverse, 4)
    return wall_terms(velocity, solved[0], solved[1], stretch_local, metric_local)


def shards(velocity, stretch, second_metric):
    rows_y = velocity.shape[3]
    total_rows = rows_y * lax.axis_size("gy")
    offset_rows = lax.axis_index("gy") * rows_y
    stream_part = x_lines(velocity)
    stretch_local = lax.dynamic_slice_in_dim(stretch, offset_rows, rows_y)
    metric_local = lax.dynamic_slice_in_dim(second_metric, offset_rows, rows_y)
    normal_part = y_blocks(velocity, stretch_local, metric_local, offset_rows, total_rows)
    return stream_part + normal_part


def solution(mesh):
    return jax.shard_map(
        shards,
        mesh=mesh,
        in_specs=(P(None, None, "gx", "gy"), P(), P()),
        out_specs=P(None, None, "gx", "gy"),
        check_vma=False,
    )
```

profile of v0, /device:TPU:0, one launch (start us, length us, event | category | flops | bytes accessed | tf_op | source)
XLA Modules:
  0.0 161.5 jit_solution(10242084571741912543)
XLA Ops:
  0.0 1.1 fusion.704
  1.1 4.9 %collective-permute-start.1 = (f32[2,3,48,2]{3,2,1,0:T(8,128)S(1)}, f32[2,3,48,2]{3,2,1,0:T(8,128)S(1)}, u32[]{:S(2)}, u32[]{:S(2)}) collective-permute-start(f32[2,3,48,2]{3,2,1,0:T(8,128)S(1)} %get-tuple-element.770), channel_id=1, source_target_pairs={{0,1},{1,2},{2,3},{4,5},{5,6},{6,7},{8,9},{9,10},{10,11},{12,13},{... | collective-permute-start | bytes 6920 | tf_op jit(solution)/shard_map/ppermute | solution.py:23
  6.1 1.3 collective-permute-start
  7.4 1.2 copy.2803
  8.5 1.3 reshape.166968
  9.9 3.7 %all-to-all-start = ((f32[8,1,4608]{2,1,0:T(1,128)}), f32[8,1,4608]{2,1,0:T(1,128)S(1)}, u32[]{:S(2)}, u32[]{:S(2)}) async-start(f32[8,1,4608]{2,1,0:T(1,128)} %reshape.166968), calls=%async_computation | async-start | bytes 294912 | tf_op jit(solution)/shard_map/all_to_all | solution.py:177
  14.5 39.1 %while.10 = (s32[]{:T(128)}, f32[4,2]{0,1:T(2,128)S(1)}, f32[4,2,127]{2,1,0:T(2,128)S(1)}, f32[3,32,4,2]{1,0,3,2:T(4,128)S(1)}, f32[3,32,4,2,127]{4,3,2,1,0:T(2,...) while((s32[]{:T(128)}, f32[4,2]{0,1:T(2,128)S(1)}, ...), condition=%wide.region_1.2_spmd.clone, body=%wide.region_0.1_spmd.sunk.clone.sunk | while | flops 98337 | bytes 935997 | solution.py:101
  54.0 0.9 dynamic-slice_bitcast_fusion
  73.3 14.0 %while.9 = (s32[]{:T(128)}, f32[4,2,127]{2,1,0:T(2,128)S(1)}, f32[3,32,4,2,127]{4,3,2,1,0:T(2,128)S(1)}, f32[3,32,4,2,127]{4,3,2,1,0:T(2,128)S(1)}, f32[3,32,4,2...) while((s32[]{:T(128)}, f32[4,2,127]{2,1,0:T(2,128)S(1)}, ...), condition=%wide.region_3.4_spmd, body=%wide.region_2.3_spmd.sunk | while | flops 95537 | bytes 832429 | solution.py:101
  89.7 1.5 collective-permute-start.3
  95.4 1.3 fusion.638
  98.1 1.4 multiply_subtract_fusion.107
  99.9 1.1 constant_dynamic-update-slice_fusion.109
  102.8 1.4 constant_dynamic-update-slice_fusion.67
  108.8 1.0 select_bitcast_fusion.1
  109.8 1.0 select_bitcast_fusion
  111.5 1.3 collective-permute-start.2
  113.3 5.0 %collective-permute-done.2 = f32[2,2,3,48]{3,1,2,0:T(2,128)S(1)} collective-permute-done((f32[2,2,3,48]{3,1,2,0:T(2,128)S(1)}, f32[2,2,3,48]{3,1,2,0:T(2,128)S(1)}, u32[]{:S(2)}, u32[]{:S(2)}) %collective-permute-start.2) | collective-permute-done | bytes 2336 | tf_op jit(solution)/shard_map/ppermute | solution.py:13
  118.4 4.1 %collective-permute-start.4 = (f32[2,2,3,48]{3,1,2,0:T(2,128)S(1)}, f32[2,2,3,48]{3,1,2,0:T(2,128)S(1)}, u32[]{:S(2)}, u32[]{:S(2)}) collective-permute-start(f32[2,2,3,48]{3,1,2,0:T(2,128)S(1)} %fusion.326), channel_id=1, source_target_pairs={{0,1},{1,2},{2,3},{4,5},{5,6},{6,7},{8,9},{9,10},{10,11},{12,13},{... | collective-permute-start | bytes 6920 | tf_op jit(solution)/shard_map/ppermute | solution.py:13
  123.8 1.3 dynamic_slice.63
  125.2 0.9 copy.3032
  127.2 0.9 reduce.8
  130.9 1.7 %fusion.288 = f32[2,8,47,2,3,16]{2,5,4,3,1,0:T(8,128)} fusion(f32[2,2,3,16,8,47]{5,4,3,2,1,0:T(8,128)S(1)} %bitcast.3405, f32[2,47,47]{2,1,0:T(8,128)S(1)} %copy.2806), kind=kOutput, calls=%fused_computation.549 | convolution fusion | flops 40716288 | bytes 595208 | tf_op jit(solution)/shard_map/tscwbx,tbkx->tscwbk/dot_general | solution.py:148
  132.7 2.0 %copy.2808 = f32[2,8,47,2,3,16]{5,1,2,4,3,0:T(8,128)S(1)} copy(f32[2,8,47,2,3,16]{2,5,4,3,1,0:T(8,128)} %fusion.288) | data formatting | bytes 577536 | tf_op jit(solution)/shard_map/tscwbx,tbkx->tscwbk/dot_general | solution.py:148
  136.8 0.9 fusion.318
  138.3 2.7 %multiply_subtract_fusion.32 = f32[2,2,3,16,8,47]{3,4,5,2,1,0:T(8,128)} fusion(f32[2,8,47]{1,2,0:T(8,128)} %copy.2819, f32[2,2,3,16,8]{3,4,2,1,0:T(8,128)S(1)} %bitcast.3424, f32[2,8,47]{1,2,0:T(8,128)} %copy.2814, f32[2,2,3,16,8]{3,4,2,1,0:T(8,128)S(1)} %pad_maximum_fusion.7, f32[2,8,47,2,3,16]{5,1,2,4,3,0:T(8,128)S(1)} %copy.2808), kind=kLoop, calls=%fused_computation.546 | loop fusion | flops 288768 | bytes 595840 | tf_op jit(solution)/shard_map/sub | solution.py:170
  141.0 2.5 %copy.2820 = f32[2,2,3,16,8,47]{5,4,3,2,1,0:T(8,128)S(1)} copy(f32[2,2,3,16,8,47]{3,4,5,2,1,0:T(8,128)} %multiply_subtract_fusion.32) | data formatting | bytes 577536 | tf_op jit(solution)/shard_map/sub | solution.py:170
  145.1 2.3 %reshape.166970 = f32[8,1,4608]{2,1,0:T(1,128)} reshape(f32[384,3,2,16]{3,2,1,0:T(2,128)S(1)} %bitcast.3407) | data formatting | bytes 294912
  147.5 4.3 %all-to-all-start.1 = ((f32[8,1,4608]{2,1,0:T(1,128)}), f32[8,1,4608]{2,1,0:T(1,128)S(1)}, u32[]{:S(2)}, u32[]{:S(2)}) async-start(f32[8,1,4608]{2,1,0:T(1,128)} %reshape.166970), calls=%async_computation.1 | async-start | bytes 294912 | tf_op jit(solution)/shard_map/all_to_all | solution.py:196
  152.0 5.5 %all-to-all-done.1 = f32[8,1,4608]{2,1,0:T(1,128)S(1)} async-done(((f32[8,1,4608]{2,1,0:T(1,128)}), f32[8,1,4608]{2,1,0:T(1,128)S(1)}, u32[]{:S(2)}, u32[]{:S(2)}) %all-to-all-start.1) | async-done | bytes 147488 | tf_op jit(solution)/shard_map/all_to_all | solution.py:196
  157.5 0.9 reduce.9
  158.4 1.6 reshape.166971
  (1106 shorter events, 98.3 us)
Async XLA Ops:
  0.0 13.8 %copy-start.2 = (f32[4,2,127]{0,1,2:T(2,128)S(1)}, f32[4,2,127]{0,1,2:T(2,128)}, u32[]{:S(2)}) copy-start(f32[4,2,127]{0,1,2:T(2,128)} %constant.162.clone) | copy-start | bytes 12196
  1.1 107.7 %collective-permute-start.1 = (f32[2,3,48,2]{3,2,1,0:T(8,128)S(1)}, f32[2,3,48,2]{3,2,1,0:T(8,128)S(1)}, u32[]{:S(2)}, u32[]{:S(2)}) collective-permute-start(f32[2,3,48,2]{3,2,1,0:T(8,128)S(1)} %get-tuple-element.770), channel_id=1, source_target_pairs={{0,1},{1,2},{2,3},{4,5},{5,6},{6,7},{8,9},{9,10},{10,11},{12,13},{... | collective-permute-start | bytes 6920 | tf_op jit(solution)/shard_map/ppermute | solution.py:23
  6.1 102.7 %collective-permute-start = (f32[2,3,48,2]{3,2,1,0:T(8,128)S(1)}, f32[2,3,48,2]{3,2,1,0:T(8,128)S(1)}, u32[]{:S(2)}, u32[]{:S(2)}) collective-permute-start(f32[2,3,48,2]{3,2,1,0:T(8,128)S(1)} %get-tuple-element.771), channel_id=1, source_target_pairs={{1,0},{2,1},{3,2},{5,4},{6,5},{7,6},{9,8},{10,9},{11,10},{13,12},{... | collective-permute-start | bytes 6920 | tf_op jit(solution)/shard_map/ppermute | solution.py:24
  9.9 116.8 %all-to-all-start = ((f32[8,1,4608]{2,1,0:T(1,128)}), f32[8,1,4608]{2,1,0:T(1,128)S(1)}, u32[]{:S(2)}, u32[]{:S(2)}) async-start(f32[8,1,4608]{2,1,0:T(1,128)} %reshape.166968), calls=%async_computation | async-start | bytes 294912 | tf_op jit(solution)/shard_map/all_to_all | solution.py:177
  87.3 7.0 %copy-start = (f32[2,3,48,128]{3,2,1,0:T(8,128)S(1)}, f32[2,3,48,128]{3,2,1,0:T(8,128)}, u32[]{:S(2)}) copy-start(f32[2,3,48,128]{3,2,1,0:T(8,128)} %param.15) | copy-start | bytes 442372
  88.9 16.0 %copy-start.7 = (f32[2]{0:T(128)S(1)}, f32[2]{0:T(128)}, u32[]{:S(2)}) copy-start(f32[2]{0:T(128)} %constant.165) | copy-start | bytes 28
  89.7 18.5 %collective-permute-start.3 = (f32[2]{0:T(128)}, f32[2]{0:T(128)}, u32[]{:S(2)}, u32[]{:S(2)}) collective-permute-start(f32[2]{0:T(128)} %slice_reduce_fusion.2), channel_id=1, source_target_pairs={{1,0},{2,1},{3,2},{5,4},{6,5},{7,6},{9,8},{10,9},{11,10},{13,12},{... | collective-permute-start | bytes 32 | tf_op jit(solution)/shard_map/ppermute | solution.py:13
  93.1 6.5 %copy-start.40 = (f32[2]{0:T(128)}, f32[2]{0:T(128)S(1)}, u32[]{:S(2)}) copy-start(f32[2]{0:T(128)S(1)} %get-tuple-element.667) | copy-start | bytes 28
  93.6 6.0 %copy-start.38 = (f32[2]{0:T(128)}, f32[2]{0:T(128)S(1)}, u32[]{:S(2)}) copy-start(f32[2]{0:T(128)S(1)} %get-tuple-element.642) | copy-start | bytes 28
  93.6 6.0 %copy-start.39 = (f32[2,1]{0,1:T(1,128)}, f32[2,1]{0,1:T(1,128)S(1)}, u32[]{:S(2)}) copy-start(f32[2,1]{0,1:T(1,128)S(1)} %get-tuple-element.644) | copy-start | bytes 28
  94.1 5.5 %copy-start.8 = (f32[2]{0:T(128)}, f32[2]{0:T(128)S(1)}, u32[]{:S(2)}) copy-start(f32[2]{0:T(128)S(1)} %get-tuple-element.920) | copy-start | bytes 28
  94.1 5.5 %copy-start.9 = (f32[2]{0:T(128)}, f32[2]{0:T(128)S(1)}, u32[]{:S(2)}) copy-start(f32[2]{0:T(128)S(1)} %get-tuple-element.921) | copy-start | bytes 28
  94.1 5.5 %copy-start.10 = (f32[2]{0:T(128)}, f32[2]{0:T(128)S(1)}, u32[]{:S(2)}) copy-start(f32[2]{0:T(128)S(1)} %get-tuple-element.922) | copy-start | bytes 28
  94.1 5.5 %copy-start.11 = (f32[2]{0:T(128)}, f32[2]{0:T(128)S(1)}, u32[]{:S(2)}) copy-start(f32[2]{0:T(128)S(1)} %get-tuple-element.923) | copy-start | bytes 28
  94.1 5.5 %copy-start.12 = (f32[2]{0:T(128)}, f32[2]{0:T(128)S(1)}, u32[]{:S(2)}) copy-start(f32[2]{0:T(128)S(1)} %get-tuple-element.924) | copy-start | bytes 28
  94.1 5.5 %copy-start.13 = (f32[2]{0:T(128)}, f32[2]{0:T(128)S(1)}, u32[]{:S(2)}) copy-start(f32[2]{0:T(128)S(1)} %get-tuple-element.925) | copy-start | bytes 28
  94.1 5.5 %copy-start.14 = (f32[2]{0:T(128)}, f32[2]{0:T(128)S(1)}, u32[]{:S(2)}) copy-start(f32[2]{0:T(128)S(1)} %get-tuple-element.926) | copy-start | bytes 28
  94.1 5.5 %copy-start.15 = (f32[2]{0:T(128)}, f32[2]{0:T(128)S(1)}, u32[]{:S(2)}) copy-start(f32[2]{0:T(128)S(1)} %get-tuple-element.927) | copy-start | bytes 28
  94.1 5.5 %copy-start.16 = (f32[2]{0:T(128)}, f32[2]{0:T(128)S(1)}, u32[]{:S(2)}) copy-start(f32[2]{0:T(128)S(1)} %get-tuple-element.928) | copy-start | bytes 28
  109.8 8.5 %copy-start.48 = (f32[2]{0:T(128)S(1)}, f32[2]{0:T(128)}, u32[]{:S(2)}) copy-start(f32[2]{0:T(128)} %get-tuple-element.812) | copy-start | bytes 28
  111.5 6.8 %collective-permute-start.2 = (f32[2,2,3,48]{3,1,2,0:T(2,128)S(1)}, f32[2,2,3,48]{3,1,2,0:T(2,128)S(1)}, u32[]{:S(2)}, u32[]{:S(2)}) collective-permute-start(f32[2,2,3,48]{3,1,2,0:T(2,128)S(1)} %bitcast.3604), channel_id=1, source_target_pairs={{1,0},{2,1},{3,2},{5,4},{6,5},{7,6},{9,8},{10,9},{11,10},{13,12},{... | collective-permute-start | bytes 6920 | tf_op jit(solution)/shard_map/ppermute | solution.py:13
  118.4 7.7 %collective-permute-start.4 = (f32[2,2,3,48]{3,1,2,0:T(2,128)S(1)}, f32[2,2,3,48]{3,1,2,0:T(2,128)S(1)}, u32[]{:S(2)}, u32[]{:S(2)}) collective-permute-start(f32[2,2,3,48]{3,1,2,0:T(2,128)S(1)} %fusion.326), channel_id=1, source_target_pairs={{0,1},{1,2},{2,3},{4,5},{5,6},{6,7},{8,9},{9,10},{10,11},{12,13},{... | collective-permute-start | bytes 6920 | tf_op jit(solution)/shard_map/ppermute | solution.py:13
  143.7 8.1 %copy-start.6 = (f32[2,2,3,48]{3,2,1,0:T(4,128)S(1)}, f32[2,2,3,48]{3,2,1,0:T(4,128)}, u32[]{:S(2)}) copy-start(f32[2,2,3,48]{3,2,1,0:T(4,128)} %copy.3030) | copy-start | bytes 6916
  143.7 8.1 %copy-start.42 = (f32[2,127]{1,0:T(2,128)S(1)}, f32[2,127]{1,0:T(2,128)}, u32[]{:S(2)}) copy-start(f32[2,127]{1,0:T(2,128)} %copy-done.41) | copy-start | bytes 3052
  143.8 8.1 %copy-start.44 = (f32[2,127]{1,0:T(2,128)S(1)}, f32[2,127]{1,0:T(2,128)}, u32[]{:S(2)}) copy-start(f32[2,127]{1,0:T(2,128)} %copy-done.43) | copy-start | bytes 3052
  147.4 13.2 %copy-start.1 = (f32[2,2,3,48,1]{4,3,2,1,0:T(8,128)S(1)}, f32[2,2,3,48,1]{4,3,2,1,0:T(8,128)}, u32[]{:S(2)}) copy-start(f32[2,2,3,48,1]{4,3,2,1,0:T(8,128)} %copy.3032) | copy-start | bytes 6916
  147.4 13.2 %copy-start.3 = (f32[2,48,128]{2,1,0:T(8,128)S(1)}, f32[2,48,128]{2,1,0:T(8,128)}, u32[]{:S(2)}) copy-start(f32[2,48,128]{2,1,0:T(8,128)} %slice_bitcast_fusion.3) | copy-start | bytes 147460
  147.4 13.2 %copy-start.45 = (f32[128]{0:T(128)S(1)}, f32[128]{0:T(128)}, u32[]{:S(2)}) copy-start(f32[128]{0:T(128)} %get-tuple-element.462) | copy-start | bytes 1540
  147.4 13.3 %copy-start.47 = (f32[128]{0:T(128)S(1)}, f32[128]{0:T(128)}, u32[]{:S(2)}) copy-start(f32[128]{0:T(128)} %copy-done.46) | copy-start | bytes 1540
  147.4 13.3 %copy-start.49 = (f32[128]{0:T(128)S(1)}, f32[128]{0:T(128)}, u32[]{:S(2)}) copy-start(f32[128]{0:T(128)} %multiply_multiply_fusion) | copy-start | bytes 1540
  147.4 13.3 %copy-start.50 = (f32[128]{0:T(128)S(1)}, f32[128]{0:T(128)}, u32[]{:S(2)}) copy-start(f32[128]{0:T(128)} %dynamic_slice.63) | copy-start | bytes 1540
  147.5 10.0 %all-to-all-start.1 = ((f32[8,1,4608]{2,1,0:T(1,128)}), f32[8,1,4608]{2,1,0:T(1,128)S(1)}, u32[]{:S(2)}, u32[]{:S(2)}) async-start(f32[8,1,4608]{2,1,0:T(1,128)} %reshape.166970), calls=%async_computation.1 | async-start | bytes 294912 | tf_op jit(solution)/shard_map/all_to_all | solution.py:196
  (26 other events, 126.8 us)
where the time goes:
time: 162 us
  local copies, waits for them, and re-layouts  83.4 us (51%)
  other arithmetic  42 us (26%)
  starting transfers between devices  21.2 us (13%)
  waiting for transfers between devices  10.5 us (6%)
  matrix products  2.18 us (1%)
  between operations  1.72 us (1%)
    mul x167, local copies, waits for them, and re-layouts, inverse_table(): lax.linalg.tridiagonal_solve(sub_band, diag_part, super_band, identity_cols)  14.8 us
    broadcast_in_dim x126, local copies, waits for them, and re-layouts, inverse_table(): lax.linalg.tridiagonal_solve(sub_band, diag_part, super_band, identity_cols)  12.3 us
    while x135, other arithmetic  12.1 us
    sub x126, local copies, waits for them, and re-layouts, inverse_table(): lax.linalg.tridiagonal_solve(sub_band, diag_part, super_band, identity_cols)  11.6 us
    unnamed x140, local copies, waits for them, and re-layouts  9.61 us
    squeeze x97, local copies, waits for them, and re-layouts, inverse_table(): lax.linalg.tridiagonal_solve(sub_band, diag_part, super_band, identity_cols)  8.84 us
    ppermute x3, starting transfers between devices, shifted(): lax.ppermute(value, axis, [(source, source + steps) for source in range(l...  6.91 us
    unnamed x53, other arithmetic  6.73 us
  transfers between devices with their start and end apart: 7, of which 2 were waited for; matrix products, arithmetic and copies ran while one was open for 63% of the time, Pallas kernels for 0%

commit v1 on v0

v1 whole, which is shorter than its diff:
```python
import functools

import jax
import jax.numpy as jnp
import numpy as np
from jax import lax
from jax.experimental import pallas as pl
from jax.experimental.pallas import tpu as pltpu
from jax.sharding import PartitionSpec as P

VISCOSITY = 0.5
COEFS = (1.0 / 3.0, 2.0 / 11.0)
WALL_COEFS = (1.0 / 4.0, 1.0 / 10.0)
HIGHEST = lax.Precision.HIGHEST


def decay(coef):
    root = (-1.0 + np.sqrt(1.0 - 4.0 * coef * coef)) / (2.0 * coef)
    return root, 1.0 / (1.0 + 2.0 * coef * root)


def toeplitz(coef, length):
    root, gain = decay(coef)
    at = np.arange(length)
    return gain * root ** np.abs(at[:, None] - at[None, :])


def wall_columns(coef, wall_coef, length):
    root, gain = decay(coef)
    size = length + 64
    band = np.full(size, coef)
    band[0], band[1] = 0.0, wall_coef
    matrix = np.eye(size) + np.diag(band[:-1], 1) + np.diag(band[1:], -1)
    inverse = np.linalg.solve(matrix, np.eye(size)[:, :3])
    at = np.arange(size)
    spread = (inverse[:, 2] - gain * root ** np.abs(at - 2.0)) / root**2
    return np.stack([inverse[:, 0], inverse[:, 1], spread], axis=1)[:length]


def inner_columns(coef, length):
    root, gain = decay(coef)
    at = np.arange(length)
    return gain * np.stack([root**at, root ** np.abs(at - 1.0), root ** (at + 1.0)], axis=1)


def edge_table(length, low_wall, high_wall):
    table = np.zeros((16, 2 * length))
    for system in range(2):
        sign = -1.0 if system == 0 else 1.0
        inner = inner_columns(COEFS[system], length)
        wall = wall_columns(COEFS[system], WALL_COEFS[system], length)
        low = wall if low_wall else inner
        high = wall if high_wall else inner
        part = slice(system * length, (system + 1) * length)
        table[6 * system : 6 * system + 3, part] = low.T
        table[6 * system + 3 : 6 * system + 6, part] = high[::-1].T
    return table.astype(np.float32)


def stencils(minus_two, minus_one, centre, plus_one, plus_two):
    first = 7.0 / 9.0 * (plus_one - minus_one) + 1.0 / 36.0 * (plus_two - minus_two)
    second = 12.0 / 11.0 * (plus_one - 2.0 * centre + minus_one) + 3.0 / 44.0 * (
        plus_two - 2.0 * centre + minus_two
    )
    return first, second


def row_stencils(field):
    rows = field.shape[-2]
    cut = lambda at: field[..., at : at + rows - 4, :]
    return stencils(cut(0), cut(1), cut(2), cut(3), cut(4))


def lane_stencils(field):
    lanes = field.shape[-1]
    axis = field.ndim - 1
    turn = lambda steps: pltpu.roll(field, steps % lanes, axis)
    return stencils(turn(2), turn(1), field, turn(-1), turn(-2))


def send_kernel(field, x_weights, y_weights, xe_out, xo_out, ye_out, yo_out):
    slabs, rows, lanes = field.shape
    x_even = lax.rem(lax.axis_index("gx"), 2) == 0
    y_even = lax.rem(lax.axis_index("gy"), 2) == 0
    value = field[...]
    first, second = row_stencils(value)
    zeros = jnp.zeros((2, lanes), jnp.float32)
    for s in range(slabs):
        sums = [
            jnp.sum(x_weights[k] * part[s], axis=0, keepdims=True)
            for k, part in enumerate((first, second, first, second))
        ]
        low = jnp.concatenate([value[s, 0:4], sums[0], sums[1], zeros], axis=0)
        high = jnp.concatenate([value[s, rows - 4 : rows], sums[2], sums[3], zeros], axis=0)
        place = pl.ds(s * lanes, lanes)
        xe_out[:, place] = jnp.where(x_even, high, low)
        xo_out[:, place] = jnp.where(x_even, low, high)
    flat = value.reshape(slabs * rows, lanes)
    first, second = lane_stencils(flat)
    contract = (((1,), (1,)), ((), ()))
    packed = sum(
        lax.dot_general(
            y_weights[k], part, contract, precision=HIGHEST, preferred_element_type=jnp.float32
        )
        for k, part in enumerate((flat, first, second))
    )
    ye_out[...] = jnp.where(y_even, packed[8:], packed[:8])
    yo_out[...] = jnp.where(y_even, packed[:8], packed[8:])


def metric_rows(stretch, metric):
    position = lax.axis_index("gy")
    inv = 1.0 / stretch[pl.ds(position, 1), :]
    curve = metric[pl.ds(position, 1), :]
    return inv, VISCOSITY * curve * inv * inv * inv, VISCOSITY * inv * inv


def combine(velocity_u, velocity_v, grad_x, curv_x, eta_one, eta_two, rows):
    inv, slope, bend = rows
    return (
        VISCOSITY * curv_x + bend * eta_two - velocity_u * grad_x - (velocity_v * inv + slope) * eta_one
    )


def bulk_kernel(field, stretch, metric, x_matrix, y_matrix, out):
    slabs, rows, lanes = field.shape
    value = field[...]
    flat = value.reshape(slabs * rows, lanes)
    lane = lax.broadcasted_iota(jnp.int32, flat.shape, 1)
    inner = (lane >= 2) & (lane < lanes - 2)
    eta = [
        jnp.dot(
            jnp.where(inner, part, 0.0),
            y_matrix[k],
            precision=HIGHEST,
            preferred_element_type=jnp.float32,
        ).reshape(slabs, rows, lanes)
        for k, part in enumerate(lane_stencils(flat))
    ]
    pad = jnp.zeros((2, lanes), jnp.float32)
    solved = [
        [
            jnp.dot(
                x_matrix[k],
                jnp.concatenate([pad, part[s], pad], axis=0),
                precision=HIGHEST,
                preferred_element_type=jnp.float32,
            )
            for s in range(slabs)
        ]
        for k, part in enumerate(row_stencils(value))
    ]
    metrics = metric_rows(stretch, metric)
    for s in range(slabs):
        plane = s // 3 * 3
        out[s] = combine(
            value[plane], value[plane + 1], solved[0][s], solved[1][s], eta[0][s], eta[1][s], metrics
        )


def edge_rows(own, other, far_sums, roots, sign):
    a1, a2, a3, a4 = own
    b1, b2, b3, b4 = other
    f0, s0 = stencils(b2, b1, a1, a2, a3)
    f1, s1 = stencils(b1, a1, a2, a3, a4)
    g1, t1 = stencils(b3, b2, b1, a1, a2)
    g2, t2 = stencils(b4, b3, b2, b1, a1)
    first_sum = sign * (g1 + roots[0] * g2) + far_sums[0]
    second_sum = t1 + roots[1] * t2 + far_sums[1]
    return (sign * f0, sign * f1, first_sum), (s0, s1, second_sum)


def wall_rows(own, own_sums, sign):
    a1, a2, a3, a4 = own
    first = (
        sign * 0.5 * (4.0 * a2 - 3.0 * a1 - a3),
        sign * 0.75 * (a3 - a1),
        own_sums[0],
    )
    second = (2.0 * a1 - 5.0 * a2 + 4.0 * a3 - a4, 1.2 * (a3 - 2.0 * a2 + a1), own_sums[1])
    return first, second


def layers(packed, ascending):
    rows = [packed[k : k + 1] for k in range(4)]
    return rows if ascending else rows[::-1]


def far(packed):
    return packed[4:5], packed[5:6]


def edge_matrix(own_low, own_high, other_low, other_high, low_wall=None, high_wall=None):
    roots = [decay(coef)[0] for coef in COEFS]
    low = edge_rows(layers(own_low, True), layers(other_low, False), far(other_low), roots, 1.0)
    high = edge_rows(layers(own_high, False), layers(other_high, True), far(other_high), roots, -1.0)
    if low_wall is not None:
        at_low = wall_rows(layers(own_low, True), far(own_low), 1.0)
        at_high = wall_rows(layers(own_high, False), far(own_high), -1.0)
        low = jax.tree.map(lambda wall, inner: jnp.where(low_wall, wall, inner), at_low, low)
        high = jax.tree.map(lambda wall, inner: jnp.where(high_wall, wall, inner), at_high, high)
    rows = [*low[0], *high[0], *low[1], *high[1]]
    rows.append(jnp.zeros((4, rows[0].shape[1]), jnp.float32))
    return jnp.concatenate(rows, axis=0)


def final_kernel(
    field, stretch, metric, x_table, y_table, bulk, xe_own, xo_own, ye_own, yo_own, xe, xo, ye, yo, out
):
    slabs, rows, lanes = field.shape
    y_at, y_count = lax.axis_index("gy"), lax.axis_size("gy")
    x_even = lax.rem(lax.axis_index("gx"), 2) == 0
    y_even = lax.rem(y_at, 2) == 0
    pick = lambda flag, one, two: jnp.where(flag, one[...], two[...])
    x_edges = edge_matrix(
        pick(x_even, xo_own, xe_own),
        pick(x_even, xe_own, xo_own),
        pick(x_even, xo, xe),
        pick(x_even, xe, xo),
    )
    y_edges = edge_matrix(
        pick(y_even, yo_own, ye_own),
        pick(y_even, ye_own, yo_own),
        pick(y_even, yo, ye),
        pick(y_even, ye, yo),
        y_at == 0,
        y_at == y_count - 1,
    )
    variant = jnp.where(y_at == 0, 0, jnp.where(y_at == y_count - 1, 2, 1))
    grad = lax.dot_general(
        x_table[...],
        x_edges,
        (((0,), (0,)), ((), ())),
        precision=HIGHEST,
        preferred_element_type=jnp.float32,
    )
    eta = lax.dot_general(
        y_edges,
        y_table[variant],
        (((0,), (0,)), ((), ())),
        precision=HIGHEST,
        preferred_element_type=jnp.float32,
    ).reshape(slabs, rows, 2 * lanes)
    metrics = metric_rows(stretch, metric)
    for s in range(slabs):
        plane = s // 3 * 3
        place = slice(s * lanes, (s + 1) * lanes)
        out[s] = bulk[s] + combine(
            field[plane],
            field[plane + 1],
            grad[:rows, place],
            grad[rows:, place],
            eta[s, :, :lanes],
            eta[s, :, lanes:],
            metrics,
        )


def exchange_pairs(x_count, y_count):
    at = lambda x, y: x * y_count + y
    x_even = lambda x: x ^ 1
    x_odd = lambda x: (x + 1) % x_count if x % 2 else (x - 1) % x_count
    cells = [(x, y) for x in range(x_count) for y in range(y_count)]
    xe = [(at(x, y), at(x_even(x), y)) for x, y in cells]
    xo = [(at(x, y), at(x_odd(x), y)) for x, y in cells]
    ye = [(at(x, y), at(x, y ^ 1)) for x, y in cells]
    yo = [
        (at(x, y), at(x_even(x), y) if y in (0, y_count - 1) else at(x, y + 1 if y % 2 else y - 1))
        for x, y in cells
    ]
    return xe, xo, ye, yo


def call(kernel, outs, name, flops, bytes_accessed):
    vmem = pl.BlockSpec(memory_space=pltpu.VMEM)
    many = isinstance(outs, list)
    return lambda *args: pl.pallas_call(
        kernel,
        out_shape=outs,
        in_specs=[vmem] * len(args),
        out_specs=[vmem] * len(outs) if many else vmem,
        cost_estimate=pl.CostEstimate(flops=flops, bytes_accessed=bytes_accessed, transcendentals=0),
        name=name,
    )(*args)


def shards(velocity, stretch, second_metric):
    planes, comps, rows, lanes = velocity.shape
    slabs = planes * comps
    x_count, y_count = lax.axis_size("gx"), lax.axis_size("gy")
    field = velocity.reshape(slabs, rows, lanes)
    stretch = stretch.reshape(y_count, lanes)
    metric = second_metric.reshape(y_count, lanes)
    roots = [decay(coef)[0] for coef in COEFS]

    at = np.arange(2, rows - 2)[:, None]
    x_weights = np.stack(
        [np.broadcast_to(w, (rows - 4, lanes)) for w in (*(r**at for r in roots), *(r ** (rows - 1 - at) for r in roots))]
    ).astype(np.float32)
    at = np.arange(2, lanes - 2)
    y_weights = np.zeros((3, 16, lanes), np.float32)
    for k in range(4):
        y_weights[0, k, k] = 1.0
        y_weights[0, 8 + k, lanes - 4 + k] = 1.0
    for k, r in enumerate(roots):
        y_weights[1 + k, 4 + k, 2:-2] = r**at
        y_weights[1 + k, 12 + k, 2:-2] = r ** (lanes - 1 - at)
    x_matrix = np.stack([toeplitz(coef, rows) for coef in COEFS]).astype(np.float32)
    y_matrix = np.stack([toeplitz(coef, lanes) for coef in COEFS]).astype(np.float32)
    x_table = edge_table(rows, False, False)
    y_table = np.stack(
        [edge_table(lanes, True, False), edge_table(lanes, False, False), edge_table(lanes, False, True)]
    )

    shape = lambda *dims: jax.ShapeDtypeStruct(dims, jnp.float32)
    x_shape, y_shape = shape(8, slabs * lanes), shape(8, slabs * rows)
    xe, xo, ye, yo = call(send_kernel, [x_shape, x_shape, y_shape, y_shape], "sends", 10**6, 10**6)(
        field, x_weights, y_weights
    )
    pairs = exchange_pairs(x_count, y_count)
    move = lambda value, way: lax.ppermute(value, ("gx", "gy"), way)
    xo_in = move(xo, pairs[1])
    ye_in = move(ye, pairs[2])
    xe_in = move(xe, pairs[0])
    yo_in = move(yo, pairs[3])
    bulk = call(bulk_kernel, shape(slabs, rows, lanes), "bulk", 10**8, 10**6)(
        field, stretch, metric, x_matrix, y_matrix
    )
    out = call(final_kernel, shape(slabs, rows, lanes), "final", 10**7, 10**6)(
        field, stretch, metric, x_table, y_table, bulk, xe, xo, ye, yo, xe_in, xo_in, ye_in, yo_in
    )
    return out.reshape(planes, comps, rows, lanes)


def solution(mesh):
    return jax.shard_map(
        shards,
        mesh=mesh,
        in_specs=(P(None, None, "gx", "gy"), P(), P()),
        out_specs=P(None, None, "gx", "gy"),
        check_vma=False,
    )
```

time: 162 us -> 14.4 us (0.09)
  the two profiles are of different devices: /device:TPU:0 before, /device:TPU:8 now
where the time goes in v1:
time: 14.4 us; the launch traced here: 14.2 us
  Pallas kernels  7.28 us (51%)
  starting transfers between devices  5.71 us (40%)
  local copies, waits for them, and re-layouts  1.19 us (8%)
    pallas_call x3, Pallas kernels, call(): pl.pallas_call(kernel, out_shape=outs, in_specs=[vmem] * len(args), out_s...  7.28 us
    ppermute x4, starting transfers between devices, shards(): move = lambda value, way: lax.ppermute(value, ('gx', 'gy'), way)  5.71 us
    unnamed x8, local copies, waits for them, and re-layouts  1.19 us
  transfers between devices with their start and end apart: 4, of which 0 were waited for; matrix products, arithmetic and copies ran while one was open for 0% of the time, Pallas kernels for 18%

profile of v1, /device:TPU:8, one launch (start us, length us, event | category | flops | bytes accessed | tf_op | source)
XLA Modules:
  0.0 14.2 jit_solution(3961298724472890347)
XLA Ops:
  0.0 2.3 %sends.1 = (f32[8,768]{1,0:T(8,128)}, f32[8,768]{1,0:T(8,128)}, f32[8,288]{1,0:T(8,128)}, f32[8,288]{1,0:T(8,128)}) custom-call(f32[6,48,128]{2,1,0:T(8,128)} %bitcast.4, f32[4,44,128]{2,1,0:T(8,128)} %constant.12.clone.x_weights, f32[3,16,128]{2,1,0:T(8,128)} %constant.13.clone.y_weights), custom_call_target="tpu_custom_call" | custom-call | flops 1000000 | bytes 1000000 | tf_op jit(solution)/shard_map/sends/pallas_call | solution.py:277
  2.3 0.0 collective-permute-start
  2.3 2.6 %collective-permute-start.1 = (f32[8,768]{1,0:T(8,128)}, f32[8,768]{1,0:T(8,128)S(1)}, u32[]{:S(2)}, u32[]{:S(2)}) collective-permute-start(f32[8,768]{1,0:T(8,128)} %get-tuple-element.10.xo_own), channel_id=1, source_target_pairs={{0,28},{1,29},{2,30},{3,31},{4,8},{5,9},{6,10},{7,11},{8,4},{9,5},... | collective-permute-start | bytes 73736 | tf_op jit(solution)/shard_map/ppermute | solution.py:321
  4.9 0.4 %collective-permute-start.2 = (f32[8,288]{1,0:T(8,128)}, f32[8,288]{1,0:T(8,128)S(1)}, u32[]{:S(2)}, u32[]{:S(2)}) collective-permute-start(f32[8,288]{1,0:T(8,128)} %get-tuple-element.11.ye_own), channel_id=1, source_target_pairs={{0,1},{1,0},{2,3},{3,2},{4,5},{5,4},{6,7},{7,6},{8,9},{9,8},{10,11... | collective-permute-start | bytes 27656 | tf_op jit(solution)/shard_map/ppermute | solution.py:321
  5.3 2.7 %collective-permute-start.3 = (f32[8,288]{1,0:T(8,128)}, f32[8,288]{1,0:T(8,128)S(1)}, u32[]{:S(2)}, u32[]{:S(2)}) collective-permute-start(f32[8,288]{1,0:T(8,128)} %get-tuple-element.12.yo_own), channel_id=1, source_target_pairs={{0,4},{1,2},{2,1},{3,7},{4,0},{5,6},{6,5},{7,3},{8,12},{9,10},{10,... | collective-permute-start | bytes 27656 | tf_op jit(solution)/shard_map/ppermute | solution.py:321
  8.0 2.5 %bulk.1 = f32[6,48,128]{2,1,0:T(8,128)} custom-call(f32[6,48,128]{2,1,0:T(8,128)} %bitcast.5, f32[4,128]{1,0:T(4,128)} %bitcast.7, f32[4,128]{1,0:T(4,128)} %bitcast.9, f32[2,48,48]{2,1,0:T(8,128)} %constant.14.clone.x_matrix, f32[2,128,128]{2,1,0:T(8,128)} %constant.15.clone.y_matrix), custom_call_target="tpu_custom_call" | custom-call | flops 100000000 | bytes 1000000 | tf_op jit(solution)/shard_map/bulk/pallas_call | solution.py:277
  10.5 0.0 collective-permute-done.2.ye
  10.6 0.0 copy-start.2
  10.6 0.0 collective-permute-done.3.yo
  10.6 0.0 copy-start.3
  10.6 0.0 collective-permute-done.xe
  10.6 0.0 copy-start
  10.6 0.0 collective-permute-done.1.xo
  10.6 0.5 %copy-done.2 = f32[8,288]{1,0:T(8,128)} copy-done((f32[8,288]{1,0:T(8,128)}, f32[8,288]{1,0:T(8,128)S(1)}, u32[]{:S(2)}) %copy-start.2) | copy-done | bytes 9240
  11.1 0.0 copy-done.3
  11.2 0.0 copy-done
  11.2 0.0 copy-start.1
  11.2 0.6 %copy-done.1 = f32[8,768]{1,0:T(8,128)} copy-done((f32[8,768]{1,0:T(8,128)}, f32[8,768]{1,0:T(8,128)S(1)}, u32[]{:S(2)}) %copy-start.1) | copy-done | bytes 24600
  11.8 2.4 %final.1 = f32[6,48,128]{2,1,0:T(8,128)} custom-call(f32[6,48,128]{2,1,0:T(8,128)} %bitcast.6, f32[4,128]{1,0:T(4,128)} %bitcast.8, f32[4,128]{1,0:T(4,128)} %bitcast.10, f32[16,96]{1,0:T(8,128)} %constant.16.clone.x_table, f32[3,16,256]{2,1,0:T(8,128)} %constant.17.clone.y_table, f32[6,48,128]{2,1,0:T(8,128)} %bulk.1, f32[8,768]{1,0:T(8,128)} %get-tuple-element.9.xe_own, ...), custom_call_target="tpu_custom_call" | custom-call | flops 10000000 | bytes 1000000 | tf_op jit(solution)/shard_map/final/pallas_call | solution.py:277
Async XLA Ops:
  2.3 8.3 %collective-permute-start = (f32[8,768]{1,0:T(8,128)}, f32[8,768]{1,0:T(8,128)S(1)}, u32[]{:S(2)}, u32[]{:S(2)}) collective-permute-start(f32[8,768]{1,0:T(8,128)} %get-tuple-element.9.xe_own), channel_id=1, source_target_pairs={{0,4},{1,5},{2,6},{3,7},{4,0},{5,1},{6,2},{7,3},{8,12},{9,13},{10,... | collective-permute-start | bytes 73736 | tf_op jit(solution)/shard_map/ppermute | solution.py:321
  2.3 8.3 %collective-permute-start.1 = (f32[8,768]{1,0:T(8,128)}, f32[8,768]{1,0:T(8,128)S(1)}, u32[]{:S(2)}, u32[]{:S(2)}) collective-permute-start(f32[8,768]{1,0:T(8,128)} %get-tuple-element.10.xo_own), channel_id=1, source_target_pairs={{0,28},{1,29},{2,30},{3,31},{4,8},{5,9},{6,10},{7,11},{8,4},{9,5},... | collective-permute-start | bytes 73736 | tf_op jit(solution)/shard_map/ppermute | solution.py:321
  4.9 5.7 %collective-permute-start.2 = (f32[8,288]{1,0:T(8,128)}, f32[8,288]{1,0:T(8,128)S(1)}, u32[]{:S(2)}, u32[]{:S(2)}) collective-permute-start(f32[8,288]{1,0:T(8,128)} %get-tuple-element.11.ye_own), channel_id=1, source_target_pairs={{0,1},{1,0},{2,3},{3,2},{4,5},{5,4},{6,7},{7,6},{8,9},{9,8},{10,11... | collective-permute-start | bytes 27656 | tf_op jit(solution)/shard_map/ppermute | solution.py:321
  5.3 5.2 %collective-permute-start.3 = (f32[8,288]{1,0:T(8,128)}, f32[8,288]{1,0:T(8,128)S(1)}, u32[]{:S(2)}, u32[]{:S(2)}) collective-permute-start(f32[8,288]{1,0:T(8,128)} %get-tuple-element.12.yo_own), channel_id=1, source_target_pairs={{0,4},{1,2},{2,1},{3,7},{4,0},{5,6},{6,5},{7,3},{8,12},{9,10},{10,... | collective-permute-start | bytes 27656 | tf_op jit(solution)/shard_map/ppermute | solution.py:321
  10.6 0.6 %copy-start.2 = (f32[8,288]{1,0:T(8,128)}, f32[8,288]{1,0:T(8,128)S(1)}, u32[]{:S(2)}) copy-start(f32[8,288]{1,0:T(8,128)S(1)} %collective-permute-done.2.ye) | copy-start | bytes 27652
  10.6 0.6 %copy-start.3 = (f32[8,288]{1,0:T(8,128)}, f32[8,288]{1,0:T(8,128)S(1)}, u32[]{:S(2)}) copy-start(f32[8,288]{1,0:T(8,128)S(1)} %collective-permute-done.3.yo) | copy-start | bytes 27652
  10.6 0.6 %copy-start = (f32[8,768]{1,0:T(8,128)}, f32[8,768]{1,0:T(8,128)S(1)}, u32[]{:S(2)}) copy-start(f32[8,768]{1,0:T(8,128)S(1)} %collective-permute-done.xe) | copy-start | bytes 73732
  11.2 0.6 %copy-start.1 = (f32[8,768]{1,0:T(8,128)}, f32[8,768]{1,0:T(8,128)S(1)}, u32[]{:S(2)}) copy-start(f32[8,768]{1,0:T(8,128)S(1)} %collective-permute-done.1.xo) | copy-start | bytes 73732

commit v2 on v1

v2 whole, which is shorter than its diff:
```python
import jax
import jax.numpy as jnp
import numpy as np
from jax import lax
from jax.experimental import pallas as pl
from jax.experimental.pallas import tpu as pltpu
from jax.sharding import PartitionSpec as P

VISCOSITY = 0.5
COEFS = (1.0 / 3.0, 2.0 / 11.0)
WALL_COEFS = (1.0 / 4.0, 1.0 / 10.0)
HIGHEST = lax.Precision.HIGHEST
TILE = 8


def decay(coef):
    root = (-1.0 + np.sqrt(1.0 - 4.0 * coef * coef)) / (2.0 * coef)
    return float(root), float(1.0 / (1.0 + 2.0 * coef * root))


ROOTS = tuple(decay(coef)[0] for coef in COEFS)


def inner_weights(system):
    root, gain = decay(COEFS[system])
    return (gain, gain / root, gain * root), (gain, gain * root, gain * root)


def wall_weights(system):
    root, gain = decay(COEFS[system])
    size = 96
    band = np.full(size, COEFS[system])
    band[0], band[1] = 0.0, WALL_COEFS[system]
    matrix = np.eye(size) + np.diag(band[:-1], 1) + np.diag(band[1:], -1)
    inverse = np.linalg.solve(matrix, np.eye(size)[:, :3])
    spread = (inverse[:2, 2] - gain * root ** np.abs(np.arange(2) - 2.0)) / root**2
    columns = np.stack([inverse[:2, 0], inverse[:2, 1], spread], axis=1)
    return tuple(map(float, columns[1] / root)), tuple(map(float, columns[0]))


def iota(shape, axis):
    return lax.broadcasted_iota(jnp.int32, shape, axis)


def powers(root, exponent):
    size = jnp.exp(exponent.astype(jnp.float32) * float(np.log(-root)))
    return jnp.where(lax.rem(exponent, 2) == 0, size, -size)


def stencils(minus_two, minus_one, centre, plus_one, plus_two):
    first = 7.0 / 9.0 * (plus_one - minus_one) + 1.0 / 36.0 * (plus_two - minus_two)
    second = 12.0 / 11.0 * (plus_one - 2.0 * centre + minus_one) + 3.0 / 44.0 * (
        plus_two - 2.0 * centre + minus_two
    )
    return first, second


def right_sides(lines):
    turn = lambda steps: pltpu.roll(lines, steps % lines.shape[0], 0)
    at = iota(lines.shape, 0)
    inner = (at >= 2) & (at < lines.shape[0] - 2)
    parts = stencils(turn(2), turn(1), lines, turn(-1), turn(-2))
    return [jnp.where(inner, part, 0.0) for part in parts]


def edge_sums(part, root):
    rows, lanes = part.shape
    tiles = [part[k : k + TILE] for k in range(0, rows, TILE)]
    step = float(root**TILE)
    low, high = tiles[-1], tiles[0]
    for tile in tiles[-2::-1]:
        low = low * step + tile
    for tile in tiles[1:]:
        high = high * step + tile
    at = iota((TILE, lanes), 0)
    low = low * powers(root, at)
    high = high * powers(root, TILE - 1 - at)
    return jnp.sum(low, axis=0, keepdims=True), jnp.sum(high, axis=0, keepdims=True)


def packed_edges(lines):
    rows, lanes = lines.shape
    sums = [edge_sums(part, root) for part, root in zip(right_sides(lines), ROOTS)]
    zeros = jnp.zeros((2, lanes), jnp.float32)
    low = jnp.concatenate([lines[0:4], sums[0][0], sums[1][0], zeros], axis=0)
    high = jnp.concatenate([lines[rows - 4 : rows], sums[0][1], sums[1][1], zeros], axis=0)
    return low, high


def send_kernel(field, ye_out, xo_out, yo_out, xe_out):
    slabs, rows, lanes = field.shape
    x_even = lax.rem(lax.axis_index("gx"), 2) == 0
    y_even = lax.rem(lax.axis_index("gy"), 2) == 0
    for s in range(slabs):
        low, high = packed_edges(field[s])
        place = pl.ds(s * lanes, lanes)
        xe_out[:, place] = jnp.where(x_even, high, low)
        xo_out[:, place] = jnp.where(x_even, low, high)
    low, high = packed_edges(jnp.transpose(field[...].reshape(slabs * rows, lanes)))
    place = pl.ds(0, slabs * rows)
    ye_out[:, place] = jnp.where(y_even, high, low)
    yo_out[:, place] = jnp.where(y_even, low, high)


def inverse_matrix(system, size):
    root, gain = decay(COEFS[system])
    return gain * powers(root, jnp.abs(iota((size, size), 0) - iota((size, size), 1)))


def solve(matrix, right_side):
    return jnp.dot(matrix, right_side, precision=HIGHEST, preferred_element_type=jnp.float32)


def bulk_kernel(field, stretch, metric, out, slope_turned, bend_turned):
    slabs, rows, lanes = field.shape
    position = pl.ds(lax.axis_index("gy"), 1)
    inv = 1.0 / stretch[position, :]
    curve = VISCOSITY * metric[position, :] * inv * inv * inv
    bend = jnp.transpose(jnp.broadcast_to(VISCOSITY * inv * inv, (lanes, lanes)))
    bend_turned[...] = bend
    slope = [-(field[plane * 3 + 1] * inv + curve) for plane in range(slabs // 3)]
    slope = jnp.transpose(jnp.concatenate([part for part in slope for _ in range(3)], axis=0))
    slope_turned[...] = slope
    first, second = right_sides(jnp.transpose(field[...].reshape(slabs * rows, lanes)))
    y_term = slope * solve(inverse_matrix(0, lanes), first)
    y_term += bend[:, :1] * solve(inverse_matrix(1, lanes), second)
    y_term = jnp.transpose(y_term)
    matrices = [inverse_matrix(system, rows) for system in range(2)]
    for s in range(slabs):
        first, second = right_sides(field[s])
        x_term = VISCOSITY * solve(matrices[1], second) - field[s // 3 * 3] * solve(matrices[0], first)
        out[s] = x_term + y_term[s * rows : (s + 1) * rows]


def edge_rows(own, other, sign):
    a1, a2, a3, a4 = layers(own, sign > 0)
    b1, b2, b3, b4 = layers(other, sign < 0)
    f0, s0 = stencils(b2, b1, a1, a2, a3)
    f1, s1 = stencils(b1, a1, a2, a3, a4)
    g1, t1 = stencils(b3, b2, b1, a1, a2)
    g2, t2 = stencils(b4, b3, b2, b1, a1)
    first_sum = sign * (g1 + ROOTS[0] * g2) + other[4:5]
    second_sum = t1 + ROOTS[1] * t2 + other[5:6]
    return (sign * f0, sign * f1, first_sum), (s0, s1, second_sum)


def wall_rows(own, sign):
    a1, a2, a3, a4 = layers(own, sign > 0)
    first = (sign * 0.5 * (4.0 * a2 - 3.0 * a1 - a3), sign * 0.75 * (a3 - a1), own[4:5])
    second = (2.0 * a1 - 5.0 * a2 + 4.0 * a3 - a4, 1.2 * (a3 - 2.0 * a2 + a1), own[5:6])
    return first, second


def layers(packed, ascending):
    rows = [packed[k : k + 1] for k in range(4)]
    return rows if ascending else rows[::-1]


def weigh(weights, values):
    return weights[0] * values[0] + weights[1] * values[1] + weights[2] * values[2]


def edge_terms(own, other, sign, wall=None):
    rows = edge_rows(own, other, sign)
    at_wall = None if wall is None else wall_rows(own, sign)
    terms = []
    for system in range(2):
        spread, first = [weigh(weights, rows[system]) for weights in inner_weights(system)]
        if wall is not None:
            pair = [weigh(weights, at_wall[system]) for weights in wall_weights(system)]
            spread = jnp.where(wall, pair[0], spread)
            first = jnp.where(wall, pair[1], first)
        at = iota((TILE, own.shape[1]), 0)
        at = at if sign > 0 else TILE - 1 - at
        far = powers(ROOTS[system], at) * spread
        terms.append((jnp.where(at == 0, first, far), far))
    return terms


def edge_update(low, high, system, tile, tiles):
    step = ROOTS[system] ** TILE
    up, down = tile, tiles - 1 - tile
    from_low = low[0] if up == 0 else low[1] * float(step**up)
    from_high = high[0] if down == 0 else high[1] * float(step**down)
    return from_low + from_high


def final_kernel(
    field, bulk, slope, bend, ye_own, xo_own, yo_own, xe_own, ye, xo, yo, xe, out
):
    slabs, rows, lanes = field.shape
    y_at, y_count = lax.axis_index("gy"), lax.axis_size("gy")
    x_even = lax.rem(lax.axis_index("gx"), 2) == 0
    y_even = lax.rem(y_at, 2) == 0
    count = slabs * rows
    pick = lambda flag, one, two: jnp.where(flag, one[...], two[...])
    pick_y = lambda flag, one, two: jnp.where(flag, one[:, :count], two[:, :count])
    low = edge_terms(pick_y(y_even, yo_own, ye_own), pick_y(y_even, yo, ye), 1.0, y_at == 0)
    high = edge_terms(
        pick_y(y_even, ye_own, yo_own), pick_y(y_even, ye, yo), -1.0, y_at == y_count - 1
    )
    tiles = lanes // TILE
    y_term = []
    for tile in range(tiles):
        place = slice(tile * TILE, (tile + 1) * TILE)
        one, two = [edge_update(low[k], high[k], k, tile, tiles) for k in range(2)]
        y_term.append(slope[place, :] * one + bend[place, :1] * two)
    y_term = jnp.transpose(jnp.concatenate(y_term, axis=0))
    low = edge_terms(pick(x_even, xo_own, xe_own), pick(x_even, xo, xe), 1.0)
    high = edge_terms(pick(x_even, xe_own, xo_own), pick(x_even, xe, xo), -1.0)
    tiles = rows // TILE
    for tile in range(tiles):
        one, two = [edge_update(low[k], high[k], k, tile, tiles) for k in range(2)]
        for s in range(slabs):
            place = slice(tile * TILE, (tile + 1) * TILE)
            part = slice(s * lanes, (s + 1) * lanes)
            turned = y_term[s * rows + tile * TILE : s * rows + (tile + 1) * TILE]
            x_term = VISCOSITY * two[:, part] - field[s // 3 * 3, place] * one[:, part]
            out[s, place] = bulk[s, place] + x_term + turned


def exchange_pairs(x_count, y_count):
    at = lambda x, y: x * y_count + y
    x_even = lambda x: x ^ 1
    x_odd = lambda x: (x + 1) % x_count if x % 2 else (x - 1) % x_count
    cells = [(x, y) for x in range(x_count) for y in range(y_count)]
    xe = [(at(x, y), at(x_even(x), y)) for x, y in cells]
    xo = [(at(x, y), at(x_odd(x), y)) for x, y in cells]
    ye = [(at(x, y), at(x, y ^ 1)) for x, y in cells]
    yo = [
        (at(x, y), at(x_even(x), y) if y in (0, y_count - 1) else at(x, y + 1 if y % 2 else y - 1))
        for x, y in cells
    ]
    return ye, xo, yo, xe


def call(kernel, outs, name, flops):
    vmem = pl.BlockSpec(memory_space=pltpu.VMEM)
    many = isinstance(outs, list)
    return lambda *args: pl.pallas_call(
        kernel,
        out_shape=outs,
        in_specs=[vmem] * len(args),
        out_specs=[vmem] * len(outs) if many else vmem,
        cost_estimate=pl.CostEstimate(flops=flops, bytes_accessed=10**6, transcendentals=0),
        compiler_params=pltpu.CompilerParams(vmem_limit_bytes=8 * 2**20),
        name=name,
    )(*args)


def shards(velocity, stretch, second_metric):
    planes, comps, rows, lanes = velocity.shape
    slabs = planes * comps
    x_count, y_count = lax.axis_size("gx"), lax.axis_size("gy")
    field = velocity.reshape(slabs, rows, lanes)
    stretch = stretch.reshape(y_count, lanes)
    metric = second_metric.reshape(y_count, lanes)

    shape = lambda *dims: jax.ShapeDtypeStruct(dims, jnp.float32)
    send = shape(8, slabs * max(lanes, rows))
    own = call(send_kernel, [send] * 4, "sends", 10**6)(field)
    pairs = exchange_pairs(x_count, y_count)
    moved = [lax.ppermute(value, ("gx", "gy"), way) for value, way in zip(own, pairs)]
    block = shape(slabs, rows, lanes)
    bulk = call(bulk_kernel, [block, shape(lanes, slabs * rows), shape(lanes, lanes)], "bulk", 10**8)(
        field, stretch, metric
    )
    out = call(final_kernel, block, "final", 10**7)(field, *bulk, *own, *moved)
    return out.reshape(planes, comps, rows, lanes)


def solution(mesh):
    return jax.shard_map(
        shards,
        mesh=mesh,
        in_specs=(P(None, None, "gx", "gy"), P(), P()),
        out_specs=P(None, None, "gx", "gy"),
        check_vma=False,
    )
```

time: 14.4 us -> 9.99 us (0.69)
  the two profiles are of different devices: /device:TPU:8 before, /device:TPU:0 now
where the time goes in v2:
time: 9.99 us; the launch traced here: 9.83 us
  starting transfers between devices  5.21 us (52%)
  Pallas kernels  2.55 us (26%)
  local copies, waits for them, and re-layouts  1.1 us (11%)
  waiting for transfers between devices  0.95 us (10%)
    ppermute x4, starting transfers between devices, shards(): lax.ppermute(value, ('gx', 'gy'), way)  5.21 us
    pallas_call x3, Pallas kernels, call(): pl.pallas_call(kernel, out_shape=outs, in_specs=[vmem] * len(args), out_s...  2.55 us
    unnamed x6, local copies, waits for them, and re-layouts  1.1 us
    ppermute x4, waiting for transfers between devices, shards(): lax.ppermute(value, ('gx', 'gy'), way)  0.95 us
  transfers between devices with their start and end apart: 4, of which 1 were waited for; matrix products, arithmetic and copies ran while one was open for 0% of the time, Pallas kernels for 11%

profile of v2, /device:TPU:0, one launch (start us, length us, event | category | flops | bytes accessed | tf_op | source)
XLA Modules:
  0.0 9.8 jit_solution(6185852677926949336)
XLA Ops:
  0.0 0.0 copy-start
  0.0 0.9 %copy-done = f32[2,3,48,128]{3,2,1,0:T(8,128)S(1)} copy-done((f32[2,3,48,128]{3,2,1,0:T(8,128)S(1)}, f32[2,3,48,128]{3,2,1,0:T(8,128)}, u32[]{:S(2)}) %copy-start) | copy-done | bytes 147480
  0.9 0.5 %sends.1 = (f32[8,768]{1,0:T(8,128)S(1)}, f32[8,768]{1,0:T(8,128)S(1)}, f32[8,768]{1,0:T(8,128)S(1)}, f32[8,768]{1,0:T(8,128)S(1)}) custom-call(f32[6,48,128]{2,1,0:T(8,128)S(1)} %bitcast.4), custom_call_target="tpu_custom_call" | custom-call | flops 1000000 | bytes 1000000 | tf_op jit(solution)/shard_map/sends/pallas_call | solution.py:240
  1.4 3.1 %collective-permute-start = (f32[8,768]{1,0:T(8,128)S(1)}, f32[8,768]{1,0:T(8,128)S(1)}, u32[]{:S(2)}, u32[]{:S(2)}) collective-permute-start(f32[8,768]{1,0:T(8,128)S(1)} %get-tuple-element.15.ye_own), channel_id=1, source_target_pairs={{0,1},{1,0},{2,3},{3,2},{4,5},{5,4},{6,7},{7,6},{8,9},{9,8},{10,11... | collective-permute-start | bytes 73736 | tf_op jit(solution)/shard_map/ppermute | solution.py:263
  4.5 1.6 %collective-permute-start.1 = (f32[8,768]{1,0:T(8,128)S(1)}, f32[8,768]{1,0:T(8,128)S(1)}, u32[]{:S(2)}, u32[]{:S(2)}) collective-permute-start(f32[8,768]{1,0:T(8,128)S(1)} %get-tuple-element.16.xo_own), channel_id=1, source_target_pairs={{0,28},{1,29},{2,30},{3,31},{4,8},{5,9},{6,10},{7,11},{8,4},{9,5},... | collective-permute-start | bytes 73736 | tf_op jit(solution)/shard_map/ppermute | solution.py:263
  6.1 0.0 collective-permute-start.2
  6.1 0.0 copy-start.2
  6.1 0.0 copy-start.1
  6.1 0.5 %collective-permute-start.3 = (f32[8,768]{1,0:T(8,128)S(1)}, f32[8,768]{1,0:T(8,128)S(1)}, u32[]{:S(2)}, u32[]{:S(2)}) collective-permute-start(f32[8,768]{1,0:T(8,128)S(1)} %get-tuple-element.18.xe_own), channel_id=1, source_target_pairs={{0,4},{1,5},{2,6},{3,7},{4,0},{5,1},{6,2},{7,3},{8,12},{9,13},{10,... | collective-permute-start | bytes 73736 | tf_op jit(solution)/shard_map/ppermute | solution.py:263
  6.6 0.2 %copy-done.2 = f32[512]{0:T(512)S(1)} copy-done((f32[512]{0:T(512)S(1)}, f32[512]{0:T(512)}, u32[]{:S(2)}) %copy-start.2) | copy-done | bytes 2072
  6.8 0.0 copy-done.1
  6.8 1.0 %bulk.1 = (f32[6,48,128]{2,1,0:T(8,128)S(1)}, f32[128,288]{1,0:T(8,128)S(1)}, f32[128,128]{1,0:T(8,128)S(1)}) custom-call(f32[6,48,128]{2,1,0:T(8,128)S(1)} %bitcast.5, f32[4,128]{1,0:T(4,128)S(1)} %bitcast.7, f32[4,128]{1,0:T(4,128)S(1)} %bitcast.8), custom_call_target="tpu_custom_call" | custom-call | flops 100000000 | bytes 1000000 | tf_op jit(solution)/shard_map/bulk/pallas_call | solution.py:240
  7.8 0.0 collective-permute-done.ye
  7.8 0.9 %collective-permute-done.1.xo = f32[8,768]{1,0:T(8,128)S(1)} collective-permute-done((f32[8,768]{1,0:T(8,128)S(1)}, f32[8,768]{1,0:T(8,128)S(1)}, u32[]{:S(2)}, u32[]{:S(2)}) %collective-permute-start.1) | collective-permute-done | bytes 24608 | tf_op jit(solution)/shard_map/ppermute | solution.py:263
  8.8 0.0 collective-permute-done.2.yo
  8.8 0.0 collective-permute-done.3.xe
  8.8 1.0 %final.1 = f32[6,48,128]{2,1,0:T(8,128)} custom-call(f32[6,48,128]{2,1,0:T(8,128)S(1)} %bitcast.6, f32[6,48,128]{2,1,0:T(8,128)S(1)} %get-tuple-element.12.bulk, f32[128,288]{1,0:T(8,128)S(1)} %get-tuple-element.13.slope, f32[128,128]{1,0:T(8,128)S(1)} %get-tuple-element.14.bend, f32[8,768]{1,0:T(8,128)S(1)} %get-tuple-element.15.ye_own, ...), custom_call_target="tpu_custom_call" | custom-call | flops 10000000 | bytes 1000000 | tf_op jit(solution)/shard_map/final/pallas_call | solution.py:240
Async XLA Ops:
  0.0 0.9 %copy-start = (f32[2,3,48,128]{3,2,1,0:T(8,128)S(1)}, f32[2,3,48,128]{3,2,1,0:T(8,128)}, u32[]{:S(2)}) copy-start(f32[2,3,48,128]{3,2,1,0:T(8,128)} %param.3) | copy-start | bytes 442372
  1.4 6.5 %collective-permute-start = (f32[8,768]{1,0:T(8,128)S(1)}, f32[8,768]{1,0:T(8,128)S(1)}, u32[]{:S(2)}, u32[]{:S(2)}) collective-permute-start(f32[8,768]{1,0:T(8,128)S(1)} %get-tuple-element.15.ye_own), channel_id=1, source_target_pairs={{0,1},{1,0},{2,3},{3,2},{4,5},{5,4},{6,7},{7,6},{8,9},{9,8},{10,11... | collective-permute-start | bytes 73736 | tf_op jit(solution)/shard_map/ppermute | solution.py:263
  4.5 4.3 %collective-permute-start.1 = (f32[8,768]{1,0:T(8,128)S(1)}, f32[8,768]{1,0:T(8,128)S(1)}, u32[]{:S(2)}, u32[]{:S(2)}) collective-permute-start(f32[8,768]{1,0:T(8,128)S(1)} %get-tuple-element.16.xo_own), channel_id=1, source_target_pairs={{0,28},{1,29},{2,30},{3,31},{4,8},{5,9},{6,10},{7,11},{8,4},{9,5},... | collective-permute-start | bytes 73736 | tf_op jit(solution)/shard_map/ppermute | solution.py:263
  6.1 2.7 %collective-permute-start.2 = (f32[8,768]{1,0:T(8,128)S(1)}, f32[8,768]{1,0:T(8,128)S(1)}, u32[]{:S(2)}, u32[]{:S(2)}) collective-permute-start(f32[8,768]{1,0:T(8,128)S(1)} %get-tuple-element.17.yo_own), channel_id=1, source_target_pairs={{0,4},{1,2},{2,1},{3,7},{4,0},{5,6},{6,5},{7,3},{8,12},{9,10},{10,... | collective-permute-start | bytes 73736 | tf_op jit(solution)/shard_map/ppermute | solution.py:263
  6.1 0.7 %copy-start.2 = (f32[512]{0:T(512)S(1)}, f32[512]{0:T(512)}, u32[]{:S(2)}) copy-start(f32[512]{0:T(512)} %param.5) | copy-start | bytes 6148
  6.1 0.7 %copy-start.1 = (f32[512]{0:T(512)S(1)}, f32[512]{0:T(512)}, u32[]{:S(2)}) copy-start(f32[512]{0:T(512)} %param.4) | copy-start | bytes 6148
  6.1 2.7 %collective-permute-start.3 = (f32[8,768]{1,0:T(8,128)S(1)}, f32[8,768]{1,0:T(8,128)S(1)}, u32[]{:S(2)}, u32[]{:S(2)}) collective-permute-start(f32[8,768]{1,0:T(8,128)S(1)} %get-tuple-element.18.xe_own), channel_id=1, source_target_pairs={{0,4},{1,5},{2,6},{3,7},{4,0},{5,1},{6,2},{7,3},{8,12},{9,13},{10,... | collective-permute-start | bytes 73736 | tf_op jit(solution)/shard_map/ppermute | solution.py:263

commit v3 on v2

v3 whole, which is shorter than its diff:
```python
import jax
import jax.numpy as jnp
import numpy as np
from jax import lax
from jax.experimental import pallas as pl
from jax.experimental.pallas import tpu as pltpu
from jax.sharding import PartitionSpec as P

VISCOSITY = 0.5
COEFS = (1.0 / 3.0, 2.0 / 11.0)
WALL_COEFS = (1.0 / 4.0, 1.0 / 10.0)
HIGHEST = lax.Precision.HIGHEST
TILE = 8
ROUNDS = ("eeoe", "o11o", "1oe1", "2222")


def decay(coef):
    root = (-1.0 + np.sqrt(1.0 - 4.0 * coef * coef)) / (2.0 * coef)
    return float(root), float(1.0 / (1.0 + 2.0 * coef * root))


ROOTS = tuple(decay(coef)[0] for coef in COEFS)


def inner_weights(system):
    root, gain = decay(COEFS[system])
    return (gain, gain / root, gain * root), (gain, gain * root, gain * root)


def wall_weights(system):
    root, gain = decay(COEFS[system])
    size = 96
    band = np.full(size, COEFS[system])
    band[0], band[1] = 0.0, WALL_COEFS[system]
    matrix = np.eye(size) + np.diag(band[:-1], 1) + np.diag(band[1:], -1)
    inverse = np.linalg.solve(matrix, np.eye(size)[:, :3])
    spread = (inverse[:2, 2] - gain * root ** np.abs(np.arange(2) - 2.0)) / root**2
    columns = np.stack([inverse[:2, 0], inverse[:2, 1], spread], axis=1)
    return tuple(map(float, columns[1] / root)), tuple(map(float, columns[0]))


def iota(shape, axis):
    return lax.broadcasted_iota(jnp.int32, shape, axis)


def powers(root, exponent):
    size = jnp.exp(exponent.astype(jnp.float32) * float(np.log(-root)))
    return jnp.where(lax.rem(exponent, 2) == 0, size, -size)


def stencils(minus_two, minus_one, centre, plus_one, plus_two):
    first = 7.0 / 9.0 * (plus_one - minus_one) + 1.0 / 36.0 * (plus_two - minus_two)
    second = 12.0 / 11.0 * (plus_one - 2.0 * centre + minus_one) + 3.0 / 44.0 * (
        plus_two - 2.0 * centre + minus_two
    )
    return first, second


def right_sides(lines):
    turn = lambda steps: pltpu.roll(lines, steps % lines.shape[0], 0)
    at = iota(lines.shape, 0)
    inner = (at >= 2) & (at < lines.shape[0] - 2)
    parts = stencils(turn(2), turn(1), lines, turn(-1), turn(-2))
    return [jnp.where(inner, part, 0.0) for part in parts]


def edge_sums(part, root):
    rows, lanes = part.shape
    tiles = [part[k : k + TILE] for k in range(0, rows, TILE)]
    step = float(root**TILE)
    low, high = tiles[-1], tiles[0]
    for tile in tiles[-2::-1]:
        low = low * step + tile
    for tile in tiles[1:]:
        high = high * step + tile
    at = iota((TILE, lanes), 0)
    low = low * powers(root, at)
    high = high * powers(root, TILE - 1 - at)
    return jnp.sum(low, axis=0, keepdims=True), jnp.sum(high, axis=0, keepdims=True)


def own_edges(lines):
    rows = lines.shape[0]
    sums = [edge_sums(part, root) for part, root in zip(right_sides(lines), ROOTS)]
    low = [lines[k : k + 1] for k in range(4)], [sums[0][0], sums[1][0]]
    high = [lines[rows - 1 - k : rows - k] for k in range(4)], [sums[0][1], sums[1][1]]
    return low, high


def sent_rows(layers, sums, sign):
    b1, b2, b3, b4 = layers
    d2, d3, d4 = b2 - b1, b3 - b1, b4 - b1
    one, two = ROOTS
    first = 7.0 / 9.0 * (d2 + one * d3) + 1.0 / 36.0 * (d3 + one * d4)
    second = 12.0 / 11.0 * (d2 + two * (d3 - 2.0 * d2)) + 3.0 / 44.0 * (d3 + two * (d4 - 2.0 * d2))
    return [b1, b2, sums[0] - sign * first, sums[1] + second]


def received_sums(layers, received, sign):
    a1, a2 = layers[0] - received[0], layers[1] - received[0]
    one, two = ROOTS
    first = 7.0 / 9.0 * a1 + 1.0 / 36.0 * (a2 + one * a1)
    second = 12.0 / 11.0 * a1 + 3.0 / 44.0 * (a2 + two * a1)
    return received[2] + sign * first, received[3] + second


def turned(field):
    slabs, rows, lanes = field.shape
    fill = -(slabs * rows) % lanes
    lines = field.reshape(slabs * rows, lanes)
    if fill:
        lines = jnp.concatenate([lines, jnp.zeros((fill, lanes), jnp.float32)], axis=0)
    return jnp.transpose(lines)


def beyond(way, kind):
    return kind ^ 2 if way in "eo" else kind ^ 1


def arrival_rounds(way):
    return [
        next(k for k, ways in enumerate(ROUNDS) if ways[beyond(way, kind)] == way)
        for kind in range(4)
    ]


def by_kind(options):
    x_even = lax.rem(lax.axis_index("gx"), 2) == 0
    y_even = lax.rem(lax.axis_index("gy"), 2) == 0
    choose = lambda flag, one, two: one if one is two else jnp.where(flag, one, two)
    return choose(
        x_even, choose(y_even, options[0], options[1]), choose(y_even, options[2], options[3])
    )


def sends(edges, even, rows):
    low = [sent_rows(*at_low, -1.0) for at_low, _ in edges]
    high = [sent_rows(*at_high, 1.0) for _, at_high in edges]
    fill = rows - 4 * len(edges)
    fill = [jnp.zeros((fill, low[0][0].shape[1]), jnp.float32)] if fill else []
    from_low = jnp.concatenate([rows_of[k] for k in range(4) for rows_of in low] + fill, axis=0)
    from_high = jnp.concatenate([rows_of[k] for k in range(4) for rows_of in high] + fill, axis=0)
    return jnp.where(even, from_high, from_low), jnp.where(even, from_low, from_high)


def send_kernel(field, *outs):
    *outs, y_own = outs
    slabs, _, lanes = field.shape
    x_even = lax.rem(lax.axis_index("gx"), 2) == 0
    y_even = lax.rem(lax.axis_index("gy"), 2) == 0
    rows = outs[0].shape[0]
    lines = turned(field[...])
    edges = [own_edges(lines[:, k : k + lanes]) for k in range(0, lines.shape[1], lanes)]
    sent = {}
    sent["1"], sent["2"] = sends(edges, y_even, rows)
    for side in range(2):
        for k in range(6):
            values = [(edge[side][0] + edge[side][1])[k] for edge in edges]
            y_own[6 * side + k, : len(values)] = jnp.concatenate(values, axis=0)
    edges = [own_edges(field[s]) for s in range(slabs)]
    sent["e"], sent["o"] = sends(edges, x_even, rows)
    for out, ways in zip(outs, ROUNDS):
        out[...] = by_kind([sent[way] for way in ways])


def inverse_matrix(system, size):
    root, gain = decay(COEFS[system])
    return gain * powers(root, jnp.abs(iota((size, size), 0) - iota((size, size), 1)))


def solve(matrix, right_side):
    return jnp.dot(matrix, right_side, precision=HIGHEST, preferred_element_type=jnp.float32)


def bulk_kernel(field, stretch, metric, out, slope_turned, bend_turned, x_own):
    slabs, rows, lanes = field.shape
    position = pl.ds(lax.axis_index("gy"), 1)
    inv = 1.0 / stretch[position, :]
    curve = VISCOSITY * metric[position, :] * inv * inv * inv
    bend = jnp.transpose(jnp.broadcast_to(VISCOSITY * inv * inv, (lanes, lanes)))
    bend_turned[...] = bend
    slope = [-(field[plane * 3 + 1] * inv + curve) for plane in range(slabs // 3)]
    slope = turned(jnp.stack([part for part in slope for _ in range(3)], axis=0))
    slope_turned[...] = slope
    first, second = right_sides(turned(field[...]))
    y_term = slope * solve(inverse_matrix(0, lanes), first)
    y_term += bend[:, :1] * solve(inverse_matrix(1, lanes), second)
    y_term = jnp.transpose(y_term)
    matrices = [inverse_matrix(system, rows) for system in range(2)]
    for s in range(slabs):
        first, second = right_sides(field[s])
        x_term = VISCOSITY * solve(matrices[1], second) - field[s // 3 * 3] * solve(matrices[0], first)
        out[s] = x_term + y_term[s * rows : (s + 1) * rows]
        for k in range(4):
            x_own[k, s : s + 1] = field[s, k : k + 1]
            x_own[4 + k, s : s + 1] = field[s, rows - 1 - k : rows - k]


def edge_rows(own, received, sign):
    a1, a2, a3, a4 = own
    b1, b2 = received[:2]
    f0, s0 = stencils(b2, b1, a1, a2, a3)
    f1, s1 = stencils(b1, a1, a2, a3, a4)
    first_sum, second_sum = received_sums(own, received, sign)
    return (sign * f0, sign * f1, first_sum), (s0, s1, second_sum)


def wall_rows(own, sums, sign):
    a1, a2, a3, a4 = own
    first = (sign * 0.5 * (4.0 * a2 - 3.0 * a1 - a3), sign * 0.75 * (a3 - a1), sums[0])
    second = (2.0 * a1 - 5.0 * a2 + 4.0 * a3 - a4, 1.2 * (a3 - 2.0 * a2 + a1), sums[1])
    return first, second


def weigh(weights, values):
    return weights[0] * values[0] + weights[1] * values[1] + weights[2] * values[2]


def edge_numbers(own, received, sign, wall=None, sums=None):
    rows = edge_rows(own, received, sign)
    at_wall = None if wall is None else wall_rows(own, sums, sign)
    numbers = []
    for system in range(2):
        pair = [weigh(weights, rows[system]) for weights in inner_weights(system)]
        if wall is not None:
            other = [weigh(weights, at_wall[system]) for weights in wall_weights(system)]
            pair = [jnp.where(wall, there, here) for there, here in zip(other, pair)]
        numbers.append(pair)
    return numbers


def edge_tiles(pair, root, sign):
    at = iota((TILE, pair[0].shape[1]), 0)
    at = at if sign > 0 else TILE - 1 - at
    far = powers(root, at) * pair[0]
    return jnp.where(at == 0, pair[1], far), far


def line_tiles(numbers, line, sign):
    lines = [[part[line : line + 1] for part in pair] for pair in numbers]
    return [edge_tiles(pair, root, sign) for pair, root in zip(lines, ROOTS)]


def received(way, moved, groups):
    rounds = arrival_rounds(way)
    numbers = []
    for k in range(4):
        values = [part[k * groups : (k + 1) * groups, :] for part in moved]
        numbers.append(by_kind([values[at] for at in rounds]))
    return numbers


def select(flag, one, two):
    return [jnp.where(flag, there, here) for there, here in zip(one, two)]


def edge_update(low, high, root, tile, tiles):
    step = root**TILE
    up, down = tile, tiles - 1 - tile
    from_low = low[0] if up == 0 else low[1] * float(step**up)
    from_high = high[0] if down == 0 else high[1] * float(step**down)
    return from_low + from_high


def final_kernel(
    field, bulk, slope, bend, x_own, y_own, *refs
):
    *moved, out, block, sems = refs
    slabs, rows, lanes = field.shape
    y_at, y_count = lax.axis_index("gy"), lax.axis_size("gy")
    x_even = lax.rem(lax.axis_index("gx"), 2) == 0
    y_even = lax.rem(y_at, 2) == 0
    groups = slope.shape[1] // lanes
    own = [y_own[k, :groups] for k in range(12)]
    even, odd = [received(way, moved, groups) for way in "12"]
    from_low, from_high = select(y_even, odd, even), select(y_even, even, odd)
    low = edge_numbers(own[:4], from_low, 1.0, y_at == 0, own[4:6])
    high = edge_numbers(own[6:10], from_high, -1.0, y_at == y_count - 1, own[10:])
    tiles = lanes // TILE
    y_term = []
    for group in range(groups):
        at_low, at_high = line_tiles(low, group, 1.0), line_tiles(high, group, -1.0)
        part = slice(group * lanes, (group + 1) * lanes)
        column = []
        for tile in range(tiles):
            place = slice(tile * TILE, (tile + 1) * TILE)
            one, two = [edge_update(at_low[k], at_high[k], ROOTS[k], tile, tiles) for k in range(2)]
            column.append(slope[place, part] * one + bend[place, :] * two)
        y_term.append(jnp.transpose(jnp.concatenate(column, axis=0)))
    y_term = jnp.concatenate(y_term, axis=0)
    own = [x_own[k, :slabs] for k in range(8)]
    even, odd = [received(way, moved, slabs) for way in "eo"]
    low = edge_numbers(own[:4], select(x_even, odd, even), 1.0)
    high = edge_numbers(own[4:], select(x_even, even, odd), -1.0)
    tiles = rows // TILE
    copies = []
    for s in range(slabs):
        at_low, at_high = line_tiles(low, s, 1.0), line_tiles(high, s, -1.0)
        for tile in range(tiles):
            place = slice(tile * TILE, (tile + 1) * TILE)
            one, two = [edge_update(at_low[k], at_high[k], ROOTS[k], tile, tiles) for k in range(2)]
            turned = y_term[s * rows + tile * TILE : s * rows + (tile + 1) * TILE]
            x_term = VISCOSITY * two - field[s // 3 * 3, place] * one
            block[s, place] = bulk[s, place] + x_term + turned
        copies.append(pltpu.make_async_copy(block.at[s], out.at[s], sems.at[s]))
        copies[-1].start()
    for copy in copies:
        copy.wait()


def partner(way, x, y, x_count, y_count):
    if way == "2" and y in (0, y_count - 1):
        way = "e"
    if way in "eo":
        step = 1 if (x % 2 == 0) == (way == "e") else -1
        return (x + step) % x_count, y
    return x, y + (1 if (y % 2 == 0) == (way == "1") else -1)


def exchange_pairs(ways, x_count, y_count):
    at = lambda x, y: x * y_count + y
    return [
        (at(x, y), at(*partner(ways[x % 2 * 2 + y % 2], x, y, x_count, y_count)))
        for x in range(x_count)
        for y in range(y_count)
    ]


def call(kernel, outs, name, flops, out_space=pltpu.VMEM, scratch=()):
    vmem = pl.BlockSpec(memory_space=pltpu.VMEM)
    return lambda *args: pl.pallas_call(
        kernel,
        out_shape=outs,
        in_specs=[vmem] * len(args),
        out_specs=[pl.BlockSpec(memory_space=out_space)] * len(outs),
        scratch_shapes=scratch,
        cost_estimate=pl.CostEstimate(flops=flops, bytes_accessed=10**6, transcendentals=0),
        compiler_params=pltpu.CompilerParams(vmem_limit_bytes=8 * 2**20),
        name=name,
    )(*args)


def shards(velocity, stretch, second_metric):
    planes, comps, rows, lanes = velocity.shape
    slabs = planes * comps
    x_count, y_count = lax.axis_size("gx"), lax.axis_size("gy")
    field = velocity.reshape(slabs, rows, lanes)
    stretch = stretch.reshape(y_count, lanes)
    metric = second_metric.reshape(y_count, lanes)

    shape = lambda *dims: jax.ShapeDtypeStruct(dims, jnp.float32)
    groups = -(-slabs * rows // lanes)
    send = shape(4 * max(slabs, groups), lanes)
    *sent, y_own = call(send_kernel, [send] * len(ROUNDS) + [shape(12, TILE, lanes)], "sends", 10**6)(field)
    moved = [
        lax.ppermute(value, ("gx", "gy"), exchange_pairs(ways, x_count, y_count))
        for value, ways in zip(sent, ROUNDS)
    ]
    block = shape(slabs, rows, lanes)
    *bulk, x_own = call(
        bulk_kernel,
        [block, shape(lanes, groups * lanes), shape(lanes, lanes), shape(8, TILE, lanes)],
        "bulk",
        10**8,
    )(field, stretch, metric)
    (out,) = call(
        final_kernel,
        [block],
        "final",
        10**7,
        pl.ANY,
        [pltpu.VMEM(block.shape, jnp.float32), pltpu.SemaphoreType.DMA((slabs,))],
    )(field, *bulk, x_own, y_own, *moved)
    return out.reshape(planes, comps, rows, lanes)


def solution(mesh):
    return jax.shard_map(
        shards,
        mesh=mesh,
        in_specs=(P(None, None, "gx", "gy"), P(), P()),
        out_specs=P(None, None, "gx", "gy"),
        check_vma=False,
    )
```

time: 9.99 us -> 8.93 us (0.89)
  the two profiles are of different devices: /device:TPU:0 before, /device:TPU:8 now
where the time goes in v3:
time: 8.93 us; the launch traced here: 8.78 us
  starting transfers between devices  4.26 us (48%)
  Pallas kernels  2.44 us (27%)
  waiting for transfers between devices  1.11 us (12%)
  local copies, waits for them, and re-layouts  0.92 us (10%)
    ppermute x4, starting transfers between devices, shards(): lax.ppermute(value, ('gx', 'gy'), exchange_pairs(ways, x_count, y_count))  4.26 us
    pallas_call x3, Pallas kernels, call(): pl.pallas_call(kernel, out_shape=outs, in_specs=[vmem] * len(args), out_s...  2.44 us
    ppermute x4, waiting for transfers between devices, shards(): lax.ppermute(value, ('gx', 'gy'), exchange_pairs(ways, x_count, y_count))  1.11 us
    unnamed x6, local copies, waits for them, and re-layouts  0.92 us
  transfers between devices with their start and end apart: 4, of which 1 were waited for; matrix products, arithmetic and copies ran while one was open for 0% of the time, Pallas kernels for 12%

profile of v3, /device:TPU:8, one launch (start us, length us, event | category | flops | bytes accessed | tf_op | source)
XLA Modules:
  0.0 8.8 jit_solution(9183289774972627718)
XLA Ops:
  0.0 0.0 copy-start
  0.0 0.9 %copy-done = f32[2,3,48,128]{3,2,1,0:T(8,128)S(1)} copy-done((f32[2,3,48,128]{3,2,1,0:T(8,128)S(1)}, f32[2,3,48,128]{3,2,1,0:T(8,128)}, u32[]{:S(2)}) %copy-start) | copy-done | bytes 147480
  0.9 0.5 %sends.1 = (f32[24,128]{1,0:T(8,128)S(1)}, f32[24,128]{1,0:T(8,128)S(1)}, f32[24,128]{1,0:T(8,128)S(1)}, f32[24,128]{1,0:T(8,128)S(1)}, f32[12,8,128]{2,1,0:T(8,128)S(1)}) custom-call(f32[6,48,128]{2,1,0:T(8,128)S(1)} %bitcast.4), custom_call_target="tpu_custom_call" | custom-call | flops 1000000 | bytes 1000000 | tf_op jit(solution)/shard_map/sends/pallas_call | solution.py:331
  1.5 0.1 collective-permute-start
  1.5 0.1 collective-permute-start.1
  1.6 2.6 %collective-permute-start.2 = (f32[24,128]{1,0:T(8,128)S(1)}, f32[24,128]{1,0:T(8,128)S(1)}, u32[]{:S(2)}, u32[]{:S(2)}) collective-permute-start(f32[24,128]{1,0:T(8,128)S(1)} %get-tuple-element.21), channel_id=1, source_target_pairs={{0,1},{1,29},{2,3},{3,31},{4,0},{5,4},{6,2},{7,6},{8,9},{9,5},{10,... | collective-permute-start | bytes 36872 | tf_op jit(solution)/shard_map/ppermute | solution.py:356
  4.2 0.0 copy-start.2
  4.2 0.0 copy-start.1
  4.2 1.5 %collective-permute-start.3 = (f32[24,128]{1,0:T(8,128)S(1)}, f32[24,128]{1,0:T(8,128)S(1)}, u32[]{:S(2)}, u32[]{:S(2)}) collective-permute-start(f32[24,128]{1,0:T(8,128)S(1)} %get-tuple-element.22), channel_id=1, source_target_pairs={{0,4},{1,2},{2,1},{3,7},{4,0},{5,6},{6,5},{7,3},{8,12},{9,10},{10,... | collective-permute-start | bytes 36872 | tf_op jit(solution)/shard_map/ppermute | solution.py:356
  5.7 0.0 copy-done.2
  5.7 0.0 copy-done.1
  5.7 1.1 %bulk.1 = (f32[6,48,128]{2,1,0:T(8,128)S(1)}, f32[128,384]{1,0:T(8,128)S(1)}, f32[128,128]{1,0:T(8,128)S(1)}, f32[8,8,128]{2,1,0:T(8,128)S(1)}) custom-call(f32[6,48,128]{2,1,0:T(8,128)S(1)} %bitcast.5, f32[4,128]{1,0:T(4,128)S(1)} %bitcast.7, f32[4,128]{1,0:T(4,128)S(1)} %bitcast.8), custom_call_target="tpu_custom_call" | custom-call | flops 100000000 | bytes 1000000 | tf_op jit(solution)/shard_map/bulk/pallas_call | solution.py:331
  6.8 0.0 collective-permute-done.refs_0_
  6.8 0.0 collective-permute-done.1.refs_1_
  6.8 0.0 collective-permute-done.2.refs_2_
  6.8 1.1 %collective-permute-done.3.refs_3_ = f32[24,128]{1,0:T(8,128)S(1)} collective-permute-done((f32[24,128]{1,0:T(8,128)S(1)}, f32[24,128]{1,0:T(8,128)S(1)}, u32[]{:S(2)}, u32[]{:S(2)}) %collective-permute-start.3) | collective-permute-done | bytes 12320 | tf_op jit(solution)/shard_map/ppermute | solution.py:356
  7.9 0.9 %final.1 = f32[6,48,128]{2,1,0:T(8,128)} custom-call(f32[6,48,128]{2,1,0:T(8,128)S(1)} %bitcast.6, f32[6,48,128]{2,1,0:T(8,128)S(1)} %get-tuple-element.14.bulk, f32[128,384]{1,0:T(8,128)S(1)} %get-tuple-element.15.slope, f32[128,128]{1,0:T(8,128)S(1)} %get-tuple-element.16.bend, f32[8,8,128]{2,1,0:T(8,128)S(1)} %get-tuple-element.17.x_own, ...), custom_call_target="tpu_custom_call" | custom-call | flops 10000000 | bytes 1000000 | tf_op jit(solution)/shard_map/final/pallas_call | solution.py:331
Async XLA Ops:
  0.0 0.9 %copy-start = (f32[2,3,48,128]{3,2,1,0:T(8,128)S(1)}, f32[2,3,48,128]{3,2,1,0:T(8,128)}, u32[]{:S(2)}) copy-start(f32[2,3,48,128]{3,2,1,0:T(8,128)} %param.3) | copy-start | bytes 442372
  1.5 5.3 %collective-permute-start = (f32[24,128]{1,0:T(8,128)S(1)}, f32[24,128]{1,0:T(8,128)S(1)}, u32[]{:S(2)}, u32[]{:S(2)}) collective-permute-start(f32[24,128]{1,0:T(8,128)S(1)} %get-tuple-element.19), channel_id=1, source_target_pairs={{0,4},{1,5},{2,6},{3,7},{4,8},{5,1},{6,10},{7,3},{8,12},{9,13},{10... | collective-permute-start | bytes 36872 | tf_op jit(solution)/shard_map/ppermute | solution.py:356
  1.5 5.3 %collective-permute-start.1 = (f32[24,128]{1,0:T(8,128)S(1)}, f32[24,128]{1,0:T(8,128)S(1)}, u32[]{:S(2)}, u32[]{:S(2)}) collective-permute-start(f32[24,128]{1,0:T(8,128)S(1)} %get-tuple-element.20), channel_id=1, source_target_pairs={{0,28},{1,0},{2,30},{3,2},{4,5},{5,9},{6,7},{7,11},{8,4},{9,8},{10... | collective-permute-start | bytes 36872 | tf_op jit(solution)/shard_map/ppermute | solution.py:356
  1.6 5.2 %collective-permute-start.2 = (f32[24,128]{1,0:T(8,128)S(1)}, f32[24,128]{1,0:T(8,128)S(1)}, u32[]{:S(2)}, u32[]{:S(2)}) collective-permute-start(f32[24,128]{1,0:T(8,128)S(1)} %get-tuple-element.21), channel_id=1, source_target_pairs={{0,1},{1,29},{2,3},{3,31},{4,0},{5,4},{6,2},{7,6},{8,9},{9,5},{10,... | collective-permute-start | bytes 36872 | tf_op jit(solution)/shard_map/ppermute | solution.py:356
  4.2 1.5 %copy-start.2 = (f32[512]{0:T(512)S(1)}, f32[512]{0:T(512)}, u32[]{:S(2)}) copy-start(f32[512]{0:T(512)} %param.5) | copy-start | bytes 6148
  4.2 1.5 %copy-start.1 = (f32[512]{0:T(512)S(1)}, f32[512]{0:T(512)}, u32[]{:S(2)}) copy-start(f32[512]{0:T(512)} %param.4) | copy-start | bytes 6148
  4.2 3.7 %collective-permute-start.3 = (f32[24,128]{1,0:T(8,128)S(1)}, f32[24,128]{1,0:T(8,128)S(1)}, u32[]{:S(2)}, u32[]{:S(2)}) collective-permute-start(f32[24,128]{1,0:T(8,128)S(1)} %get-tuple-element.22), channel_id=1, source_target_pairs={{0,4},{1,2},{2,1},{3,7},{4,0},{5,6},{6,5},{7,3},{8,12},{9,10},{10,... | collective-permute-start | bytes 36872 | tf_op jit(solution)/shard_map/ppermute | solution.py:356

commit v4 on v3

--- a/solution.py
+++ b/solution.py
@@ -11,7 +11,13 @@
 WALL_COEFS = (1.0 / 4.0, 1.0 / 10.0)
 HIGHEST = lax.Precision.HIGHEST
 TILE = 8
-ROUNDS = ("eeoe", "o11o", "1oe1", "2222")
+WAYS = "eo12"
+ROUNDS = (
+    "2oeo22eooe22oeo2",
+    "o211oo2e11ooe22o",
+    "1eoee1o2eo1e2oe1",
+    "e1221e1122e1111e",
+)
 
 
 def decay(coef):
@@ -64,7 +70,7 @@
     return [jnp.where(inner, part, 0.0) for part in parts]
 
 
-def edge_sums(part, root):
+def tile_sums(part, root):
     rows, lanes = part.shape
     tiles = [part[k : k + TILE] for k in range(0, rows, TILE)]
     step = float(root**TILE)
@@ -79,12 +85,43 @@
     return jnp.sum(low, axis=0, keepdims=True), jnp.sum(high, axis=0, keepdims=True)
 
 
-def own_edges(lines):
+def difference_sums(lines):
     rows = lines.shape[0]
-    sums = [edge_sums(part, root) for part, root in zip(right_sides(lines), ROOTS)]
-    low = [lines[k : k + 1] for k in range(4)], [sums[0][0], sums[1][0]]
-    high = [lines[rows - 1 - k : rows - k] for k in range(4)], [sums[0][1], sums[1][1]]
-    return low, high
+    at = iota(lines.shape, 0)
+    first = jnp.where(at == rows - 1, 0.0, pltpu.roll(lines, rows - 1, 0) - lines)
+    second = jnp.where((at == 0) | (at == rows - 1), 0.0, first - pltpu.roll(first, 1, 0))
+    return *tile_sums(first, ROOTS[0]), *tile_sums(second, ROOTS[1])
+
+
+def right_side_sums(layers, sums, rows):
+    (one, two), size = ROOTS, rows
+    steps = [[line[k + 1] - line[k] for k in range(3)] for line in layers]
+    bends = [[line[k + 1] - line[k] for k in range(2)] for line in steps]
+    near, far = 7.0 / 9.0 + 1.0 / 36.0, 1.0 / 36.0
+    mid, side = 12.0 / 11.0 + 6.0 / 44.0, 3.0 / 44.0
+    result = []
+    for end in range(2):
+        d0, d1, d2 = steps[end]
+        z0, z1, z2 = [-step for step in steps[1 - end]]
+        e1, e2 = bends[end]
+        y1, y2 = bends[1 - end]
+        total = sums[0] if end == 0 else sums[1] * float(-1.0 / one)
+        last0, last1, last2 = [z * float(one ** (size - 2 - k)) for k, z in enumerate((z0, z1, z2))]
+        first = (
+            near * (total - d0 - one * d1 - last0)
+            + (near * one) * (total - d0 - last0 - last1)
+            + (far / one) * (total - d0 - one * d1 - one * one * d2)
+            + (far * one * one) * (total - last0 - last1 - last2)
+        )
+        total = sums[2 + end]
+        last1, last2 = y1 * float(two ** (size - 2)), y2 * float(two ** (size - 3))
+        second = (
+            mid * (total - two * e1 - last1)
+            + (side / two) * (total - two * e1 - two * two * e2)
+            + (side * two) * (total - last1 - last2)
+        )
+        result.append((first if end == 0 else -first, second))
+    return result
 
 
 def sent_rows(layers, sums, sign):
@@ -113,54 +150,74 @@
     return jnp.transpose(lines)
 
 
+def kind_of(x, y):
+    return 8 * (x % 2) + 4 * (x // 2 % 2) + 2 * (y % 2) + y // 2 % 2
+
+
 def beyond(way, kind):
-    return kind ^ 2 if way in "eo" else kind ^ 1
+    return kind ^ {"e": 8, "o": 12, "1": 2, "2": 3}[way]
 
 
 def arrival_rounds(way):
     return [
         next(k for k, ways in enumerate(ROUNDS) if ways[beyond(way, kind)] == way)
-        for kind in range(4)
+        for kind in range(16)
     ]
 
 
-def by_kind(options):
-    x_even = lax.rem(lax.axis_index("gx"), 2) == 0
-    y_even = lax.rem(lax.axis_index("gy"), 2) == 0
-    choose = lambda flag, one, two: one if one is two else jnp.where(flag, one, two)
-    return choose(
-        x_even, choose(y_even, options[0], options[1]), choose(y_even, options[2], options[3])
-    )
-
-
-def sends(edges, even, rows):
-    low = [sent_rows(*at_low, -1.0) for at_low, _ in edges]
-    high = [sent_rows(*at_high, 1.0) for _, at_high in edges]
-    fill = rows - 4 * len(edges)
-    fill = [jnp.zeros((fill, low[0][0].shape[1]), jnp.float32)] if fill else []
-    from_low = jnp.concatenate([rows_of[k] for k in range(4) for rows_of in low] + fill, axis=0)
-    from_high = jnp.concatenate([rows_of[k] for k in range(4) for rows_of in high] + fill, axis=0)
-    return jnp.where(even, from_high, from_low), jnp.where(even, from_low, from_high)
-
-
-def send_kernel(field, *outs):
-    *outs, y_own = outs
+def by_kind(numbers, options):
+    packed = np.int64(sum(number << 2 * kind for kind, number in enumerate(numbers)))
+    kind = kind_of(lax.axis_index("gx"), lax.axis_index("gy"))
+    number = lax.shift_right_logical(jnp.int32(packed.astype(np.int32)), 2 * kind) & 3
+    first, *others = sorted(set(numbers))
+    chosen = options[first]
+    for other in others:
+        chosen = jnp.where(number == other, options[other], chosen)
+    return chosen
+
+
+def ends_of(groups):
+    rows = groups[0].shape[0]
+    stack = lambda values: jnp.concatenate(values, axis=0)
+    layers = [
+        [stack([group[at : at + 1] for group in groups]) for at in range(4)],
+        [stack([group[rows - 1 - at : rows - at] for group in groups]) for at in range(4)],
+    ]
+    sums = [stack(values) for values in zip(*[difference_sums(group) for group in groups])]
+    return layers, right_side_sums(layers, sums, rows)
+
+
+def sends(layers, sums, even):
+    low = sent_rows(layers[0], sums[0], -1.0)
+    high = sent_rows(layers[1], sums[1], 1.0)
+    return select(even, high, low), select(even, low, high)
+
+
+def send_kernel(field, stretch, metric, _, *refs):
+    *outs, metrics, x_own, y_own = refs
+    metrics[...] = metric_rows(stretch, metric)
     slabs, _, lanes = field.shape
     x_even = lax.rem(lax.axis_index("gx"), 2) == 0
     y_even = lax.rem(lax.axis_index("gy"), 2) == 0
-    rows = outs[0].shape[0]
+    groups = [field[s] for s in range(slabs)]
+    layers, sums = ends_of(groups)
+    sent = dict(zip("eo", sends(layers, sums, x_even)))
+    for k, layer in enumerate(layers[0] + layers[1]):
+        x_own[k, :slabs] = layer
     lines = turned(field[...])
-    edges = [own_edges(lines[:, k : k + lanes]) for k in range(0, lines.shape[1], lanes)]
-    sent = {}
-    sent["1"], sent["2"] = sends(edges, y_even, rows)
-    for side in range(2):
-        for k in range(6):
-            values = [(edge[side][0] + edge[side][1])[k] for edge in edges]
-            y_own[6 * side + k, : len(values)] = jnp.concatenate(values, axis=0)
-    edges = [own_edges(field[s]) for s in range(slabs)]
-    sent["e"], sent["o"] = sends(edges, x_even, rows)
+    layers, sums = ends_of([lines[:, k : k + lanes] for k in range(0, lines.shape[1], lanes)])
+    sent.update(zip("12", sends(layers, sums, y_even)))
+    for k, values in enumerate([*layers[0], *sums[0], *layers[1], *sums[1]]):
+        y_own[k, : values.shape[0]] = values
     for out, ways in zip(outs, ROUNDS):
-        out[...] = by_kind([sent[way] for way in ways])
+        count = out.shape[0] // 4
+        options = {}
+        for number, way in enumerate(WAYS):
+            if way in ways:
+                fill = jnp.zeros((count - sent[way][0].shape[0], lanes), jnp.float32)
+                parts = [part for value in sent[way] for part in (value, fill) if part.shape[0]]
+                options[number] = jnp.concatenate(parts, axis=0)
+        out[...] = by_kind([WAYS.index(way) for way in ways], options)
 
 
 def inverse_matrix(system, size):
@@ -172,28 +229,35 @@
     return jnp.dot(matrix, right_side, precision=HIGHEST, preferred_element_type=jnp.float32)
 
 
-def bulk_kernel(field, stretch, metric, out, slope_turned, bend_turned, x_own):
-    slabs, rows, lanes = field.shape
+def table_kernel(y_out, x_out):
+    for system in range(2):
+        y_out[system] = inverse_matrix(system, y_out.shape[1])
+        x_out[system] = inverse_matrix(system, x_out.shape[1])
+
+
+def metric_rows(stretch, metric):
     position = pl.ds(lax.axis_index("gy"), 1)
     inv = 1.0 / stretch[position, :]
     curve = VISCOSITY * metric[position, :] * inv * inv * inv
-    bend = jnp.transpose(jnp.broadcast_to(VISCOSITY * inv * inv, (lanes, lanes)))
+    fill = jnp.zeros((TILE - 3, inv.shape[1]), jnp.float32)
+    return jnp.concatenate([inv, curve, VISCOSITY * inv * inv, fill], axis=0)
+
+
+def bulk_kernel(field, metrics, y_matrix, x_matrix, out, slope_turned, bend_turned):
+    slabs, rows, lanes = field.shape
+    inv, curve, bend = metrics[0:1, :], metrics[1:2, :], metrics[2:3, :]
+    bend = jnp.transpose(jnp.broadcast_to(bend, (lanes, lanes)))
     bend_turned[...] = bend
     slope = [-(field[plane * 3 + 1] * inv + curve) for plane in range(slabs // 3)]
     slope = turned(jnp.stack([part for part in slope for _ in range(3)], axis=0))
     slope_turned[...] = slope
     first, second = right_sides(turned(field[...]))
-    y_term = slope * solve(inverse_matrix(0, lanes), first)
-    y_term += bend[:, :1] * solve(inverse_matrix(1, lanes), second)
+    y_term = slope * solve(y_matrix[0], first) + bend[:, :1] * solve(y_matrix[1], second)
     y_term = jnp.transpose(y_term)
-    matrices = [inverse_matrix(system, rows) for system in range(2)]
     for s in range(slabs):
         first, second = right_sides(field[s])
-        x_term = VISCOSITY * solve(matrices[1], second) - field[s // 3 * 3] * solve(matrices[0], first)
+        x_term = VISCOSITY * solve(x_matrix[1], second) - field[s // 3 * 3] * solve(x_matrix[0], first)
         out[s] = x_term + y_term[s * rows : (s + 1) * rows]
-        for k in range(4):
-            x_own[k, s : s + 1] = field[s, k : k + 1]
-            x_own[4 + k, s : s + 1] = field[s, rows - 1 - k : rows - k]
 
 
 def edge_rows(own, received, sign):
@@ -245,8 +309,10 @@
     rounds = arrival_rounds(way)
     numbers = []
     for k in range(4):
-        values = [part[k * groups : (k + 1) * groups, :] for part in moved]
-        numbers.append(by_kind([values[at] for at in rounds]))
+        values = {
+            at: moved[at][pl.ds(k * (moved[at].shape[0] // 4), groups), :] for at in set(rounds)
+        }
+        numbers.append(by_kind(rounds, values))
     return numbers
 
 
@@ -320,21 +386,20 @@
 def exchange_pairs(ways, x_count, y_count):
     at = lambda x, y: x * y_count + y
     return [
-        (at(x, y), at(*partner(ways[x % 2 * 2 + y % 2], x, y, x_count, y_count)))
+        (at(x, y), at(*partner(ways[kind_of(x, y)], x, y, x_count, y_count)))
         for x in range(x_count)
         for y in range(y_count)
     ]
 
 
 def call(kernel, outs, name, flops, out_space=pltpu.VMEM, scratch=()):
-    vmem = pl.BlockSpec(memory_space=pltpu.VMEM)
     return lambda *args: pl.pallas_call(
         kernel,
         out_shape=outs,
-        in_specs=[vmem] * len(args),
+        in_specs=[pl.BlockSpec(memory_space=pltpu.VMEM)] * len(args),
         out_specs=[pl.BlockSpec(memory_space=out_space)] * len(outs),
         scratch_shapes=scratch,
-        cost_estimate=pl.CostEstimate(flops=flops, bytes_accessed=10**6, transcendentals=0),
+        cost_estimate=pl.CostEstimate(flops=flops, bytes_accessed=0, transcendentals=0),
         compiler_params=pltpu.CompilerParams(vmem_limit_bytes=8 * 2**20),
         name=name,
     )(*args)
@@ -344,25 +409,29 @@
     planes, comps, rows, lanes = velocity.shape
     slabs = planes * comps
     x_count, y_count = lax.axis_size("gx"), lax.axis_size("gy")
-    field = velocity.reshape(slabs, rows, lanes)
     stretch = stretch.reshape(y_count, lanes)
     metric = second_metric.reshape(y_count, lanes)
-
     shape = lambda *dims: jax.ShapeDtypeStruct(dims, jnp.float32)
+    block = shape(slabs, rows, lanes)
+    move = lambda value, ways: lax.ppermute(
+        value, ("gx", "gy"), exchange_pairs(ways, x_count, y_count)
+    )
+
+    tables = call(table_kernel, [shape(2, lanes, lanes), shape(2, rows, rows)], "tables", 10**8)()
+    field = velocity.reshape(slabs, rows, lanes)
     groups = -(-slabs * rows // lanes)
     send = shape(4 * max(slabs, groups), lanes)
-    *sent, y_own = call(send_kernel, [send] * len(ROUNDS) + [shape(12, TILE, lanes)], "sends", 10**6)(field)
-    moved = [
-        lax.ppermute(value, ("gx", "gy"), exchange_pairs(ways, x_count, y_count))
-        for value, ways in zip(sent, ROUNDS)
-    ]
-    block = shape(slabs, rows, lanes)
-    *bulk, x_own = call(
-        bulk_kernel,
-        [block, shape(lanes, groups * lanes), shape(lanes, lanes), shape(8, TILE, lanes)],
-        "bulk",
-        10**8,
-    )(field, stretch, metric)
+    *sent, metrics, x_own, y_own = call(
+        send_kernel,
+        [send] * len(ROUNDS)
+        + [shape(TILE, lanes), shape(8, TILE, lanes), shape(12, TILE, lanes)],
+        "sends",
+        10**6,
+    )(field, stretch, metric, tables[1])
+    moved = [move(value, ways) for value, ways in zip(sent, ROUNDS)]
+    bulk = call(
+        bulk_kernel, [block, shape(lanes, groups * lanes), shape(lanes, lanes)], "bulk", 10**8
+    )(field, metrics, *tables)
     (out,) = call(
         final_kernel,
         [block],

time: 8.93 us -> 8.37 us (0.937)
  the two profiles are of different devices: /device:TPU:8 before, /device:TPU:24 now
where the time goes in v4:
time: 8.37 us; the launch traced here: 8.23 us
  starting transfers between devices  2.92 us (35%)
  Pallas kernels  2.27 us (27%)
  waiting for transfers between devices  2.16 us (26%)
  local copies, waits for them, and re-layouts  0.84 us (10%)
    ppermute x4, starting transfers between devices, shards(): lax.ppermute(value, ('gx', 'gy'), exchange_pairs(ways, x_count, y_count))  2.92 us
    pallas_call x4, Pallas kernels, call(): pl.pallas_call(kernel, out_shape=outs, in_specs=[pl.BlockSpec(memory_spac...  2.27 us
    ppermute x4, waiting for transfers between devices, shards(): lax.ppermute(value, ('gx', 'gy'), exchange_pairs(ways, x_count, y_count))  2.16 us
    unnamed x6, local copies, waits for them, and re-layouts  0.84 us
  transfers between devices with their start and end apart: 4, of which 2 were waited for; matrix products, arithmetic and copies ran while one was open for 0% of the time, Pallas kernels for 12%

profile of v4, /device:TPU:24, one launch (start us, length us, event | category | flops | bytes accessed | tf_op | source)
XLA Modules:
  0.0 8.2 jit_solution(14557517324037955530)
XLA Ops:
  0.0 0.0 copy-start
  0.0 0.1 tables.1
  0.1 0.0 copy-start.2
  0.1 0.0 copy-start.1
  0.1 0.8 %copy-done = f32[2,3,48,128]{3,2,1,0:T(8,128)S(1)} copy-done((f32[2,3,48,128]{3,2,1,0:T(8,128)S(1)}, f32[2,3,48,128]{3,2,1,0:T(8,128)}, u32[]{:S(2)}) %copy-start) | copy-done | bytes 147480
  0.9 0.0 copy-done.2
  0.9 0.0 copy-done.1
  0.9 0.3 %sends.1 = (f32[24,128]{1,0:T(8,128)S(1)}, f32[24,128]{1,0:T(8,128)S(1)}, f32[24,128]{1,0:T(8,128)S(1)}, f32[24,128]{1,0:T(8,128)S(1)}, f32[8,128]{1,0:T(8,128)S...) custom-call(f32[6,48,128]{2,1,0:T(8,128)S(1)} %bitcast.4, f32[4,128]{1,0:T(4,128)S(1)} %bitcast.7, ...), custom_call_target="tpu_custom_call" | custom-call | flops 1000000 | tf_op jit(solution)/shard_map/sends/pallas_call | solution.py:396
  1.3 1.9 %collective-permute-start = (f32[24,128]{1,0:T(8,128)S(1)}, f32[24,128]{1,0:T(8,128)S(1)}, u32[]{:S(2)}, u32[]{:S(2)}) collective-permute-start(f32[24,128]{1,0:T(8,128)S(1)} %get-tuple-element.25), channel_id=1, source_target_pairs={{0,4},{1,5},{2,30},{3,31},{4,8},{5,6},{6,2},{7,3},{8,12},{9,13},{1... | collective-permute-start | bytes 36872 | tf_op jit(solution)/shard_map/ppermute | solution.py:416
  3.2 0.5 %collective-permute-start.1 = (f32[24,128]{1,0:T(8,128)S(1)}, f32[24,128]{1,0:T(8,128)S(1)}, u32[]{:S(2)}, u32[]{:S(2)}) collective-permute-start(f32[24,128]{1,0:T(8,128)S(1)} %get-tuple-element.26), channel_id=1, source_target_pairs={{0,28},{1,0},{2,1},{3,2},{4,5},{5,9},{6,7},{7,11},{8,4},{9,10},{10... | collective-permute-start | bytes 36872 | tf_op jit(solution)/shard_map/ppermute | solution.py:416
  3.7 0.0 collective-permute-start.2
  3.7 0.5 %collective-permute-start.3 = (f32[24,128]{1,0:T(8,128)S(1)}, f32[24,128]{1,0:T(8,128)S(1)}, u32[]{:S(2)}, u32[]{:S(2)}) collective-permute-start(f32[24,128]{1,0:T(8,128)S(1)} %get-tuple-element.28), channel_id=1, source_target_pairs={{0,4},{1,2},{2,3},{3,7},{4,0},{5,1},{6,5},{7,6},{8,9},{9,8},{10,14... | collective-permute-start | bytes 36872 | tf_op jit(solution)/shard_map/ppermute | solution.py:416
  4.2 1.0 %bulk.1 = (f32[6,48,128]{2,1,0:T(8,128)S(1)}, f32[128,384]{1,0:T(8,128)S(1)}, f32[128,128]{1,0:T(8,128)S(1)}) custom-call(f32[6,48,128]{2,1,0:T(8,128)S(1)} %bitcast.5, f32[8,128]{1,0:T(8,128)S(1)} %get-tuple-element.18.metrics, f32[2,128,128]{2,1,0:T(8,128)S(1)} %get-tuple-element.19.y_matrix, f32[2,48,48]{2,1,0:T(8,128)S(1)} %get-tuple-element.17._.x_matrix), custom_call_target="tpu_custom_call" | custom-call | flops 100000000 | tf_op jit(solution)/shard_map/bulk/pallas_call | solution.py:396
  5.2 0.0 collective-permute-done.refs_0_
  5.2 2.0 %collective-permute-done.1.refs_1_ = f32[24,128]{1,0:T(8,128)S(1)} collective-permute-done((f32[24,128]{1,0:T(8,128)S(1)}, f32[24,128]{1,0:T(8,128)S(1)}, u32[]{:S(2)}, u32[]{:S(2)}) %collective-permute-start.1) | collective-permute-done | bytes 12320 | tf_op jit(solution)/shard_map/ppermute | solution.py:416
  7.2 0.0 collective-permute-done.2.refs_2_
  7.2 0.1 %collective-permute-done.3.refs_3_ = f32[24,128]{1,0:T(8,128)S(1)} collective-permute-done((f32[24,128]{1,0:T(8,128)S(1)}, f32[24,128]{1,0:T(8,128)S(1)}, u32[]{:S(2)}, u32[]{:S(2)}) %collective-permute-start.3) | collective-permute-done | bytes 12320 | tf_op jit(solution)/shard_map/ppermute | solution.py:416
  7.4 0.9 %final.1 = f32[6,48,128]{2,1,0:T(8,128)} custom-call(f32[6,48,128]{2,1,0:T(8,128)S(1)} %bitcast.6, f32[6,48,128]{2,1,0:T(8,128)S(1)} %get-tuple-element.20.bulk, f32[128,384]{1,0:T(8,128)S(1)} %get-tuple-element.21.slope, f32[128,128]{1,0:T(8,128)S(1)} %get-tuple-element.22.bend, f32[8,8,128]{2,1,0:T(8,128)S(1)} %get-tuple-element.23.x_own, ...), custom_call_target="tpu_custom_call" | custom-call | flops 10000000 | tf_op jit(solution)/shard_map/final/pallas_call | solution.py:396
Async XLA Ops:
  0.0 0.9 %copy-start = (f32[2,3,48,128]{3,2,1,0:T(8,128)S(1)}, f32[2,3,48,128]{3,2,1,0:T(8,128)}, u32[]{:S(2)}) copy-start(f32[2,3,48,128]{3,2,1,0:T(8,128)} %param.3) | copy-start | bytes 442372
  0.1 0.8 %copy-start.2 = (f32[512]{0:T(512)S(1)}, f32[512]{0:T(512)}, u32[]{:S(2)}) copy-start(f32[512]{0:T(512)} %param.5) | copy-start | bytes 6148
  0.1 0.8 %copy-start.1 = (f32[512]{0:T(512)S(1)}, f32[512]{0:T(512)}, u32[]{:S(2)}) copy-start(f32[512]{0:T(512)} %param.4) | copy-start | bytes 6148
  1.3 3.9 %collective-permute-start = (f32[24,128]{1,0:T(8,128)S(1)}, f32[24,128]{1,0:T(8,128)S(1)}, u32[]{:S(2)}, u32[]{:S(2)}) collective-permute-start(f32[24,128]{1,0:T(8,128)S(1)} %get-tuple-element.25), channel_id=1, source_target_pairs={{0,4},{1,5},{2,30},{3,31},{4,8},{5,6},{6,2},{7,3},{8,12},{9,13},{1... | collective-permute-start | bytes 36872 | tf_op jit(solution)/shard_map/ppermute | solution.py:416
  3.2 4.0 %collective-permute-start.1 = (f32[24,128]{1,0:T(8,128)S(1)}, f32[24,128]{1,0:T(8,128)S(1)}, u32[]{:S(2)}, u32[]{:S(2)}) collective-permute-start(f32[24,128]{1,0:T(8,128)S(1)} %get-tuple-element.26), channel_id=1, source_target_pairs={{0,28},{1,0},{2,1},{3,2},{4,5},{5,9},{6,7},{7,11},{8,4},{9,10},{10... | collective-permute-start | bytes 36872 | tf_op jit(solution)/shard_map/ppermute | solution.py:416
  3.7 3.6 %collective-permute-start.2 = (f32[24,128]{1,0:T(8,128)S(1)}, f32[24,128]{1,0:T(8,128)S(1)}, u32[]{:S(2)}, u32[]{:S(2)}) collective-permute-start(f32[24,128]{1,0:T(8,128)S(1)} %get-tuple-element.27), channel_id=1, source_target_pairs={{0,1},{1,29},{2,6},{3,7},{4,0},{5,4},{6,10},{7,3},{8,12},{9,5},{10... | collective-permute-start | bytes 36872 | tf_op jit(solution)/shard_map/ppermute | solution.py:416
  3.7 3.7 %collective-permute-start.3 = (f32[24,128]{1,0:T(8,128)S(1)}, f32[24,128]{1,0:T(8,128)S(1)}, u32[]{:S(2)}, u32[]{:S(2)}) collective-permute-start(f32[24,128]{1,0:T(8,128)S(1)} %get-tuple-element.28), channel_id=1, source_target_pairs={{0,4},{1,2},{2,3},{3,7},{4,0},{5,1},{6,5},{7,6},{8,9},{9,8},{10,14... | collective-permute-start | bytes 36872 | tf_op jit(solution)/shard_map/ppermute | solution.py:416

commit v5 on v4

--- a/solution.py
+++ b/solution.py
@@ -70,27 +70,27 @@
     return [jnp.where(inner, part, 0.0) for part in parts]
 
 
-def tile_sums(part, root):
-    rows, lanes = part.shape
-    tiles = [part[k : k + TILE] for k in range(0, rows, TILE)]
-    step = float(root**TILE)
-    low, high = tiles[-1], tiles[0]
-    for tile in tiles[-2::-1]:
-        low = low * step + tile
-    for tile in tiles[1:]:
-        high = high * step + tile
+def ramps(lanes):
     at = iota((TILE, lanes), 0)
-    low = low * powers(root, at)
-    high = high * powers(root, TILE - 1 - at)
-    return jnp.sum(low, axis=0, keepdims=True), jnp.sum(high, axis=0, keepdims=True)
-
-
-def difference_sums(lines):
-    rows = lines.shape[0]
-    at = iota(lines.shape, 0)
-    first = jnp.where(at == rows - 1, 0.0, pltpu.roll(lines, rows - 1, 0) - lines)
-    second = jnp.where((at == 0) | (at == rows - 1), 0.0, first - pltpu.roll(first, 1, 0))
-    return *tile_sums(first, ROOTS[0]), *tile_sums(second, ROOTS[1])
+    return [(powers(root, at), powers(root, TILE - 1 - at)) for root in ROOTS]
+
+
+def difference_sums(lines, ramp):
+    rows, lanes = lines.shape
+    steps = pltpu.roll(lines, rows - 1, 0) - lines
+    tiles = [steps[k : k + TILE] for k in range(0, rows, TILE)]
+    tiles[-1] = jnp.where(iota((TILE, lanes), 0) == TILE - 1, 0.0, tiles[-1])
+    sums = []
+    for root, (up, down) in zip(ROOTS, ramp):
+        step = float(root**TILE)
+        low, high = tiles[-1], tiles[0]
+        for tile in tiles[-2::-1]:
+            low = low * step + tile
+        for tile in tiles[1:]:
+            high = high * step + tile
+        sums.append(jnp.sum(low * up, axis=0, keepdims=True))
+        sums.append(jnp.sum(high * down, axis=0, keepdims=True))
+    return sums
 
 
 def right_side_sums(layers, sums, rows):
@@ -113,7 +113,8 @@
             + (far / one) * (total - d0 - one * d1 - one * one * d2)
             + (far * one * one) * (total - last0 - last1 - last2)
         )
-        total = sums[2 + end]
+        total = sums[2] if end == 0 else sums[3] * float(-1.0 / two)
+        total = (1.0 - two) * total - d0 + z0 * float(two ** (size - 1))
         last1, last2 = y1 * float(two ** (size - 2)), y2 * float(two ** (size - 3))
         second = (
             mid * (total - two * e1 - last1)
@@ -176,14 +177,14 @@
     return chosen
 
 
-def ends_of(groups):
+def ends_of(groups, ramp):
     rows = groups[0].shape[0]
     stack = lambda values: jnp.concatenate(values, axis=0)
     layers = [
         [stack([group[at : at + 1] for group in groups]) for at in range(4)],
         [stack([group[rows - 1 - at : rows - at] for group in groups]) for at in range(4)],
     ]
-    sums = [stack(values) for values in zip(*[difference_sums(group) for group in groups])]
+    sums = [stack(values) for values in zip(*[difference_sums(group, ramp) for group in groups])]
     return layers, right_side_sums(layers, sums, rows)
 
 
@@ -200,12 +201,15 @@
     x_even = lax.rem(lax.axis_index("gx"), 2) == 0
     y_even = lax.rem(lax.axis_index("gy"), 2) == 0
     groups = [field[s] for s in range(slabs)]
-    layers, sums = ends_of(groups)
+    ramp = ramps(lanes)
+    layers, sums = ends_of(groups, ramp)
     sent = dict(zip("eo", sends(layers, sums, x_even)))
     for k, layer in enumerate(layers[0] + layers[1]):
         x_own[k, :slabs] = layer
     lines = turned(field[...])
-    layers, sums = ends_of([lines[:, k : k + lanes] for k in range(0, lines.shape[1], lanes)])
+    layers, sums = ends_of(
+        [lines[:, k : k + lanes] for k in range(0, lines.shape[1], lanes)], ramp
+    )
     sent.update(zip("12", sends(layers, sums, y_even)))
     for k, values in enumerate([*layers[0], *sums[0], *layers[1], *sums[1]]):
         y_own[k, : values.shape[0]] = values
@@ -293,16 +297,13 @@
     return numbers
 
 
-def edge_tiles(pair, root, sign):
-    at = iota((TILE, pair[0].shape[1]), 0)
-    at = at if sign > 0 else TILE - 1 - at
-    far = powers(root, at) * pair[0]
-    return jnp.where(at == 0, pair[1], far), far
-
-
-def line_tiles(numbers, line, sign):
-    lines = [[part[line : line + 1] for part in pair] for pair in numbers]
-    return [edge_tiles(pair, root, sign) for pair, root in zip(lines, ROOTS)]
+def edge_tiles(numbers, line, side, ramp):
+    tiles = []
+    for (spread, first), powers_of in zip(numbers, ramp):
+        far = powers_of[side] * spread[line : line + 1]
+        at_edge = iota(far.shape, 0) == (TILE - 1 if side else 0)
+        tiles.append((jnp.where(at_edge, first[line : line + 1], far), far))
+    return tiles
 
 
 def received(way, moved, groups):
@@ -321,11 +322,12 @@
 
 
 def edge_update(low, high, root, tile, tiles):
-    step = root**TILE
-    up, down = tile, tiles - 1 - tile
-    from_low = low[0] if up == 0 else low[1] * float(step**up)
-    from_high = high[0] if down == 0 else high[1] * float(step**down)
-    return from_low + from_high
+    parts = []
+    for (near, far), steps in ((low, tile), (high, tiles - 1 - tile)):
+        scale = float(root ** (TILE * steps))
+        if abs(scale) > np.finfo(np.float32).tiny:
+            parts.append(far * scale if steps else near)
+    return sum(parts[1:], parts[0]) if parts else None
 
 
 def final_kernel(
@@ -342,31 +344,34 @@
     from_low, from_high = select(y_even, odd, even), select(y_even, even, odd)
     low = edge_numbers(own[:4], from_low, 1.0, y_at == 0, own[4:6])
     high = edge_numbers(own[6:10], from_high, -1.0, y_at == y_count - 1, own[10:])
-    tiles = lanes // TILE
+    tiles, ramp = lanes // TILE, ramps(lanes)
     y_term = []
     for group in range(groups):
-        at_low, at_high = line_tiles(low, group, 1.0), line_tiles(high, group, -1.0)
+        at_low, at_high = edge_tiles(low, group, 0, ramp), edge_tiles(high, group, 1, ramp)
         part = slice(group * lanes, (group + 1) * lanes)
         column = []
         for tile in range(tiles):
             place = slice(tile * TILE, (tile + 1) * TILE)
             one, two = [edge_update(at_low[k], at_high[k], ROOTS[k], tile, tiles) for k in range(2)]
-            column.append(slope[place, part] * one + bend[place, :] * two)
+            term = slope[place, part] * one
+            column.append(term if two is None else term + bend[place, :] * two)
         y_term.append(jnp.transpose(jnp.concatenate(column, axis=0)))
     y_term = jnp.concatenate(y_term, axis=0)
     own = [x_own[k, :slabs] for k in range(8)]
     even, odd = [received(way, moved, slabs) for way in "eo"]
     low = edge_numbers(own[:4], select(x_even, odd, even), 1.0)
     high = edge_numbers(own[4:], select(x_even, even, odd), -1.0)
+    for _, second in (low, high):
+        second[:] = [VISCOSITY * number for number in second]
     tiles = rows // TILE
     copies = []
     for s in range(slabs):
-        at_low, at_high = line_tiles(low, s, 1.0), line_tiles(high, s, -1.0)
+        at_low, at_high = edge_tiles(low, s, 0, ramp), edge_tiles(high, s, 1, ramp)
         for tile in range(tiles):
             place = slice(tile * TILE, (tile + 1) * TILE)
             one, two = [edge_update(at_low[k], at_high[k], ROOTS[k], tile, tiles) for k in range(2)]
             turned = y_term[s * rows + tile * TILE : s * rows + (tile + 1) * TILE]
-            x_term = VISCOSITY * two - field[s // 3 * 3, place] * one
+            x_term = two - field[s // 3 * 3, place] * one
             block[s, place] = bulk[s, place] + x_term + turned
         copies.append(pltpu.make_async_copy(block.at[s], out.at[s], sems.at[s]))
         copies[-1].start()

time: 8.37 us -> 8.3 us (level)
  no operation moved by 1% of the time
where the time goes in v5:
time: 8.3 us; the launch traced here: 8.16 us
  starting transfers between devices  2.92 us (35%)
  Pallas kernels  2.2 us (27%)
  waiting for transfers between devices  2.16 us (26%)
  local copies, waits for them, and re-layouts  0.84 us (10%)
    ppermute x4, starting transfers between devices, shards(): lax.ppermute(value, ('gx', 'gy'), exchange_pairs(ways, x_count, y_count))  2.92 us
    pallas_call x4, Pallas kernels, call(): pl.pallas_call(kernel, out_shape=outs, in_specs=[pl.BlockSpec(memory_spac...  2.2 us
    ppermute x4, waiting for transfers between devices, shards(): lax.ppermute(value, ('gx', 'gy'), exchange_pairs(ways, x_count, y_count))  2.16 us
    unnamed x6, local copies, waits for them, and re-layouts  0.84 us
  transfers between devices with their start and end apart: 4, of which 2 were waited for; matrix products, arithmetic and copies ran while one was open for 0% of the time, Pallas kernels for 12%

profile of v5, /device:TPU:24, one launch (start us, length us, event | category | flops | bytes accessed | tf_op | source)
XLA Modules:
  0.0 8.2 jit_solution(3375473072067389892)
XLA Ops:
  0.0 0.0 copy-start
  0.0 0.1 tables.1
  0.1 0.0 copy-start.2
  0.1 0.0 copy-start.1
  0.1 0.8 %copy-done = f32[2,3,48,128]{3,2,1,0:T(8,128)S(1)} copy-done((f32[2,3,48,128]{3,2,1,0:T(8,128)S(1)}, f32[2,3,48,128]{3,2,1,0:T(8,128)}, u32[]{:S(2)}) %copy-start) | copy-done | bytes 147480
  0.9 0.0 copy-done.2
  0.9 0.0 copy-done.1
  0.9 0.3 %sends.1 = (f32[24,128]{1,0:T(8,128)S(1)}, f32[24,128]{1,0:T(8,128)S(1)}, f32[24,128]{1,0:T(8,128)S(1)}, f32[24,128]{1,0:T(8,128)S(1)}, f32[8,128]{1,0:T(8,128)S...) custom-call(f32[6,48,128]{2,1,0:T(8,128)S(1)} %bitcast.4, f32[4,128]{1,0:T(4,128)S(1)} %bitcast.7, ...), custom_call_target="tpu_custom_call" | custom-call | flops 1000000 | tf_op jit(solution)/shard_map/sends/pallas_call | solution.py:401
  1.2 1.9 %collective-permute-start = (f32[24,128]{1,0:T(8,128)S(1)}, f32[24,128]{1,0:T(8,128)S(1)}, u32[]{:S(2)}, u32[]{:S(2)}) collective-permute-start(f32[24,128]{1,0:T(8,128)S(1)} %get-tuple-element.25), channel_id=1, source_target_pairs={{0,4},{1,5},{2,30},{3,31},{4,8},{5,6},{6,2},{7,3},{8,12},{9,13},{1... | collective-permute-start | bytes 36872 | tf_op jit(solution)/shard_map/ppermute | solution.py:421
  3.1 0.5 %collective-permute-start.1 = (f32[24,128]{1,0:T(8,128)S(1)}, f32[24,128]{1,0:T(8,128)S(1)}, u32[]{:S(2)}, u32[]{:S(2)}) collective-permute-start(f32[24,128]{1,0:T(8,128)S(1)} %get-tuple-element.26), channel_id=1, source_target_pairs={{0,28},{1,0},{2,1},{3,2},{4,5},{5,9},{6,7},{7,11},{8,4},{9,10},{10... | collective-permute-start | bytes 36872 | tf_op jit(solution)/shard_map/ppermute | solution.py:421
  3.6 0.0 collective-permute-start.2
  3.6 0.5 %collective-permute-start.3 = (f32[24,128]{1,0:T(8,128)S(1)}, f32[24,128]{1,0:T(8,128)S(1)}, u32[]{:S(2)}, u32[]{:S(2)}) collective-permute-start(f32[24,128]{1,0:T(8,128)S(1)} %get-tuple-element.28), channel_id=1, source_target_pairs={{0,4},{1,2},{2,3},{3,7},{4,0},{5,1},{6,5},{7,6},{8,9},{9,8},{10,14... | collective-permute-start | bytes 36872 | tf_op jit(solution)/shard_map/ppermute | solution.py:421
  4.1 1.0 %bulk.1 = (f32[6,48,128]{2,1,0:T(8,128)S(1)}, f32[128,384]{1,0:T(8,128)S(1)}, f32[128,128]{1,0:T(8,128)S(1)}) custom-call(f32[6,48,128]{2,1,0:T(8,128)S(1)} %bitcast.5, f32[8,128]{1,0:T(8,128)S(1)} %get-tuple-element.18.metrics, f32[2,128,128]{2,1,0:T(8,128)S(1)} %get-tuple-element.19.y_matrix, f32[2,48,48]{2,1,0:T(8,128)S(1)} %get-tuple-element.17._.x_matrix), custom_call_target="tpu_custom_call" | custom-call | flops 100000000 | tf_op jit(solution)/shard_map/bulk/pallas_call | solution.py:401
  5.1 0.0 collective-permute-done.refs_0_
  5.2 2.0 %collective-permute-done.1.refs_1_ = f32[24,128]{1,0:T(8,128)S(1)} collective-permute-done((f32[24,128]{1,0:T(8,128)S(1)}, f32[24,128]{1,0:T(8,128)S(1)}, u32[]{:S(2)}, u32[]{:S(2)}) %collective-permute-start.1) | collective-permute-done | bytes 12320 | tf_op jit(solution)/shard_map/ppermute | solution.py:421
  7.2 0.0 collective-permute-done.2.refs_2_
  7.2 0.1 %collective-permute-done.3.refs_3_ = f32[24,128]{1,0:T(8,128)S(1)} collective-permute-done((f32[24,128]{1,0:T(8,128)S(1)}, f32[24,128]{1,0:T(8,128)S(1)}, u32[]{:S(2)}, u32[]{:S(2)}) %collective-permute-start.3) | collective-permute-done | bytes 12320 | tf_op jit(solution)/shard_map/ppermute | solution.py:421
  7.3 0.9 %final.1 = f32[6,48,128]{2,1,0:T(8,128)} custom-call(f32[6,48,128]{2,1,0:T(8,128)S(1)} %bitcast.6, f32[6,48,128]{2,1,0:T(8,128)S(1)} %get-tuple-element.20.bulk, f32[128,384]{1,0:T(8,128)S(1)} %get-tuple-element.21.slope, f32[128,128]{1,0:T(8,128)S(1)} %get-tuple-element.22.bend, f32[8,8,128]{2,1,0:T(8,128)S(1)} %get-tuple-element.23.x_own, ...), custom_call_target="tpu_custom_call" | custom-call | flops 10000000 | tf_op jit(solution)/shard_map/final/pallas_call | solution.py:401
Async XLA Ops:
  0.0 0.9 %copy-start = (f32[2,3,48,128]{3,2,1,0:T(8,128)S(1)}, f32[2,3,48,128]{3,2,1,0:T(8,128)}, u32[]{:S(2)}) copy-start(f32[2,3,48,128]{3,2,1,0:T(8,128)} %param.3) | copy-start | bytes 442372
  0.1 0.8 %copy-start.2 = (f32[512]{0:T(512)S(1)}, f32[512]{0:T(512)}, u32[]{:S(2)}) copy-start(f32[512]{0:T(512)} %param.5) | copy-start | bytes 6148
  0.1 0.8 %copy-start.1 = (f32[512]{0:T(512)S(1)}, f32[512]{0:T(512)}, u32[]{:S(2)}) copy-start(f32[512]{0:T(512)} %param.4) | copy-start | bytes 6148
  1.2 3.9 %collective-permute-start = (f32[24,128]{1,0:T(8,128)S(1)}, f32[24,128]{1,0:T(8,128)S(1)}, u32[]{:S(2)}, u32[]{:S(2)}) collective-permute-start(f32[24,128]{1,0:T(8,128)S(1)} %get-tuple-element.25), channel_id=1, source_target_pairs={{0,4},{1,5},{2,30},{3,31},{4,8},{5,6},{6,2},{7,3},{8,12},{9,13},{1... | collective-permute-start | bytes 36872 | tf_op jit(solution)/shard_map/ppermute | solution.py:421
  3.1 4.0 %collective-permute-start.1 = (f32[24,128]{1,0:T(8,128)S(1)}, f32[24,128]{1,0:T(8,128)S(1)}, u32[]{:S(2)}, u32[]{:S(2)}) collective-permute-start(f32[24,128]{1,0:T(8,128)S(1)} %get-tuple-element.26), channel_id=1, source_target_pairs={{0,28},{1,0},{2,1},{3,2},{4,5},{5,9},{6,7},{7,11},{8,4},{9,10},{10... | collective-permute-start | bytes 36872 | tf_op jit(solution)/shard_map/ppermute | solution.py:421
  3.6 3.6 %collective-permute-start.2 = (f32[24,128]{1,0:T(8,128)S(1)}, f32[24,128]{1,0:T(8,128)S(1)}, u32[]{:S(2)}, u32[]{:S(2)}) collective-permute-start(f32[24,128]{1,0:T(8,128)S(1)} %get-tuple-element.27), channel_id=1, source_target_pairs={{0,1},{1,29},{2,6},{3,7},{4,0},{5,4},{6,10},{7,3},{8,12},{9,5},{10... | collective-permute-start | bytes 36872 | tf_op jit(solution)/shard_map/ppermute | solution.py:421
  3.6 3.7 %collective-permute-start.3 = (f32[24,128]{1,0:T(8,128)S(1)}, f32[24,128]{1,0:T(8,128)S(1)}, u32[]{:S(2)}, u32[]{:S(2)}) collective-permute-start(f32[24,128]{1,0:T(8,128)S(1)} %get-tuple-element.28), channel_id=1, source_target_pairs={{0,4},{1,2},{2,3},{3,7},{4,0},{5,1},{6,5},{7,6},{8,9},{9,8},{10,14... | collective-permute-start | bytes 36872 | tf_op jit(solution)/shard_map/ppermute | solution.py:421

commit v6 on v5

--- a/solution.py
+++ b/solution.py
@@ -134,14 +134,6 @@
     return [b1, b2, sums[0] - sign * first, sums[1] + second]
 
 
-def received_sums(layers, received, sign):
-    a1, a2 = layers[0] - received[0], layers[1] - received[0]
-    one, two = ROOTS
-    first = 7.0 / 9.0 * a1 + 1.0 / 36.0 * (a2 + one * a1)
-    second = 12.0 / 11.0 * a1 + 3.0 / 44.0 * (a2 + two * a1)
-    return received[2] + sign * first, received[3] + second
-
-
 def turned(field):
     slabs, rows, lanes = field.shape
     fill = -(slabs * rows) % lanes
@@ -247,8 +239,21 @@
     return jnp.concatenate([inv, curve, VISCOSITY * inv * inv, fill], axis=0)
 
 
-def bulk_kernel(field, metrics, y_matrix, x_matrix, out, slope_turned, bend_turned):
+def bulk_kernel(
+    field, metrics, x_own, y_own, y_matrix, x_matrix,
+    out, slope_turned, bend_turned, x_shares, y_shares,
+):
     slabs, rows, lanes = field.shape
+    y_at, y_count = lax.axis_index("gy"), lax.axis_size("gy")
+    own = [x_own[k] for k in range(8)]
+    shares = own_numbers(own[:4], 1.0) + own_numbers(own[4:], -1.0)
+    for k, share in enumerate(shares):
+        x_shares[k] = share
+    own = [y_own[k] for k in range(12)]
+    shares = own_numbers(own[:4], 1.0, y_at == 0, own[4:6])
+    shares += own_numbers(own[6:10], -1.0, y_at == y_count - 1, own[10:])
+    for k, share in enumerate(shares):
+        y_shares[k] = share
     inv, curve, bend = metrics[0:1, :], metrics[1:2, :], metrics[2:3, :]
     bend = jnp.transpose(jnp.broadcast_to(bend, (lanes, lanes)))
     bend_turned[...] = bend
@@ -264,35 +269,49 @@
         out[s] = x_term + y_term[s * rows : (s + 1) * rows]
 
 
-def edge_rows(own, received, sign):
-    a1, a2, a3, a4 = own
-    b1, b2 = received[:2]
-    f0, s0 = stencils(b2, b1, a1, a2, a3)
-    f1, s1 = stencils(b1, a1, a2, a3, a4)
-    first_sum, second_sum = received_sums(own, received, sign)
-    return (sign * f0, sign * f1, first_sum), (s0, s1, second_sum)
-
-
-def wall_rows(own, sums, sign):
-    a1, a2, a3, a4 = own
-    first = (sign * 0.5 * (4.0 * a2 - 3.0 * a1 - a3), sign * 0.75 * (a3 - a1), sums[0])
-    second = (2.0 * a1 - 5.0 * a2 + 4.0 * a3 - a4, 1.2 * (a3 - 2.0 * a2 + a1), sums[1])
-    return first, second
-
-
 def weigh(weights, values):
     return weights[0] * values[0] + weights[1] * values[1] + weights[2] * values[2]
 
 
-def edge_numbers(own, received, sign, wall=None, sums=None):
-    rows = edge_rows(own, received, sign)
-    at_wall = None if wall is None else wall_rows(own, sums, sign)
+def own_numbers(own, sign, wall=None, sums=None):
+    a2, a3, a4 = [layer - own[0] for layer in own[1:]]
+    first = (
+        sign * (7.0 / 9.0 * a2 + 1.0 / 36.0 * a3),
+        sign * (7.0 / 9.0 * a3 + 1.0 / 36.0 * a4),
+        sign * (1.0 / 36.0 * a2),
+    )
+    second = (
+        12.0 / 11.0 * a2 + 3.0 / 44.0 * a3,
+        12.0 / 11.0 * (a3 - 2.0 * a2) + 3.0 / 44.0 * (a4 - 2.0 * a2),
+        3.0 / 44.0 * a2,
+    )
     numbers = []
-    for system in range(2):
-        pair = [weigh(weights, rows[system]) for weights in inner_weights(system)]
-        if wall is not None:
-            other = [weigh(weights, at_wall[system]) for weights in wall_weights(system)]
-            pair = [jnp.where(wall, there, here) for there, here in zip(other, pair)]
+    for system, rows in enumerate((first, second)):
+        numbers += [weigh(weights, rows) for weights in inner_weights(system)]
+    if wall is None:
+        return numbers
+    first = (sign * (2.0 * a2 - 0.5 * a3), sign * 0.75 * a3, sums[0])
+    second = (4.0 * a3 - 5.0 * a2 - a4, 1.2 * (a3 - 2.0 * a2), sums[1])
+    at_wall = []
+    for system, rows in enumerate((first, second)):
+        at_wall += [weigh(weights, rows) for weights in wall_weights(system)]
+    return [jnp.where(wall, there, here) for there, here in zip(at_wall, numbers)]
+
+
+def edge_numbers(shares, nearest, received, sign, wall=None):
+    b1, b2 = received[0] - nearest, received[1] - nearest
+    numbers = []
+    for system, root in enumerate(ROOTS):
+        pair = []
+        for share, (w0, w1, w2) in zip(shares[2 * system :], inner_weights(system)):
+            if system == 0:
+                near = -sign * (7.0 / 9.0 * (w0 + w2) + 1.0 / 36.0 * (w1 + w2 * (1.0 + root)))
+                next_one = -sign * (1.0 / 36.0 * w0)
+            else:
+                near = 12.0 / 11.0 * (w0 - w2) + 3.0 / 44.0 * (w1 - w2 * (1.0 + root))
+                next_one = 3.0 / 44.0 * w0
+            part = near * b1 + next_one * b2 + w2 * received[2 + system]
+            pair.append(share + (part if wall is None else jnp.where(wall, 0.0, part)))
         numbers.append(pair)
     return numbers
 
@@ -331,19 +350,19 @@
 
 
 def final_kernel(
-    field, bulk, slope, bend, x_own, y_own, *refs
+    field, bulk, slope, bend, x_shares, y_shares, x_own, y_own, *refs
 ):
-    *moved, out, block, sems = refs
+    *moved, out = refs
     slabs, rows, lanes = field.shape
     y_at, y_count = lax.axis_index("gy"), lax.axis_size("gy")
     x_even = lax.rem(lax.axis_index("gx"), 2) == 0
     y_even = lax.rem(y_at, 2) == 0
     groups = slope.shape[1] // lanes
-    own = [y_own[k, :groups] for k in range(12)]
+    shares = [y_shares[k, :groups] for k in range(8)]
     even, odd = [received(way, moved, groups) for way in "12"]
     from_low, from_high = select(y_even, odd, even), select(y_even, even, odd)
-    low = edge_numbers(own[:4], from_low, 1.0, y_at == 0, own[4:6])
-    high = edge_numbers(own[6:10], from_high, -1.0, y_at == y_count - 1, own[10:])
+    low = edge_numbers(shares[:4], y_own[0, :groups], from_low, 1.0, y_at == 0)
+    high = edge_numbers(shares[4:], y_own[6, :groups], from_high, -1.0, y_at == y_count - 1)
     tiles, ramp = lanes // TILE, ramps(lanes)
     y_term = []
     for group in range(groups):
@@ -357,14 +376,13 @@
             column.append(term if two is None else term + bend[place, :] * two)
         y_term.append(jnp.transpose(jnp.concatenate(column, axis=0)))
     y_term = jnp.concatenate(y_term, axis=0)
-    own = [x_own[k, :slabs] for k in range(8)]
+    shares = [x_shares[k, :slabs] for k in range(8)]
     even, odd = [received(way, moved, slabs) for way in "eo"]
-    low = edge_numbers(own[:4], select(x_even, odd, even), 1.0)
-    high = edge_numbers(own[4:], select(x_even, even, odd), -1.0)
+    low = edge_numbers(shares[:4], x_own[0, :slabs], select(x_even, odd, even), 1.0)
+    high = edge_numbers(shares[4:], x_own[4, :slabs], select(x_even, even, odd), -1.0)
     for _, second in (low, high):
         second[:] = [VISCOSITY * number for number in second]
     tiles = rows // TILE
-    copies = []
     for s in range(slabs):
         at_low, at_high = edge_tiles(low, s, 0, ramp), edge_tiles(high, s, 1, ramp)
         for tile in range(tiles):
@@ -372,11 +390,7 @@
             one, two = [edge_update(at_low[k], at_high[k], ROOTS[k], tile, tiles) for k in range(2)]
             turned = y_term[s * rows + tile * TILE : s * rows + (tile + 1) * TILE]
             x_term = two - field[s // 3 * 3, place] * one
-            block[s, place] = bulk[s, place] + x_term + turned
-        copies.append(pltpu.make_async_copy(block.at[s], out.at[s], sems.at[s]))
-        copies[-1].start()
-    for copy in copies:
-        copy.wait()
+            out[s, place] = bulk[s, place] + x_term + turned
 
 
 def partner(way, x, y, x_count, y_count):
@@ -435,15 +449,16 @@
     )(field, stretch, metric, tables[1])
     moved = [move(value, ways) for value, ways in zip(sent, ROUNDS)]
     bulk = call(
-        bulk_kernel, [block, shape(lanes, groups * lanes), shape(lanes, lanes)], "bulk", 10**8
-    )(field, metrics, *tables)
+        bulk_kernel,
+        [block, shape(lanes, groups * lanes), shape(lanes, lanes)] + [shape(8, TILE, lanes)] * 2,
+        "bulk",
+        10**8,
+    )(field, metrics, x_own, y_own, *tables)
     (out,) = call(
         final_kernel,
         [block],
         "final",
         10**7,
-        pl.ANY,
-        [pltpu.VMEM(block.shape, jnp.float32), pltpu.SemaphoreType.DMA((slabs,))],
     )(field, *bulk, x_own, y_own, *moved)
     return out.reshape(planes, comps, rows, lanes)
 

time: 8.3 us -> 8.26 us (level)
  transfers between devices with their start and end apart: 4 -> 4, of which waited for: 2 -> 2; matrix products, arithmetic and copies ran while one was open for 0% -> 0% of each run, Pallas kernels for 12% -> 13%
where the time goes in v6:
time: 8.26 us; the launch traced here: 8.12 us
  starting transfers between devices  2.92 us (35%)
  Pallas kernels  2.19 us (27%)
  waiting for transfers between devices  2.13 us (26%)
  local copies, waits for them, and re-layouts  0.84 us (10%)
    ppermute x4, starting transfers between devices, shards(): lax.ppermute(value, ('gx', 'gy'), exchange_pairs(ways, x_count, y_count))  2.92 us
    pallas_call x4, Pallas kernels, call(): pl.pallas_call(kernel, out_shape=outs, in_specs=[pl.BlockSpec(memory_spac...  2.19 us
    ppermute x4, waiting for transfers between devices, shards(): lax.ppermute(value, ('gx', 'gy'), exchange_pairs(ways, x_count, y_count))  2.13 us
    unnamed x6, local copies, waits for them, and re-layouts  0.84 us
  transfers between devices with their start and end apart: 4, of which 2 were waited for; matrix products, arithmetic and copies ran while one was open for 0% of the time, Pallas kernels for 13%

profile of v6, /device:TPU:24, one launch (start us, length us, event | category | flops | bytes accessed | tf_op | source)
XLA Modules:
  0.0 8.1 jit_solution(7199774354471230467)
XLA Ops:
  0.0 0.0 copy-start
  0.0 0.1 tables.1
  0.1 0.0 copy-start.2
  0.1 0.0 copy-start.1
  0.1 0.8 %copy-done = f32[2,3,48,128]{3,2,1,0:T(8,128)S(1)} copy-done((f32[2,3,48,128]{3,2,1,0:T(8,128)S(1)}, f32[2,3,48,128]{3,2,1,0:T(8,128)}, u32[]{:S(2)}) %copy-start) | copy-done | bytes 147480
  0.9 0.0 copy-done.2
  0.9 0.0 copy-done.1
  0.9 0.3 %sends.1 = (f32[24,128]{1,0:T(8,128)S(1)}, f32[24,128]{1,0:T(8,128)S(1)}, f32[24,128]{1,0:T(8,128)S(1)}, f32[24,128]{1,0:T(8,128)S(1)}, f32[8,128]{1,0:T(8,128)S...) custom-call(f32[6,48,128]{2,1,0:T(8,128)S(1)} %bitcast.4, f32[4,128]{1,0:T(4,128)S(1)} %bitcast.7, ...), custom_call_target="tpu_custom_call" | custom-call | flops 1000000 | tf_op jit(solution)/shard_map/sends/pallas_call | solution.py:415
  1.2 1.9 %collective-permute-start = (f32[24,128]{1,0:T(8,128)S(1)}, f32[24,128]{1,0:T(8,128)S(1)}, u32[]{:S(2)}, u32[]{:S(2)}) collective-permute-start(f32[24,128]{1,0:T(8,128)S(1)} %get-tuple-element.29), channel_id=1, source_target_pairs={{0,4},{1,5},{2,30},{3,31},{4,8},{5,6},{6,2},{7,3},{8,12},{9,13},{1... | collective-permute-start | bytes 36872 | tf_op jit(solution)/shard_map/ppermute | solution.py:435
  3.1 0.5 %collective-permute-start.1 = (f32[24,128]{1,0:T(8,128)S(1)}, f32[24,128]{1,0:T(8,128)S(1)}, u32[]{:S(2)}, u32[]{:S(2)}) collective-permute-start(f32[24,128]{1,0:T(8,128)S(1)} %get-tuple-element.30), channel_id=1, source_target_pairs={{0,28},{1,0},{2,1},{3,2},{4,5},{5,9},{6,7},{7,11},{8,4},{9,10},{10... | collective-permute-start | bytes 36872 | tf_op jit(solution)/shard_map/ppermute | solution.py:435
  3.6 0.0 collective-permute-start.2
  3.6 0.5 %collective-permute-start.3 = (f32[24,128]{1,0:T(8,128)S(1)}, f32[24,128]{1,0:T(8,128)S(1)}, u32[]{:S(2)}, u32[]{:S(2)}) collective-permute-start(f32[24,128]{1,0:T(8,128)S(1)} %get-tuple-element.32), channel_id=1, source_target_pairs={{0,4},{1,2},{2,3},{3,7},{4,0},{5,1},{6,5},{7,6},{8,9},{9,8},{10,14... | collective-permute-start | bytes 36872 | tf_op jit(solution)/shard_map/ppermute | solution.py:435
  4.1 1.1 %bulk.1 = (f32[6,48,128]{2,1,0:T(8,128)S(1)}, f32[128,384]{1,0:T(8,128)S(1)}, f32[128,128]{1,0:T(8,128)S(1)}, f32[8,8,128]{2,1,0:T(8,128)S(1)}, f32[8,8,128]{2,1,0:T(8,128)S(1)}) custom-call(f32[6,48,128]{2,1,0:T(8,128)S(1)} %bitcast.5, f32[8,128]{1,0:T(8,128)S(1)} %get-tuple-element.20.metrics, f32[8,8,128]{2,1,0:T(8,128)S(1)} %get-tuple-element.21.x_own, ...), custom_call_target="tpu_custom_call" | custom-call | flops 100000000 | tf_op jit(solution)/shard_map/bulk/pallas_call | solution.py:415
  5.2 0.0 collective-permute-done.refs_0_
  5.2 2.0 %collective-permute-done.1.refs_1_ = f32[24,128]{1,0:T(8,128)S(1)} collective-permute-done((f32[24,128]{1,0:T(8,128)S(1)}, f32[24,128]{1,0:T(8,128)S(1)}, u32[]{:S(2)}, u32[]{:S(2)}) %collective-permute-start.1) | collective-permute-done | bytes 12320 | tf_op jit(solution)/shard_map/ppermute | solution.py:435
  7.2 0.0 collective-permute-done.2.refs_2_
  7.2 0.1 %collective-permute-done.3.refs_3_ = f32[24,128]{1,0:T(8,128)S(1)} collective-permute-done((f32[24,128]{1,0:T(8,128)S(1)}, f32[24,128]{1,0:T(8,128)S(1)}, u32[]{:S(2)}, u32[]{:S(2)}) %collective-permute-start.3) | collective-permute-done | bytes 12320 | tf_op jit(solution)/shard_map/ppermute | solution.py:435
  7.3 0.8 %final.1 = f32[6,48,128]{2,1,0:T(8,128)} custom-call(f32[6,48,128]{2,1,0:T(8,128)S(1)} %bitcast.6, f32[6,48,128]{2,1,0:T(8,128)S(1)} %get-tuple-element.24.bulk, f32[128,384]{1,0:T(8,128)S(1)} %get-tuple-element.25.slope, f32[128,128]{1,0:T(8,128)S(1)} %get-tuple-element.26.bend, f32[8,8,128]{2,1,0:T(8,128)S(1)} %get-tuple-element.27.x_shares, ...), custom_call_target="tpu_custom_call" | custom-call | flops 10000000 | tf_op jit(solution)/shard_map/final/pallas_call | solution.py:415
Async XLA Ops:
  0.0 0.9 %copy-start = (f32[2,3,48,128]{3,2,1,0:T(8,128)S(1)}, f32[2,3,48,128]{3,2,1,0:T(8,128)}, u32[]{:S(2)}) copy-start(f32[2,3,48,128]{3,2,1,0:T(8,128)} %param.3) | copy-start | bytes 442372
  0.1 0.8 %copy-start.2 = (f32[512]{0:T(512)S(1)}, f32[512]{0:T(512)}, u32[]{:S(2)}) copy-start(f32[512]{0:T(512)} %param.5) | copy-start | bytes 6148
  0.1 0.8 %copy-start.1 = (f32[512]{0:T(512)S(1)}, f32[512]{0:T(512)}, u32[]{:S(2)}) copy-start(f32[512]{0:T(512)} %param.4) | copy-start | bytes 6148
  1.2 4.0 %collective-permute-start = (f32[24,128]{1,0:T(8,128)S(1)}, f32[24,128]{1,0:T(8,128)S(1)}, u32[]{:S(2)}, u32[]{:S(2)}) collective-permute-start(f32[24,128]{1,0:T(8,128)S(1)} %get-tuple-element.29), channel_id=1, source_target_pairs={{0,4},{1,5},{2,30},{3,31},{4,8},{5,6},{6,2},{7,3},{8,12},{9,13},{1... | collective-permute-start | bytes 36872 | tf_op jit(solution)/shard_map/ppermute | solution.py:435
  3.1 4.0 %collective-permute-start.1 = (f32[24,128]{1,0:T(8,128)S(1)}, f32[24,128]{1,0:T(8,128)S(1)}, u32[]{:S(2)}, u32[]{:S(2)}) collective-permute-start(f32[24,128]{1,0:T(8,128)S(1)} %get-tuple-element.30), channel_id=1, source_target_pairs={{0,28},{1,0},{2,1},{3,2},{4,5},{5,9},{6,7},{7,11},{8,4},{9,10},{10... | collective-permute-start | bytes 36872 | tf_op jit(solution)/shard_map/ppermute | solution.py:435
  3.6 3.6 %collective-permute-start.2 = (f32[24,128]{1,0:T(8,128)S(1)}, f32[24,128]{1,0:T(8,128)S(1)}, u32[]{:S(2)}, u32[]{:S(2)}) collective-permute-start(f32[24,128]{1,0:T(8,128)S(1)} %get-tuple-element.31), channel_id=1, source_target_pairs={{0,1},{1,29},{2,6},{3,7},{4,0},{5,4},{6,10},{7,3},{8,12},{9,5},{10... | collective-permute-start | bytes 36872 | tf_op jit(solution)/shard_map/ppermute | solution.py:435
  3.6 3.7 %collective-permute-start.3 = (f32[24,128]{1,0:T(8,128)S(1)}, f32[24,128]{1,0:T(8,128)S(1)}, u32[]{:S(2)}, u32[]{:S(2)}) collective-permute-start(f32[24,128]{1,0:T(8,128)S(1)} %get-tuple-element.32), channel_id=1, source_target_pairs={{0,4},{1,2},{2,3},{3,7},{4,0},{5,1},{6,5},{7,6},{8,9},{9,8},{10,14... | collective-permute-start | bytes 36872 | tf_op jit(solution)/shard_map/ppermute | solution.py:435

commit v7 on v6

--- a/solution.py
+++ b/solution.py
@@ -83,10 +83,12 @@
     sums = []
     for root, (up, down) in zip(ROOTS, ramp):
         step = float(root**TILE)
-        low, high = tiles[-1], tiles[0]
-        for tile in tiles[-2::-1]:
+        reach = sum(16.0 * abs(step) ** k > np.finfo(np.float32).tiny for k in range(len(tiles)))
+        near_low, near_high = tiles[:reach], tiles[len(tiles) - reach :]
+        low, high = near_low[-1], near_high[0]
+        for tile in near_low[-2::-1]:
             low = low * step + tile
-        for tile in tiles[1:]:
+        for tile in near_high[1:]:
             high = high * step + tile
         sums.append(jnp.sum(low * up, axis=0, keepdims=True))
         sums.append(jnp.sum(high * down, axis=0, keepdims=True))
@@ -205,15 +207,14 @@
     sent.update(zip("12", sends(layers, sums, y_even)))
     for k, values in enumerate([*layers[0], *sums[0], *layers[1], *sums[1]]):
         y_own[k, : values.shape[0]] = values
+    count = outs[0].shape[0] // 4
+    packed = []
+    for way in WAYS:
+        fill = jnp.zeros((count - sent[way][0].shape[0], lanes), jnp.float32)
+        parts = [part for value in sent[way] for part in (value, fill) if part.shape[0]]
+        packed.append(jnp.concatenate(parts, axis=0))
     for out, ways in zip(outs, ROUNDS):
-        count = out.shape[0] // 4
-        options = {}
-        for number, way in enumerate(WAYS):
-            if way in ways:
-                fill = jnp.zeros((count - sent[way][0].shape[0], lanes), jnp.float32)
-                parts = [part for value in sent[way] for part in (value, fill) if part.shape[0]]
-                options[number] = jnp.concatenate(parts, axis=0)
-        out[...] = by_kind([WAYS.index(way) for way in ways], options)
+        out[...] = by_kind([WAYS.index(way) for way in ways], packed)
 
 
 def inverse_matrix(system, size):
@@ -326,14 +327,9 @@
 
 
 def received(way, moved, groups):
-    rounds = arrival_rounds(way)
-    numbers = []
-    for k in range(4):
-        values = {
-            at: moved[at][pl.ds(k * (moved[at].shape[0] // 4), groups), :] for at in set(rounds)
-        }
-        numbers.append(by_kind(rounds, values))
-    return numbers
+    packed = by_kind(arrival_rounds(way), [part[...] for part in moved])
+    count = packed.shape[0] // 4
+    return [packed[k * count : k * count + groups] for k in range(4)]
 
 
 def select(flag, one, two):

time: 8.26 us -> 8.24 us (level)
  no operation moved by 1% of the time
where the time goes in v7:
time: 8.24 us; the launch traced here: 8.1 us
  starting transfers between devices  2.92 us (35%)
  Pallas kernels  2.18 us (26%)
  waiting for transfers between devices  2.12 us (26%)
  local copies, waits for them, and re-layouts  0.84 us (10%)
    ppermute x4, starting transfers between devices, shards(): lax.ppermute(value, ('gx', 'gy'), exchange_pairs(ways, x_count, y_count))  2.92 us
    pallas_call x4, Pallas kernels, call(): pl.pallas_call(kernel, out_shape=outs, in_specs=[pl.BlockSpec(memory_spac...  2.18 us
    ppermute x4, waiting for transfers between devices, shards(): lax.ppermute(value, ('gx', 'gy'), exchange_pairs(ways, x_count, y_count))  2.12 us
    unnamed x6, local copies, waits for them, and re-layouts  0.84 us
  transfers between devices with their start and end apart: 4, of which 2 were waited for; matrix products, arithmetic and copies ran while one was open for 0% of the time, Pallas kernels for 13%

profile of v7, /device:TPU:24, one launch (start us, length us, event | category | flops | bytes accessed | tf_op | source)
XLA Modules:
  0.0 8.1 jit_solution(4999684592551682859)
XLA Ops:
  0.0 0.0 copy-start
  0.0 0.1 tables.1
  0.1 0.0 copy-start.2
  0.1 0.0 copy-start.1
  0.1 0.8 %copy-done = f32[2,3,48,128]{3,2,1,0:T(8,128)S(1)} copy-done((f32[2,3,48,128]{3,2,1,0:T(8,128)S(1)}, f32[2,3,48,128]{3,2,1,0:T(8,128)}, u32[]{:S(2)}) %copy-start) | copy-done | bytes 147480
  0.9 0.0 copy-done.2
  0.9 0.0 copy-done.1
  0.9 0.3 %sends.1 = (f32[24,128]{1,0:T(8,128)S(1)}, f32[24,128]{1,0:T(8,128)S(1)}, f32[24,128]{1,0:T(8,128)S(1)}, f32[24,128]{1,0:T(8,128)S(1)}, f32[8,128]{1,0:T(8,128)S...) custom-call(f32[6,48,128]{2,1,0:T(8,128)S(1)} %bitcast.4, f32[4,128]{1,0:T(4,128)S(1)} %bitcast.7, ...), custom_call_target="tpu_custom_call" | custom-call | flops 1000000 | tf_op jit(solution)/shard_map/sends/pallas_call | solution.py:411
  1.2 1.9 %collective-permute-start = (f32[24,128]{1,0:T(8,128)S(1)}, f32[24,128]{1,0:T(8,128)S(1)}, u32[]{:S(2)}, u32[]{:S(2)}) collective-permute-start(f32[24,128]{1,0:T(8,128)S(1)} %get-tuple-element.29), channel_id=1, source_target_pairs={{0,4},{1,5},{2,30},{3,31},{4,8},{5,6},{6,2},{7,3},{8,12},{9,13},{1... | collective-permute-start | bytes 36872 | tf_op jit(solution)/shard_map/ppermute | solution.py:431
  3.1 0.5 %collective-permute-start.1 = (f32[24,128]{1,0:T(8,128)S(1)}, f32[24,128]{1,0:T(8,128)S(1)}, u32[]{:S(2)}, u32[]{:S(2)}) collective-permute-start(f32[24,128]{1,0:T(8,128)S(1)} %get-tuple-element.30), channel_id=1, source_target_pairs={{0,28},{1,0},{2,1},{3,2},{4,5},{5,9},{6,7},{7,11},{8,4},{9,10},{10... | collective-permute-start | bytes 36872 | tf_op jit(solution)/shard_map/ppermute | solution.py:431
  3.6 0.0 collective-permute-start.2
  3.6 0.5 %collective-permute-start.3 = (f32[24,128]{1,0:T(8,128)S(1)}, f32[24,128]{1,0:T(8,128)S(1)}, u32[]{:S(2)}, u32[]{:S(2)}) collective-permute-start(f32[24,128]{1,0:T(8,128)S(1)} %get-tuple-element.32), channel_id=1, source_target_pairs={{0,4},{1,2},{2,3},{3,7},{4,0},{5,1},{6,5},{7,6},{8,9},{9,8},{10,14... | collective-permute-start | bytes 36872 | tf_op jit(solution)/shard_map/ppermute | solution.py:431
  4.1 1.1 %bulk.1 = (f32[6,48,128]{2,1,0:T(8,128)S(1)}, f32[128,384]{1,0:T(8,128)S(1)}, f32[128,128]{1,0:T(8,128)S(1)}, f32[8,8,128]{2,1,0:T(8,128)S(1)}, f32[8,8,128]{2,1,0:T(8,128)S(1)}) custom-call(f32[6,48,128]{2,1,0:T(8,128)S(1)} %bitcast.5, f32[8,128]{1,0:T(8,128)S(1)} %get-tuple-element.20.metrics, f32[8,8,128]{2,1,0:T(8,128)S(1)} %get-tuple-element.21.x_own, ...), custom_call_target="tpu_custom_call" | custom-call | flops 100000000 | tf_op jit(solution)/shard_map/bulk/pallas_call | solution.py:411
  5.2 0.0 collective-permute-done.refs_0_
  5.2 2.0 %collective-permute-done.1.refs_1_ = f32[24,128]{1,0:T(8,128)S(1)} collective-permute-done((f32[24,128]{1,0:T(8,128)S(1)}, f32[24,128]{1,0:T(8,128)S(1)}, u32[]{:S(2)}, u32[]{:S(2)}) %collective-permute-start.1) | collective-permute-done | bytes 12320 | tf_op jit(solution)/shard_map/ppermute | solution.py:431
  7.1 0.0 collective-permute-done.2.refs_2_
  7.1 0.1 %collective-permute-done.3.refs_3_ = f32[24,128]{1,0:T(8,128)S(1)} collective-permute-done((f32[24,128]{1,0:T(8,128)S(1)}, f32[24,128]{1,0:T(8,128)S(1)}, u32[]{:S(2)}, u32[]{:S(2)}) %collective-permute-start.3) | collective-permute-done | bytes 12320 | tf_op jit(solution)/shard_map/ppermute | solution.py:431
  7.3 0.8 %final.1 = f32[6,48,128]{2,1,0:T(8,128)} custom-call(f32[6,48,128]{2,1,0:T(8,128)S(1)} %bitcast.6, f32[6,48,128]{2,1,0:T(8,128)S(1)} %get-tuple-element.24.bulk, f32[128,384]{1,0:T(8,128)S(1)} %get-tuple-element.25.slope, f32[128,128]{1,0:T(8,128)S(1)} %get-tuple-element.26.bend, f32[8,8,128]{2,1,0:T(8,128)S(1)} %get-tuple-element.27.x_shares, ...), custom_call_target="tpu_custom_call" | custom-call | flops 10000000 | tf_op jit(solution)/shard_map/final/pallas_call | solution.py:411
Async XLA Ops:
  0.0 0.9 %copy-start = (f32[2,3,48,128]{3,2,1,0:T(8,128)S(1)}, f32[2,3,48,128]{3,2,1,0:T(8,128)}, u32[]{:S(2)}) copy-start(f32[2,3,48,128]{3,2,1,0:T(8,128)} %param.3) | copy-start | bytes 442372
  0.1 0.8 %copy-start.2 = (f32[512]{0:T(512)S(1)}, f32[512]{0:T(512)}, u32[]{:S(2)}) copy-start(f32[512]{0:T(512)} %param.5) | copy-start | bytes 6148
  0.1 0.8 %copy-start.1 = (f32[512]{0:T(512)S(1)}, f32[512]{0:T(512)}, u32[]{:S(2)}) copy-start(f32[512]{0:T(512)} %param.4) | copy-start | bytes 6148
  1.2 4.0 %collective-permute-start = (f32[24,128]{1,0:T(8,128)S(1)}, f32[24,128]{1,0:T(8,128)S(1)}, u32[]{:S(2)}, u32[]{:S(2)}) collective-permute-start(f32[24,128]{1,0:T(8,128)S(1)} %get-tuple-element.29), channel_id=1, source_target_pairs={{0,4},{1,5},{2,30},{3,31},{4,8},{5,6},{6,2},{7,3},{8,12},{9,13},{1... | collective-permute-start | bytes 36872 | tf_op jit(solution)/shard_map/ppermute | solution.py:431
  3.1 4.0 %collective-permute-start.1 = (f32[24,128]{1,0:T(8,128)S(1)}, f32[24,128]{1,0:T(8,128)S(1)}, u32[]{:S(2)}, u32[]{:S(2)}) collective-permute-start(f32[24,128]{1,0:T(8,128)S(1)} %get-tuple-element.30), channel_id=1, source_target_pairs={{0,28},{1,0},{2,1},{3,2},{4,5},{5,9},{6,7},{7,11},{8,4},{9,10},{10... | collective-permute-start | bytes 36872 | tf_op jit(solution)/shard_map/ppermute | solution.py:431
  3.6 3.6 %collective-permute-start.2 = (f32[24,128]{1,0:T(8,128)S(1)}, f32[24,128]{1,0:T(8,128)S(1)}, u32[]{:S(2)}, u32[]{:S(2)}) collective-permute-start(f32[24,128]{1,0:T(8,128)S(1)} %get-tuple-element.31), channel_id=1, source_target_pairs={{0,1},{1,29},{2,6},{3,7},{4,0},{5,4},{6,10},{7,3},{8,12},{9,5},{10... | collective-permute-start | bytes 36872 | tf_op jit(solution)/shard_map/ppermute | solution.py:431
  3.6 3.7 %collective-permute-start.3 = (f32[24,128]{1,0:T(8,128)S(1)}, f32[24,128]{1,0:T(8,128)S(1)}, u32[]{:S(2)}, u32[]{:S(2)}) collective-permute-start(f32[24,128]{1,0:T(8,128)S(1)} %get-tuple-element.32), channel_id=1, source_target_pairs={{0,4},{1,2},{2,3},{3,7},{4,0},{5,1},{6,5},{7,6},{8,9},{9,8},{10,14... | collective-permute-start | bytes 36872 | tf_op jit(solution)/shard_map/ppermute | solution.py:431

commit v8 on v7

--- a/solution.py
+++ b/solution.py
@@ -354,6 +354,12 @@
     x_even = lax.rem(lax.axis_index("gx"), 2) == 0
     y_even = lax.rem(y_at, 2) == 0
     groups = slope.shape[1] // lanes
+    shares = [x_shares[k, :slabs] for k in range(8)]
+    even, odd = [received(way, moved, slabs) for way in "eo"]
+    x_low = edge_numbers(shares[:4], x_own[0, :slabs], select(x_even, odd, even), 1.0)
+    x_high = edge_numbers(shares[4:], x_own[4, :slabs], select(x_even, even, odd), -1.0)
+    for _, second in (x_low, x_high):
+        second[:] = [VISCOSITY * number for number in second]
     shares = [y_shares[k, :groups] for k in range(8)]
     even, odd = [received(way, moved, groups) for way in "12"]
     from_low, from_high = select(y_even, odd, even), select(y_even, even, odd)
@@ -372,15 +378,9 @@
             column.append(term if two is None else term + bend[place, :] * two)
         y_term.append(jnp.transpose(jnp.concatenate(column, axis=0)))
     y_term = jnp.concatenate(y_term, axis=0)
-    shares = [x_shares[k, :slabs] for k in range(8)]
-    even, odd = [received(way, moved, slabs) for way in "eo"]
-    low = edge_numbers(shares[:4], x_own[0, :slabs], select(x_even, odd, even), 1.0)
-    high = edge_numbers(shares[4:], x_own[4, :slabs], select(x_even, even, odd), -1.0)
-    for _, second in (low, high):
-        second[:] = [VISCOSITY * number for number in second]
     tiles = rows // TILE
     for s in range(slabs):
-        at_low, at_high = edge_tiles(low, s, 0, ramp), edge_tiles(high, s, 1, ramp)
+        at_low, at_high = edge_tiles(x_low, s, 0, ramp), edge_tiles(x_high, s, 1, ramp)
         for tile in range(tiles):
             place = slice(tile * TILE, (tile + 1) * TILE)
             one, two = [edge_update(at_low[k], at_high[k], ROOTS[k], tile, tiles) for k in range(2)]

time: 8.24 us -> 8.25 us (level)
  no operation moved by 1% of the time
where the time goes in v8:
time: 8.25 us; the launch traced here: 8.1 us
  starting transfers between devices  2.92 us (35%)
  Pallas kernels  2.19 us (27%)
  waiting for transfers between devices  2.12 us (26%)
  local copies, waits for them, and re-layouts  0.84 us (10%)
    ppermute x4, starting transfers between devices, shards(): lax.ppermute(value, ('gx', 'gy'), exchange_pairs(ways, x_count, y_count))  2.92 us
    pallas_call x4, Pallas kernels, call(): pl.pallas_call(kernel, out_shape=outs, in_specs=[pl.BlockSpec(memory_spac...  2.19 us
    ppermute x4, waiting for transfers between devices, shards(): lax.ppermute(value, ('gx', 'gy'), exchange_pairs(ways, x_count, y_count))  2.12 us
    unnamed x6, local copies, waits for them, and re-layouts  0.84 us
  transfers between devices with their start and end apart: 4, of which 2 were waited for; matrix products, arithmetic and copies ran while one was open for 0% of the time, Pallas kernels for 13%

profile of v8, /device:TPU:24, one launch (start us, length us, event | category | flops | bytes accessed | tf_op | source)
XLA Modules:
  0.0 8.1 jit_solution(11399666335623275648)
XLA Ops:
  0.0 0.0 copy-start
  0.0 0.1 tables.1
  0.1 0.0 copy-start.2
  0.1 0.0 copy-start.1
  0.1 0.8 %copy-done = f32[2,3,48,128]{3,2,1,0:T(8,128)S(1)} copy-done((f32[2,3,48,128]{3,2,1,0:T(8,128)S(1)}, f32[2,3,48,128]{3,2,1,0:T(8,128)}, u32[]{:S(2)}) %copy-start) | copy-done | bytes 147480
  0.9 0.0 copy-done.2
  0.9 0.0 copy-done.1
  0.9 0.3 %sends.1 = (f32[24,128]{1,0:T(8,128)S(1)}, f32[24,128]{1,0:T(8,128)S(1)}, f32[24,128]{1,0:T(8,128)S(1)}, f32[24,128]{1,0:T(8,128)S(1)}, f32[8,128]{1,0:T(8,128)S...) custom-call(f32[6,48,128]{2,1,0:T(8,128)S(1)} %bitcast.4, f32[4,128]{1,0:T(4,128)S(1)} %bitcast.7, ...), custom_call_target="tpu_custom_call" | custom-call | flops 1000000 | tf_op jit(solution)/shard_map/sends/pallas_call | solution.py:411
  1.2 1.9 %collective-permute-start = (f32[24,128]{1,0:T(8,128)S(1)}, f32[24,128]{1,0:T(8,128)S(1)}, u32[]{:S(2)}, u32[]{:S(2)}) collective-permute-start(f32[24,128]{1,0:T(8,128)S(1)} %get-tuple-element.29), channel_id=1, source_target_pairs={{0,4},{1,5},{2,30},{3,31},{4,8},{5,6},{6,2},{7,3},{8,12},{9,13},{1... | collective-permute-start | bytes 36872 | tf_op jit(solution)/shard_map/ppermute | solution.py:431
  3.1 0.5 %collective-permute-start.1 = (f32[24,128]{1,0:T(8,128)S(1)}, f32[24,128]{1,0:T(8,128)S(1)}, u32[]{:S(2)}, u32[]{:S(2)}) collective-permute-start(f32[24,128]{1,0:T(8,128)S(1)} %get-tuple-element.30), channel_id=1, source_target_pairs={{0,28},{1,0},{2,1},{3,2},{4,5},{5,9},{6,7},{7,11},{8,4},{9,10},{10... | collective-permute-start | bytes 36872 | tf_op jit(solution)/shard_map/ppermute | solution.py:431
  3.6 0.0 collective-permute-start.2
  3.6 0.5 %collective-permute-start.3 = (f32[24,128]{1,0:T(8,128)S(1)}, f32[24,128]{1,0:T(8,128)S(1)}, u32[]{:S(2)}, u32[]{:S(2)}) collective-permute-start(f32[24,128]{1,0:T(8,128)S(1)} %get-tuple-element.32), channel_id=1, source_target_pairs={{0,4},{1,2},{2,3},{3,7},{4,0},{5,1},{6,5},{7,6},{8,9},{9,8},{10,14... | collective-permute-start | bytes 36872 | tf_op jit(solution)/shard_map/ppermute | solution.py:431
  4.1 1.1 %bulk.1 = (f32[6,48,128]{2,1,0:T(8,128)S(1)}, f32[128,384]{1,0:T(8,128)S(1)}, f32[128,128]{1,0:T(8,128)S(1)}, f32[8,8,128]{2,1,0:T(8,128)S(1)}, f32[8,8,128]{2,1,0:T(8,128)S(1)}) custom-call(f32[6,48,128]{2,1,0:T(8,128)S(1)} %bitcast.5, f32[8,128]{1,0:T(8,128)S(1)} %get-tuple-element.20.metrics, f32[8,8,128]{2,1,0:T(8,128)S(1)} %get-tuple-element.21.x_own, ...), custom_call_target="tpu_custom_call" | custom-call | flops 100000000 | tf_op jit(solution)/shard_map/bulk/pallas_call | solution.py:411
  5.2 0.0 collective-permute-done.refs_0_
  5.2 2.0 %collective-permute-done.1.refs_1_ = f32[24,128]{1,0:T(8,128)S(1)} collective-permute-done((f32[24,128]{1,0:T(8,128)S(1)}, f32[24,128]{1,0:T(8,128)S(1)}, u32[]{:S(2)}, u32[]{:S(2)}) %collective-permute-start.1) | collective-permute-done | bytes 12320 | tf_op jit(solution)/shard_map/ppermute | solution.py:431
  7.1 0.0 collective-permute-done.2.refs_2_
  7.1 0.1 %collective-permute-done.3.refs_3_ = f32[24,128]{1,0:T(8,128)S(1)} collective-permute-done((f32[24,128]{1,0:T(8,128)S(1)}, f32[24,128]{1,0:T(8,128)S(1)}, u32[]{:S(2)}, u32[]{:S(2)}) %collective-permute-start.3) | collective-permute-done | bytes 12320 | tf_op jit(solution)/shard_map/ppermute | solution.py:431
  7.3 0.8 %final.1 = f32[6,48,128]{2,1,0:T(8,128)} custom-call(f32[6,48,128]{2,1,0:T(8,128)S(1)} %bitcast.6, f32[6,48,128]{2,1,0:T(8,128)S(1)} %get-tuple-element.24.bulk, f32[128,384]{1,0:T(8,128)S(1)} %get-tuple-element.25.slope, f32[128,128]{1,0:T(8,128)S(1)} %get-tuple-element.26.bend, f32[8,8,128]{2,1,0:T(8,128)S(1)} %get-tuple-element.27.x_shares, ...), custom_call_target="tpu_custom_call" | custom-call | flops 10000000 | tf_op jit(solution)/shard_map/final/pallas_call | solution.py:411
Async XLA Ops:
  0.0 0.9 %copy-start = (f32[2,3,48,128]{3,2,1,0:T(8,128)S(1)}, f32[2,3,48,128]{3,2,1,0:T(8,128)}, u32[]{:S(2)}) copy-start(f32[2,3,48,128]{3,2,1,0:T(8,128)} %param.3) | copy-start | bytes 442372
  0.1 0.8 %copy-start.2 = (f32[512]{0:T(512)S(1)}, f32[512]{0:T(512)}, u32[]{:S(2)}) copy-start(f32[512]{0:T(512)} %param.5) | copy-start | bytes 6148
  0.1 0.8 %copy-start.1 = (f32[512]{0:T(512)S(1)}, f32[512]{0:T(512)}, u32[]{:S(2)}) copy-start(f32[512]{0:T(512)} %param.4) | copy-start | bytes 6148
  1.2 4.0 %collective-permute-start = (f32[24,128]{1,0:T(8,128)S(1)}, f32[24,128]{1,0:T(8,128)S(1)}, u32[]{:S(2)}, u32[]{:S(2)}) collective-permute-start(f32[24,128]{1,0:T(8,128)S(1)} %get-tuple-element.29), channel_id=1, source_target_pairs={{0,4},{1,5},{2,30},{3,31},{4,8},{5,6},{6,2},{7,3},{8,12},{9,13},{1... | collective-permute-start | bytes 36872 | tf_op jit(solution)/shard_map/ppermute | solution.py:431
  3.1 4.0 %collective-permute-start.1 = (f32[24,128]{1,0:T(8,128)S(1)}, f32[24,128]{1,0:T(8,128)S(1)}, u32[]{:S(2)}, u32[]{:S(2)}) collective-permute-start(f32[24,128]{1,0:T(8,128)S(1)} %get-tuple-element.30), channel_id=1, source_target_pairs={{0,28},{1,0},{2,1},{3,2},{4,5},{5,9},{6,7},{7,11},{8,4},{9,10},{10... | collective-permute-start | bytes 36872 | tf_op jit(solution)/shard_map/ppermute | solution.py:431
  3.6 3.6 %collective-permute-start.2 = (f32[24,128]{1,0:T(8,128)S(1)}, f32[24,128]{1,0:T(8,128)S(1)}, u32[]{:S(2)}, u32[]{:S(2)}) collective-permute-start(f32[24,128]{1,0:T(8,128)S(1)} %get-tuple-element.31), channel_id=1, source_target_pairs={{0,1},{1,29},{2,6},{3,7},{4,0},{5,4},{6,10},{7,3},{8,12},{9,5},{10... | collective-permute-start | bytes 36872 | tf_op jit(solution)/shard_map/ppermute | solution.py:431
  3.6 3.7 %collective-permute-start.3 = (f32[24,128]{1,0:T(8,128)S(1)}, f32[24,128]{1,0:T(8,128)S(1)}, u32[]{:S(2)}, u32[]{:S(2)}) collective-permute-start(f32[24,128]{1,0:T(8,128)S(1)} %get-tuple-element.32), channel_id=1, source_target_pairs={{0,4},{1,2},{2,3},{3,7},{4,0},{5,1},{6,5},{7,6},{8,9},{9,8},{10,14... | collective-permute-start | bytes 36872 | tf_op jit(solution)/shard_map/ppermute | solution.py:431

commit v9 on v7

--- a/solution.py
+++ b/solution.py
@@ -188,14 +188,14 @@
     return select(even, high, low), select(even, low, high)
 
 
-def send_kernel(field, stretch, metric, _, *refs):
+def send_kernel(field, stretch, metric, ramp_in, *refs):
     *outs, metrics, x_own, y_own = refs
     metrics[...] = metric_rows(stretch, metric)
     slabs, _, lanes = field.shape
     x_even = lax.rem(lax.axis_index("gx"), 2) == 0
     y_even = lax.rem(lax.axis_index("gy"), 2) == 0
     groups = [field[s] for s in range(slabs)]
-    ramp = ramps(lanes)
+    ramp = [(ramp_in[0], ramp_in[1]), (ramp_in[2], ramp_in[3])]
     layers, sums = ends_of(groups, ramp)
     sent = dict(zip("eo", sends(layers, sums, x_even)))
     for k, layer in enumerate(layers[0] + layers[1]):
@@ -226,7 +226,9 @@
     return jnp.dot(matrix, right_side, precision=HIGHEST, preferred_element_type=jnp.float32)
 
 
-def table_kernel(y_out, x_out):
+def table_kernel(y_out, x_out, ramp_out):
+    for k, ramp in enumerate(ramps(y_out.shape[1])):
+        ramp_out[2 * k], ramp_out[2 * k + 1] = ramp
     for system in range(2):
         y_out[system] = inverse_matrix(system, y_out.shape[1])
         x_out[system] = inverse_matrix(system, x_out.shape[1])
@@ -346,7 +348,7 @@
 
 
 def final_kernel(
-    field, bulk, slope, bend, x_shares, y_shares, x_own, y_own, *refs
+    field, bulk, slope, bend, x_shares, y_shares, x_own, y_own, ramp_in, *refs
 ):
     *moved, out = refs
     slabs, rows, lanes = field.shape
@@ -359,7 +361,8 @@
     from_low, from_high = select(y_even, odd, even), select(y_even, even, odd)
     low = edge_numbers(shares[:4], y_own[0, :groups], from_low, 1.0, y_at == 0)
     high = edge_numbers(shares[4:], y_own[6, :groups], from_high, -1.0, y_at == y_count - 1)
-    tiles, ramp = lanes // TILE, ramps(lanes)
+    tiles = lanes // TILE
+    ramp = [(ramp_in[0], ramp_in[1]), (ramp_in[2], ramp_in[3])]
     y_term = []
     for group in range(groups):
         at_low, at_high = edge_tiles(low, group, 0, ramp), edge_tiles(high, group, 1, ramp)
@@ -432,7 +435,7 @@
         value, ("gx", "gy"), exchange_pairs(ways, x_count, y_count)
     )
 
-    tables = call(table_kernel, [shape(2, lanes, lanes), shape(2, rows, rows)], "tables", 10**8)()
+    *tables, ramp = call(table_kernel, [shape(2, lanes, lanes), shape(2, rows, rows), shape(4, TILE, lanes)], "tables", 10**8)()
     field = velocity.reshape(slabs, rows, lanes)
     groups = -(-slabs * rows // lanes)
     send = shape(4 * max(slabs, groups), lanes)
@@ -442,7 +445,7 @@
         + [shape(TILE, lanes), shape(8, TILE, lanes), shape(12, TILE, lanes)],
         "sends",
         10**6,
-    )(field, stretch, metric, tables[1])
+    )(field, stretch, metric, ramp)
     moved = [move(value, ways) for value, ways in zip(sent, ROUNDS)]
     bulk = call(
         bulk_kernel,
@@ -455,7 +458,7 @@
         [block],
         "final",
         10**7,
-    )(field, *bulk, x_own, y_own, *moved)
+    )(field, *bulk, x_own, y_own, ramp, *moved)
     return out.reshape(planes, comps, rows, lanes)
 
 

time: 8.24 us -> 8.23 us (level)
  no operation moved by 1% of the time
where the time goes in v9:
time: 8.23 us; the launch traced here: 8.09 us
  starting transfers between devices  2.92 us (35%)
  Pallas kernels  2.17 us (26%)
  waiting for transfers between devices  2.13 us (26%)
  local copies, waits for them, and re-layouts  0.83 us (10%)
    ppermute x4, starting transfers between devices, shards(): lax.ppermute(value, ('gx', 'gy'), exchange_pairs(ways, x_count, y_count))  2.92 us
    pallas_call x4, Pallas kernels, call(): pl.pallas_call(kernel, out_shape=outs, in_specs=[pl.BlockSpec(memory_spac...  2.17 us
    ppermute x4, waiting for transfers between devices, shards(): lax.ppermute(value, ('gx', 'gy'), exchange_pairs(ways, x_count, y_count))  2.13 us
    unnamed x6, local copies, waits for them, and re-layouts  0.83 us
  transfers between devices with their start and end apart: 4, of which 2 were waited for; matrix products, arithmetic and copies ran while one was open for 0% of the time, Pallas kernels for 13%

profile of v9, /device:TPU:24, one launch (start us, length us, event | category | flops | bytes accessed | tf_op | source)
XLA Modules:
  0.0 8.1 jit_solution(9066900843845184961)
XLA Ops:
  0.0 0.0 copy-start
  0.0 0.1 tables.1
  0.1 0.0 copy-start.2
  0.1 0.0 copy-start.1
  0.1 0.8 %copy-done = f32[2,3,48,128]{3,2,1,0:T(8,128)S(1)} copy-done((f32[2,3,48,128]{3,2,1,0:T(8,128)S(1)}, f32[2,3,48,128]{3,2,1,0:T(8,128)}, u32[]{:S(2)}) %copy-start) | copy-done | bytes 147480
  0.9 0.0 copy-done.2
  0.9 0.0 copy-done.1
  0.9 0.3 %sends.1 = (f32[24,128]{1,0:T(8,128)S(1)}, f32[24,128]{1,0:T(8,128)S(1)}, f32[24,128]{1,0:T(8,128)S(1)}, f32[24,128]{1,0:T(8,128)S(1)}, f32[8,128]{1,0:T(8,128)S...) custom-call(f32[6,48,128]{2,1,0:T(8,128)S(1)} %bitcast.4, f32[4,128]{1,0:T(4,128)S(1)} %bitcast.7, ...), custom_call_target="tpu_custom_call" | custom-call | flops 1000000 | tf_op jit(solution)/shard_map/sends/pallas_call | solution.py:414
  1.2 1.9 %collective-permute-start = (f32[24,128]{1,0:T(8,128)S(1)}, f32[24,128]{1,0:T(8,128)S(1)}, u32[]{:S(2)}, u32[]{:S(2)}) collective-permute-start(f32[24,128]{1,0:T(8,128)S(1)} %get-tuple-element.31), channel_id=1, source_target_pairs={{0,4},{1,5},{2,30},{3,31},{4,8},{5,6},{6,2},{7,3},{8,12},{9,13},{1... | collective-permute-start | bytes 36872 | tf_op jit(solution)/shard_map/ppermute | solution.py:434
  3.1 0.5 %collective-permute-start.1 = (f32[24,128]{1,0:T(8,128)S(1)}, f32[24,128]{1,0:T(8,128)S(1)}, u32[]{:S(2)}, u32[]{:S(2)}) collective-permute-start(f32[24,128]{1,0:T(8,128)S(1)} %get-tuple-element.32), channel_id=1, source_target_pairs={{0,28},{1,0},{2,1},{3,2},{4,5},{5,9},{6,7},{7,11},{8,4},{9,10},{10... | collective-permute-start | bytes 36872 | tf_op jit(solution)/shard_map/ppermute | solution.py:434
  3.6 0.0 collective-permute-start.2
  3.6 0.5 %collective-permute-start.3 = (f32[24,128]{1,0:T(8,128)S(1)}, f32[24,128]{1,0:T(8,128)S(1)}, u32[]{:S(2)}, u32[]{:S(2)}) collective-permute-start(f32[24,128]{1,0:T(8,128)S(1)} %get-tuple-element.34), channel_id=1, source_target_pairs={{0,4},{1,2},{2,3},{3,7},{4,0},{5,1},{6,5},{7,6},{8,9},{9,8},{10,14... | collective-permute-start | bytes 36872 | tf_op jit(solution)/shard_map/ppermute | solution.py:434
  4.1 1.1 %bulk.1 = (f32[6,48,128]{2,1,0:T(8,128)S(1)}, f32[128,384]{1,0:T(8,128)S(1)}, f32[128,128]{1,0:T(8,128)S(1)}, f32[8,8,128]{2,1,0:T(8,128)S(1)}, f32[8,8,128]{2,1,0:T(8,128)S(1)}) custom-call(f32[6,48,128]{2,1,0:T(8,128)S(1)} %bitcast.5, f32[8,128]{1,0:T(8,128)S(1)} %get-tuple-element.21.metrics, f32[8,8,128]{2,1,0:T(8,128)S(1)} %get-tuple-element.22.x_own, ...), custom_call_target="tpu_custom_call" | custom-call | flops 100000000 | tf_op jit(solution)/shard_map/bulk/pallas_call | solution.py:414
  5.2 0.0 collective-permute-done.refs_0_
  5.2 2.0 %collective-permute-done.1.refs_1_ = f32[24,128]{1,0:T(8,128)S(1)} collective-permute-done((f32[24,128]{1,0:T(8,128)S(1)}, f32[24,128]{1,0:T(8,128)S(1)}, u32[]{:S(2)}, u32[]{:S(2)}) %collective-permute-start.1) | collective-permute-done | bytes 12320 | tf_op jit(solution)/shard_map/ppermute | solution.py:434
  7.1 0.0 collective-permute-done.2.refs_2_
  7.1 0.1 %collective-permute-done.3.refs_3_ = f32[24,128]{1,0:T(8,128)S(1)} collective-permute-done((f32[24,128]{1,0:T(8,128)S(1)}, f32[24,128]{1,0:T(8,128)S(1)}, u32[]{:S(2)}, u32[]{:S(2)}) %collective-permute-start.3) | collective-permute-done | bytes 12320 | tf_op jit(solution)/shard_map/ppermute | solution.py:434
  7.3 0.8 %final.1 = f32[6,48,128]{2,1,0:T(8,128)} custom-call(f32[6,48,128]{2,1,0:T(8,128)S(1)} %bitcast.6, f32[6,48,128]{2,1,0:T(8,128)S(1)} %get-tuple-element.26.bulk, f32[128,384]{1,0:T(8,128)S(1)} %get-tuple-element.27.slope, f32[128,128]{1,0:T(8,128)S(1)} %get-tuple-element.28.bend, f32[8,8,128]{2,1,0:T(8,128)S(1)} %get-tuple-element.29.x_shares, ...), custom_call_target="tpu_custom_call" | custom-call | flops 10000000 | tf_op jit(solution)/shard_map/final/pallas_call | solution.py:414
Async XLA Ops:
  0.0 0.9 %copy-start = (f32[2,3,48,128]{3,2,1,0:T(8,128)S(1)}, f32[2,3,48,128]{3,2,1,0:T(8,128)}, u32[]{:S(2)}) copy-start(f32[2,3,48,128]{3,2,1,0:T(8,128)} %param.3) | copy-start | bytes 442372
  0.1 0.8 %copy-start.2 = (f32[512]{0:T(512)S(1)}, f32[512]{0:T(512)}, u32[]{:S(2)}) copy-start(f32[512]{0:T(512)} %param.5) | copy-start | bytes 6148
  0.1 0.8 %copy-start.1 = (f32[512]{0:T(512)S(1)}, f32[512]{0:T(512)}, u32[]{:S(2)}) copy-start(f32[512]{0:T(512)} %param.4) | copy-start | bytes 6148
  1.2 4.0 %collective-permute-start = (f32[24,128]{1,0:T(8,128)S(1)}, f32[24,128]{1,0:T(8,128)S(1)}, u32[]{:S(2)}, u32[]{:S(2)}) collective-permute-start(f32[24,128]{1,0:T(8,128)S(1)} %get-tuple-element.31), channel_id=1, source_target_pairs={{0,4},{1,5},{2,30},{3,31},{4,8},{5,6},{6,2},{7,3},{8,12},{9,13},{1... | collective-permute-start | bytes 36872 | tf_op jit(solution)/shard_map/ppermute | solution.py:434
  3.1 4.0 %collective-permute-start.1 = (f32[24,128]{1,0:T(8,128)S(1)}, f32[24,128]{1,0:T(8,128)S(1)}, u32[]{:S(2)}, u32[]{:S(2)}) collective-permute-start(f32[24,128]{1,0:T(8,128)S(1)} %get-tuple-element.32), channel_id=1, source_target_pairs={{0,28},{1,0},{2,1},{3,2},{4,5},{5,9},{6,7},{7,11},{8,4},{9,10},{10... | collective-permute-start | bytes 36872 | tf_op jit(solution)/shard_map/ppermute | solution.py:434
  3.6 3.6 %collective-permute-start.2 = (f32[24,128]{1,0:T(8,128)S(1)}, f32[24,128]{1,0:T(8,128)S(1)}, u32[]{:S(2)}, u32[]{:S(2)}) collective-permute-start(f32[24,128]{1,0:T(8,128)S(1)} %get-tuple-element.33), channel_id=1, source_target_pairs={{0,1},{1,29},{2,6},{3,7},{4,0},{5,4},{6,10},{7,3},{8,12},{9,5},{10... | collective-permute-start | bytes 36872 | tf_op jit(solution)/shard_map/ppermute | solution.py:434
  3.6 3.7 %collective-permute-start.3 = (f32[24,128]{1,0:T(8,128)S(1)}, f32[24,128]{1,0:T(8,128)S(1)}, u32[]{:S(2)}, u32[]{:S(2)}) collective-permute-start(f32[24,128]{1,0:T(8,128)S(1)} %get-tuple-element.34), channel_id=1, source_target_pairs={{0,4},{1,2},{2,3},{3,7},{4,0},{5,1},{6,5},{7,6},{8,9},{9,8},{10,14... | collective-permute-start | bytes 36872 | tf_op jit(solution)/shard_map/ppermute | solution.py:434
